TPU v7x, 32 devices: a whole 2x2x4 slice. The times are simulated.
32 devices in a mesh: seq: 8 (over z, x), head: 4 (over y, core).
Axes of the slice: x: 2, y: 2, z: 4, core: 2. Of those that a mesh axis runs over, the one named last changes fastest.
Arguments:
- block_input: bfloat16 [8, 256, 5120], P(None, 'seq'), may hold values from -6 to 6
- accepted: bfloat16 [8, 256, 5120], P(None, 'seq'), may hold values from -6 to 6
- accept_mask: int32 [8, 256], P(None, 'seq'), may hold values 0 or 1
- cache_lengths: int32 [8], replicated, may hold values from 1 to 8192, as said below
- page_table: int32 [512], replicated, may hold values from 0 to 511, each once
- norm_gain: float32 [5120], replicated, may hold values from 0.1 to 1.9
- w_query: bfloat16 [5120, 3072], P('seq', 'head'), may hold values from -0.078125 to 0.078125
- w_key: bfloat16 [5120, 3072], P('seq', 'head'), may hold values from -0.078125 to 0.078125
- w_value: bfloat16 [5120, 3072], P('seq', 'head'), may hold values from -0.25 to 0.25
- w_out: bfloat16 [5120, 3072], P('seq', 'head'), may hold values from -0.109375 to 0.109375
- key_cache: bfloat16 [512, 128, 3072], P('seq', None, 'head')
- value_cache: bfloat16 [512, 128, 3072], P('seq', None, 'head'), may hold values from -18 to 18
Outputs:
- first_out: bfloat16 [8, 256, 5120], P(None, 'seq', 'head')
- second_out: bfloat16 [8, 256, 5120], P(None, 'seq', 'head')
Inputs may be any that keep to these rules, and one draw needn't show every extreme that they name: `cache_lengths`: max(1, 4) requests, chosen at random, hold (63) * 128 + 1 to 8192 cached tokens, one of them exactly 8192; the others hold 1 to 256. `page_table`: A permutation of the 512 pool pages; entry r * 64 + j is the pool page of cached positions j * 128 to (j + 1) * 128 - 1 of request r.
All inputs are finite; a program needn't handle non-finite values. No bound on the sum of `accept_mask` on one device may be relied on, other than what follows from the above.
Results may differ from a plain program's by a relative error of at most 0.024.
The roundings to bfloat16 on the way count: a program that leaves them out, or rounds other values in their place, can miss the bound.
Values may be sent and summed in bfloat16 or wider, within the bound.
No kernel may reach another device: no remote copies, remote signals or barrier semaphores. Data moves between devices by JAX's collectives and lax.ppermute only.
A program may use at most 256 MiB of HBM per device.

v0:
```python
import functools
import math

import jax
import jax.numpy as jnp
from jax import lax
from jax.experimental import pallas as pl
from jax.experimental.pallas import tpu as pltpu
from jax.sharding import PartitionSpec as P

HD = 128
PAGE = 128
MAXP = 64
MASKED = -1e30
EXP2_SCALE = HD ** (-0.5) * math.log2(math.e)
SLOTS = 8
CHUNKS = 2
SUM_ROWS = 32
VMEM_BYTES = 40 * 1024 * 1024
IN_VMEM = pl.BlockSpec(memory_space=pltpu.VMEM)
IN_SMEM = pl.BlockSpec(memory_space=pltpu.SMEM)
IN_HBM = pl.BlockSpec(memory_space=pl.ANY)


def head_span(head):
    return slice(head * HD, (head + 1) * HD)


def rotate_kernel(own, received, cosine, sine, out):
    for head in range(own.shape[1] // HD):
        span = head_span(head)
        raw = own[:, span] + received[:, span].astype(jnp.float32)
        swapped = pltpu.roll(raw, HD // 2, 1)
        out[:, span] = (raw * cosine[...] + swapped * sine[...]).astype(jnp.bfloat16)


def rotated_sum(own, received, cosine, sine):
    return pl.pallas_call(
        rotate_kernel,
        out_shape=jax.ShapeDtypeStruct(own.shape, jnp.bfloat16),
        in_specs=[IN_VMEM] * 4,
        out_specs=IN_VMEM,
        cost_estimate=pl.CostEstimate(
            flops=4 * own.size, bytes_accessed=8 * own.size, transcendentals=0
        ),
        name="rotate_rows",
    )(own, received, cosine, sine)


def values_by_weights(values, weights):
    return lax.dot_general(
        values,
        weights.astype(jnp.bfloat16),
        (((0,), (0,)), ((), ())),
        preferred_element_type=jnp.float32,
    )


def cached_kernel(sources, first, order, counts, starts, lives, fulls, *refs):
    q_refs = refs[:sources]
    k_hbm, v_hbm, q_t, acc, peak, total, kbuf, vbuf, sem = refs[sources:]
    requests = acc.shape[0]
    _, rows, width = q_refs[0].shape
    heads = width // HD
    columns = sources * rows
    end = starts[first + requests]

    def copies(item):
        slot = lax.rem(item, SLOTS)
        page = order[item]
        place = pl.ds(pl.multiple_of(slot * PAGE, PAGE), PAGE)
        return (
            pltpu.make_async_copy(k_hbm.at[page], kbuf.at[place], sem.at[slot, 0]),
            pltpu.make_async_copy(v_hbm.at[page], vbuf.at[place], sem.at[slot, 1]),
        )

    def fetch(item):
        @pl.when((item < end) & (order[item] >= 0))
        def _():
            for copy in copies(item):
                copy.start()

    def await_item(item):
        for copy in copies(item):
            copy.wait()

    def absorb(r, place, alive):
        def scores_of(head):
            return jnp.dot(
                kbuf[place, head_span(head)], q_t[r, head], preferred_element_type=jnp.float32
            )

        following = scores_of(0)
        for head in range(heads):
            scores = following
            if head + 1 < heads:
                following = scores_of(head + 1)
            if alive is not None:
                scores = jnp.where(alive, scores, MASKED)
            before = peak[r, head : head + 1, :]
            top = jnp.maximum(before, jnp.max(scores, axis=0, keepdims=True))
            weights = jnp.exp2((scores - top) * EXP2_SCALE)
            shrink = jnp.exp2((before - top) * EXP2_SCALE)
            peak[r, head : head + 1, :] = top
            total[r, head : head + 1, :] = total[r, head : head + 1, :] * shrink + jnp.sum(
                weights, axis=0, keepdims=True
            )
            acc[r, head] = acc[r, head] * shrink + values_by_weights(
                vbuf[place, head_span(head)], weights
            )

    begin = starts[first]
    for item in range(SLOTS - 2):
        fetch(begin + item)

    def request(r, carry):
        for head in range(heads):
            query = jnp.concatenate([ref[first + r, :, head_span(head)] for ref in q_refs], axis=0)
            q_t[r, head] = query.T
            acc[r, head] = jnp.zeros((HD, columns), jnp.float32)
        peak[r] = jnp.full((8, columns), MASKED, jnp.float32)
        total[r] = jnp.zeros((8, columns), jnp.float32)
        start = starts[first + r]
        pairs = fulls[first + r] // 2

        def pair(step, inner):
            item = start + 2 * step
            await_item(item)
            await_item(item + 1)
            fetch(item + SLOTS - 2)
            fetch(item + SLOTS - 1)
            row = pl.multiple_of(lax.rem(item, SLOTS) * PAGE, 2 * PAGE)
            absorb(r, pl.ds(row, 2 * PAGE), None)
            return inner

        lax.fori_loop(0, pairs, pair, 0)
        rest = start + 2 * pairs
        after_rest = start + lives[first + r]

        @pl.when(rest < after_rest)
        def _():
            fetch(rest + SLOTS - 2)
            fetch(rest + SLOTS - 1)

        def single(item, inner):
            await_item(item)
            row = pl.multiple_of(lax.rem(item, SLOTS) * PAGE, PAGE)
            alive = lax.broadcasted_iota(jnp.int32, (PAGE, columns), 0) < counts[item]
            absorb(r, pl.ds(row, PAGE), alive)
            return inner

        lax.fori_loop(rest, after_rest, single, 0)
        return carry

    lax.fori_loop(0, requests, request, 0)


def cached_attention(first, queries, key_cache, value_cache, plan):
    sources = len(queries)
    whole, rows, width = queries[0].shape
    requests = whole // CHUNKS
    heads = width // HD
    columns = sources * rows
    touched = key_cache.shape[0] * PAGE // CHUNKS
    return pl.pallas_call(
        functools.partial(cached_kernel, sources, first),
        out_shape=[
            jax.ShapeDtypeStruct((requests, heads, HD, columns), jnp.bfloat16),
            jax.ShapeDtypeStruct((requests, heads, HD, columns), jnp.float32),
            jax.ShapeDtypeStruct((requests, 8, columns), jnp.float32),
            jax.ShapeDtypeStruct((requests, 8, columns), jnp.float32),
        ],
        in_specs=[IN_SMEM] * 5 + [IN_VMEM] * sources + [IN_HBM] * 2,
        out_specs=[IN_VMEM] * 4,
        scratch_shapes=[
            pltpu.VMEM((SLOTS * PAGE, width), jnp.bfloat16),
            pltpu.VMEM((SLOTS * PAGE, width), jnp.bfloat16),
            pltpu.SemaphoreType.DMA((SLOTS, 2)),
        ],
        compiler_params=pltpu.CompilerParams(vmem_limit_bytes=VMEM_BYTES),
        cost_estimate=pl.CostEstimate(
            flops=touched * columns * width // 4,
            bytes_accessed=touched * width // 4,
            transcendentals=0,
        ),
        name="cached_attention",
    )(*plan, *queries, key_cache, value_cache)


def in_three(values):
    high = values.astype(jnp.bfloat16).astype(jnp.float32)
    middle = (values - high).astype(jnp.bfloat16).astype(jnp.float32)
    return jnp.concatenate([high, middle, values - high - middle, jnp.zeros_like(values)], axis=0)


def block_kernel(sources, first, q_t, acc, peak, total, kblk, vblk, *refs):
    o_refs = refs[:sources]
    sums = refs[sources]
    requests, heads, _, columns = q_t.shape
    rows = kblk.shape[1]
    width = heads * HD
    lanes = min(HD, requests * rows)
    together = lanes // rows
    key_pass = lax.broadcasted_iota(jnp.int32, (rows, columns), 0) // (rows // 2)
    query_pass = (lax.broadcasted_iota(jnp.int32, (rows, columns), 1) // (rows // 2)) % 2
    same_pass = key_pass == query_pass
    sums[...] = jnp.zeros_like(sums)

    def group(g, carry):
        if requests == together:
            place = slice(0, lanes)
        else:
            place = pl.ds(pl.multiple_of(g * lanes, lanes), lanes)
        for head in range(heads):
            means = []
            for item in range(together):
                r = g * together + item
                scores = jnp.dot(
                    kblk[first + r, :, head_span(head)], q_t[r, head], preferred_element_type=jnp.float32
                )
                scores = jnp.where(same_pass, scores, MASKED)
                before = peak[r, head : head + 1, :]
                top = jnp.maximum(before, jnp.max(scores, axis=0, keepdims=True))
                weights = jnp.exp2((scores - top) * EXP2_SCALE)
                shrink = jnp.exp2((before - top) * EXP2_SCALE)
                weight_sum = total[r, head : head + 1, :] * shrink + jnp.sum(
                    weights, axis=0, keepdims=True
                )
                summed = acc[r, head] * shrink + values_by_weights(
                    vblk[first + r, :, head_span(head)], weights
                )
                means.append(summed * (1.0 / weight_sum))
                sums[item, head : head + 1, :] = top * EXP2_SCALE + jnp.log2(weight_sum)
            for source, ref in enumerate(o_refs):
                span = slice(source * rows, (source + 1) * rows)
                ref[head_span(head), place] = jnp.concatenate(
                    [mean[:, span] for mean in means], axis=1
                ).astype(jnp.bfloat16)
        parts = [in_three(sums[item]) for item in range(together)]
        for source, ref in enumerate(o_refs):
            span = slice(source * rows, (source + 1) * rows)
            ref[width:, place] = jnp.concatenate(
                [part[:, span] for part in parts], axis=1
            ).astype(jnp.bfloat16)
        return carry

    lax.fori_loop(0, requests // together, group, 0)


def block_attention(sources, first, state, kblk, vblk):
    requests, heads, _, columns = state[0].shape
    rows = kblk.shape[1]
    together = min(HD, requests * rows) // rows
    piece = jax.ShapeDtypeStruct((heads * HD + SUM_ROWS, requests * rows), jnp.bfloat16)
    return pl.pallas_call(
        functools.partial(block_kernel, sources, first),
        out_shape=[piece] * sources,
        in_specs=[IN_VMEM] * 6,
        out_specs=[IN_VMEM] * sources,
        scratch_shapes=[pltpu.VMEM((together, 8, columns), jnp.float32)],
        compiler_params=pltpu.CompilerParams(vmem_limit_bytes=VMEM_BYTES),
        cost_estimate=pl.CostEstimate(
            flops=requests * heads * HD * columns * rows,
            bytes_accessed=requests * heads * HD * columns,
            transcendentals=0,
        ),
        name="block_attention",
    )(*state, kblk, vblk)


def merge_kernel(own, other, out):
    width = own.shape[0] - SUM_ROWS

    def sums_of(ref):
        parts = ref[width:, :].astype(jnp.float32)
        return parts[0:8] + parts[8:16] + parts[16:24]

    own_l, other_l = sums_of(own), sums_of(other)
    top = jnp.maximum(own_l, other_l)
    own_w = jnp.exp2(own_l - top)
    other_w = jnp.exp2(other_l - top)
    both = own_w + other_w
    out[width:, :] = in_three(top + jnp.log2(both)).astype(jnp.bfloat16)
    own_share, other_share = own_w / both, other_w / both
    for head in range(width // HD):
        span = head_span(head)
        out[span, :] = (
            own[span, :].astype(jnp.float32) * own_share[head : head + 1]
            + other[span, :].astype(jnp.float32) * other_share[head : head + 1]
        ).astype(jnp.bfloat16)


def merge(own, other):
    return pl.pallas_call(
        merge_kernel,
        out_shape=jax.ShapeDtypeStruct(own.shape, own.dtype),
        in_specs=[IN_VMEM] * 2,
        out_specs=IN_VMEM,
        cost_estimate=pl.CostEstimate(
            flops=6 * own.size, bytes_accessed=6 * own.size, transcendentals=0
        ),
        name="merge_partials",
    )(own, other)


class Axis:
    def __init__(self, rank, mesh_axis, devices, stride, length):
        self.rank, self.mesh_axis, self.devices = rank, mesh_axis, devices
        self.stride, self.length = stride, length
        self.coord = (lax.axis_index(mesh_axis) // stride) % length

    def moved(self, index, steps):
        here = (index // self.stride) % self.length
        return index + ((here + steps) % self.length - here) * self.stride

    def step(self, value):
        pairs = [(index, self.moved(index, 1)) for index in range(self.devices)]
        return lax.ppermute(value, self.mesh_axis, pairs)

    def gather(self, value):
        items = [value]
        for _ in range(self.length - 1):
            items.append(self.step(items[-1]))
        return items

    def reduce(self, parts, join):
        held = parts[-1]
        for place in range(self.length - 2, -1, -1):
            held = join(parts[place], self.step(held))
        return held

    def before(self, steps):
        return (self.coord - steps + self.length) % self.length


def with_entry(key, rank, entry):
    return key[:rank] + (entry,) + key[rank + 1 :]


def gather_tree(value, axes):
    found = {(0, 0, 0): value}
    for axis in axes:
        found = {
            with_entry(key, axis.rank, steps): item
            for key, held in found.items()
            for steps, item in enumerate(axis.gather(held))
        }
    return found


def reduce_tree(parts, axes, join):
    for axis in axes:
        rank = axis.rank - 1
        ends = sorted((key for key in parts if key[rank] == 0), reverse=True)
        parts = {
            key: axis.reduce(
                [parts[with_entry(key, rank, steps)] for steps in range(axis.length)], join
            )
            for key in ends
        }
    return parts[(0, 0)]


def after(value, earlier):
    return lax.optimization_barrier((value, earlier))[0]


def per_device(
    seq_size,
    head_size,
    block_input,
    accepted,
    accept_mask,
    cache_lengths,
    page_table,
    norm_gain,
    w_query,
    w_key,
    w_value,
    w_out,
    key_cache,
    value_cache,
):
    seq_place = lax.axis_index("seq")
    head_place = lax.axis_index("head")
    requests, part_len, model_width = block_input.shape
    depth, local_width = w_query.shape
    rows = 2 * requests * part_len

    x_size = 2 ** ((seq_size.bit_length() - 2) // 2)
    half_size = seq_size // 2
    z_size = half_size // x_size
    half_axis = Axis(0, "seq", seq_size, half_size, 2)
    z_axis = Axis(1, "seq", seq_size, x_size, z_size)
    x_axis = Axis(2, "seq", seq_size, 1, x_size)
    y_axis = Axis(0, "head", head_size, 2, head_size // 2)
    core_axis = Axis(0, "head", head_size, 1, 2)
    half_order = [(0, z, x) for z in range(z_size) for x in range(x_size)]
    full_order = [(half, z, x) for half in range(2) for _, z, x in half_order]
    assert head_size == 2 * z_size and seq_size == head_size * x_size

    def place_of(half_steps, z_steps, x_steps):
        return (
            half_axis.before(half_steps) * z_size + z_axis.before(z_steps)
        ) * x_size + x_axis.before(x_steps)

    half_width = half_size * depth
    accepted_here = accept_mask[:, :, None] == 1

    def raw_rows(places):
        def picked(inputs):
            return jnp.concatenate(
                [lax.dynamic_slice_in_dim(inputs, at * depth, depth, axis=2) for at in places],
                axis=2,
            )

        first = picked(block_input)
        second = jnp.where(accepted_here, picked(accepted), first)
        return jnp.stack([first, second], axis=1).reshape(rows, len(places) * depth)

    def gather_plane(shard, z_after, x_after):
        found = {}
        for z_steps, line in enumerate(z_axis.gather(after(shard, z_after))):
            if z_steps == 0:
                line = shard if x_after is None else after(shard, x_after)
            for x_steps, item in enumerate(x_axis.gather(line)):
                found[(0, z_steps, x_steps)] = item
        return found

    share = half_size // head_size
    flats = [head_place * share + item for item in range(share)]
    picked = raw_rows([place_of(1, flat // x_size, flat % x_size) for flat in flats])
    fetched = half_axis.step(picked)
    query_shards = gather_plane(w_query, picked, None)
    key_shards = gather_plane(w_key, fetched, query_shards[half_order[-1]])
    value_shards = gather_plane(
        w_value, key_shards[(0, 1, 0)], key_shards[half_order[-1]]
    )
    far_out = half_axis.step(after(w_out, (fetched, query_shards[(0, 1, 0)])))

    def joined(shards):
        return jnp.concatenate([shards[key] for key in half_order], axis=0)

    query_weight, key_weight, value_weight = map(
        joined, (query_shards, key_shards, value_shards)
    )

    def square_mean(inputs):
        widened = inputs.astype(jnp.float32)
        return jnp.mean(widened * widened, axis=-1)

    first_mean = square_mean(after(block_input, picked))
    second_mean = jnp.where(
        accept_mask == 1, square_mean(after(accepted, picked)), first_mean
    )
    inverse = lax.rsqrt(jnp.stack([first_mean, second_mean], axis=1) + 1e-05).reshape(
        requests, 2 * part_len
    )
    other_inverse = after(half_axis.step(inverse), fetched).reshape(rows, 1)
    inverse = inverse.reshape(rows, 1)
    own_gain = jnp.concatenate(
        [
            lax.dynamic_slice_in_dim(norm_gain, place_of(*key) * depth, depth, axis=0)
            for key in half_order
        ]
    )

    def normed(raw, scale):
        return (raw.astype(jnp.float32) * scale * own_gain).astype(jnp.bfloat16)

    own_rows = normed(raw_rows([place_of(*key) for key in half_order]), inverse)
    other_raw = jnp.zeros((rows, half_width), jnp.bfloat16)
    for y_steps, line in enumerate(y_axis.gather(fetched)):
        for core_steps, item in enumerate(core_axis.gather(line)):
            source = y_axis.before(y_steps) * 2 + core_axis.before(core_steps)
            other_raw = lax.dynamic_update_slice_in_dim(
                other_raw, item, source * share * depth, axis=1
            )
    other_rows = normed(other_raw, other_inverse)

    def product(left, weight):
        return jnp.dot(left, weight, preferred_element_type=jnp.float32)

    positions = (
        cache_lengths[:, None]
        + seq_place * part_len
        + jnp.arange(part_len, dtype=jnp.int32)[None, :]
    ).astype(jnp.float32)
    frequency = 10000.0 ** (-(jnp.arange(HD // 2).astype(jnp.float32) * 2.0) / HD)
    angles = (positions[..., None] * frequency)[:, None]

    def by_row(front, back):
        both = jnp.concatenate([front, back], axis=-1)
        return jnp.broadcast_to(both, (requests, 2, part_len, HD)).reshape(rows, HD)

    cosine = by_row(jnp.cos(angles), jnp.cos(angles))
    sine = by_row(-jnp.sin(angles), jnp.sin(angles))
    piece = (requests, 2 * part_len, local_width)
    chunk = requests // CHUNKS

    sent_query = product(other_rows, query_weight).astype(jnp.bfloat16)
    received_query = after(
        half_axis.step(sent_query), (key_shards, far_out, value_shards[(0, 1, 0)])
    )
    near = rotated_sum(
        product(own_rows, query_weight), received_query, cosine, sine
    ).reshape(piece)
    far = half_axis.step(near)
    trees = [gather_tree(near, (z_axis, x_axis)), gather_tree(far, (x_axis, z_axis))]
    every_query = [trees[key[0]][with_entry(key, 0, 0)] for key in full_order]

    sent_key = product(other_rows, key_weight).astype(jnp.bfloat16)
    received_key = half_axis.step(after(sent_key, (trees[1][(0, 0, 1)], value_shards)))
    new_keys = rotated_sum(product(own_rows, key_weight), received_key, cosine, sine)
    new_keys = new_keys.reshape(piece)
    sent_value = product(other_rows, value_weight).astype(jnp.bfloat16)
    received_value = half_axis.step(after(sent_value, received_key))
    new_values = (
        (product(own_rows, value_weight) + received_value.astype(jnp.float32))
        .astype(jnp.bfloat16)
        .reshape(piece)
    )

    pages_here = key_cache.shape[0]
    page_ids = seq_place * pages_here + jnp.arange(pages_here, dtype=jnp.int32)
    table_slots = jnp.arange(page_table.shape[0], dtype=jnp.int32)
    slot_of = jnp.sum(
        jnp.where(page_table[None, :] == page_ids[:, None], table_slots[None, :], 0), axis=1
    )
    page_owner = slot_of // MAXP
    request_ids = jnp.arange(requests, dtype=jnp.int32)
    owner_match = page_owner[:, None] == request_ids[None, :]
    owner_length = jnp.sum(jnp.where(owner_match, cache_lengths[None, :], 0), axis=1)
    page_count = jnp.clip(owner_length - (slot_of % MAXP) * PAGE, 0, PAGE)
    is_live = page_count > 0
    local_ids = jnp.arange(pages_here, dtype=jnp.int32)
    live_match = owner_match & is_live[:, None]
    full_match = owner_match & (page_count == PAGE)[:, None]
    lives = jnp.sum(live_match.astype(jnp.int32), axis=0)
    fulls = jnp.sum(full_match.astype(jnp.int32), axis=0)
    even_lives = (lives + 1) // 2 * 2
    bounds = jnp.arange(requests + 1, dtype=jnp.int32)
    starts = jnp.sum(
        jnp.where(request_ids[None, :] < bounds[:, None], even_lives[None, :], 0), axis=1
    )
    rank_key = jnp.where(page_count == PAGE, 0, pages_here) + local_ids
    same_owner = page_owner[None, :] == page_owner[:, None]
    earlier = same_owner & is_live[None, :] & (rank_key[None, :] < rank_key[:, None])
    own_start = jnp.sum(jnp.where(owner_match, starts[None, :-1], 0), axis=1)
    item_of = own_start + jnp.sum(earlier.astype(jnp.int32), axis=1)
    items = jnp.arange(pages_here + requests + SLOTS, dtype=jnp.int32)
    at_item = (item_of[None, :] == items[:, None]) & is_live[None, :]
    order = jnp.sum(jnp.where(at_item, local_ids[None, :] + 1, 0), axis=1) - 1
    counts = jnp.sum(jnp.where(at_item, page_count[None, :], 0), axis=1)
    plan = (order, counts, starts, lives, fulls)

    own_out = gather_tree(after(w_out, every_query), (z_axis, x_axis))
    far_out = gather_tree(after(far_out, every_query), (x_axis, z_axis))
    out_shards = [(own_out, far_out)[key[0]][with_entry(key, 0, 0)] for key in full_order]
    out_weight = jnp.concatenate(out_shards, axis=0)
    out_width = model_width // head_size
    states = [
        cached_attention(number * chunk, every_query, key_cache, value_cache, plan)
        for number in range(CHUNKS)
    ]
    results = []
    for number in range(CHUNKS):
        block_values = new_values
        if number == CHUNKS - 1:
            block_values = after(block_values, out_shards)
        pieces = block_attention(
            seq_size, number * chunk, states[number], new_keys, block_values
        )

        def parts_for(half_steps):
            return {
                (z_steps, x_steps): pieces[
                    ((-half_steps % 2) * z_size + (-z_steps % z_size)) * x_size
                    + (-x_steps % x_size)
                ]
                for _, z_steps, x_steps in half_order
            }

        far_sum = reduce_tree(parts_for(1), (z_axis, x_axis), merge)
        near_sum = reduce_tree(parts_for(0), (x_axis, z_axis), merge)
        context = half_axis.reduce([near_sum, far_sum], merge)[:local_width]

        def features_of(target):
            line = target ^ head_place
            half_steps = (half_axis.coord - line // z_size + 2) % 2
            z_steps = (z_axis.coord - line % z_size + z_size) % z_size
            return lax.dynamic_slice_in_dim(
                out_weight, (half_steps * z_size + z_steps) * out_width, out_width, axis=0
            )

        outputs = {
            target: lax.dot_general(
                context,
                features_of(target),
                (((0,), (1,)), ((), ())),
                preferred_element_type=jnp.float32,
            )
            for target in range(head_size)
        }
        bit = 1
        while bit < head_size:
            pairs = [(index, index ^ bit) for index in range(head_size)]
            for target in [place for place in outputs if place & bit]:
                sent = outputs.pop(target).astype(jnp.bfloat16)
                outputs[target ^ bit] += lax.ppermute(sent, "head", pairs).astype(jnp.float32)
            bit *= 2
        summed = outputs[0].astype(jnp.bfloat16)
        in_order = jnp.concatenate(
            [
                lax.dynamic_slice_in_dim(
                    summed, (x_axis.coord - x + x_size) % x_size * depth, depth, axis=1
                )
                for x in range(x_size)
            ],
            axis=1,
        )
        results.append(in_order.reshape(chunk, 2, part_len, out_width))
    result = jnp.concatenate(results, axis=0)
    return (result[:, 0], result[:, 1])


def solution(mesh):
    placed = (
        P(None, "seq", None),
        P(None, "seq", None),
        P(None, "seq"),
        P(),
        P(),
        P(),
        P("seq", "head"),
        P("seq", "head"),
        P("seq", "head"),
        P("seq", "head"),
        P("seq", None, "head"),
        P("seq", None, "head"),
    )
    return jax.shard_map(
        functools.partial(per_device, mesh.shape["seq"], mesh.shape["head"]),
        mesh=mesh,
        in_specs=placed,
        out_specs=(P(None, "seq", "head"), P(None, "seq", "head")),
        check_vma=False,
    )
```

profile of v0, /device:TPU:0, one launch (start us, length us, event | category | flops | bytes accessed | tf_op | source)
XLA Modules:
  0.0 478.9 jit_solution(11569372691106325516)
XLA Ops:
  0.6 3.0 collective-permute-start
  4.3 2.5 dynamic-slice_bitcast_fusion.4
  7.8 2.6 collective-permute-start.3
  15.8 23.5 %collective-permute-done.3 = bf16[512,640]{1,0:T(8,128)(2,1)S(1)} collective-permute-done((bf16[512,640]{1,0:T(8,128)(2,1)}, bf16[512,640]{1,0:T(8,128)(2,1)S(1)}, u32[]{:S(2)}, u32[]{:S(2)}) %collective-permute-start.3) | collective-permute-done | bytes 655392 | tf_op jit(solution)/shard_map/ppermute | solution.py:318
  43.2 6.7 %collective-permute-done.1 = bf16[640,768]{1,0:T(8,128)(2,1)} collective-permute-done((bf16[640,768]{1,0:T(8,128)(2,1)}, bf16[640,768]{1,0:T(8,128)(2,1)}, u32[]{:S(2)}, u32[]{:S(2)}) %collective-permute-start.1) | collective-permute-done | bytes 983072 | tf_op jit(solution)/shard_map/ppermute | solution.py:318
  51.8 3.1 collective-permute-start.12
  59.9 25.6 %collective-permute-done.10 = bf16[640,768]{1,0:T(8,128)(2,1)} collective-permute-done((bf16[640,768]{1,0:T(8,128)(2,1)}, bf16[640,768]{1,0:T(8,128)(2,1)}, u32[]{:S(2)}, u32[]{:S(2)}) %collective-permute-start.10) | collective-permute-done | bytes 983072 | tf_op jit(solution)/shard_map/ppermute | solution.py:318
  89.0 2.3 convolution_convert_fusion.6
  91.3 3.3 collective-permute-start.8
  95.4 3.4 fusion.46.own
  98.8 30.2 %collective-permute-done.13 = bf16[640,768]{1,0:T(8,128)(2,1)} collective-permute-done((bf16[640,768]{1,0:T(8,128)(2,1)}, bf16[640,768]{1,0:T(8,128)(2,1)}, u32[]{:S(2)}, u32[]{:S(2)}) %collective-permute-start.13) | collective-permute-done | bytes 983072 | tf_op jit(solution)/shard_map/ppermute | solution.py:318
  130.5 3.1 rotate_rows.2
  133.6 2.6 collective-permute-start.17
  137.4 2.5 collective-permute-start.15
  139.9 28.2 %collective-permute-done.17.refs_4_ = bf16[8,64,768]{2,1,0:T(8,128)(2,1)S(1)} collective-permute-done((bf16[8,64,768]{2,1,0:T(8,128)(2,1)}, bf16[8,64,768]{2,1,0:T(8,128)(2,1)S(1)}, u32[]{:S(2)}, u32[]{:S(2)}) %collective-permute-start.17) | collective-permute-done | bytes 786464 | tf_op jit(solution)/shard_map/ppermute | solution.py:318
  179.3 9.3 %collective-permute-done.18.refs_5_ = bf16[8,64,768]{2,1,0:T(8,128)(2,1)S(1)} collective-permute-done((bf16[8,64,768]{2,1,0:T(8,128)(2,1)S(1)}, bf16[8,64,768]{2,1,0:T(8,128)(2,1)S(1)}, u32[]{:S(2)}, u32[]{:S(2)}) %collective-permute-start.18) | collective-permute-done | bytes 786464 | tf_op jit(solution)/shard_map/ppermute | solution.py:318
  189.0 2.3 convolution_convert_fusion.5
  191.3 18.3 %collective-permute-done.22 = bf16[640,768]{1,0:T(8,128)(2,1)S(1)} collective-permute-done((bf16[640,768]{1,0:T(8,128)(2,1)}, bf16[640,768]{1,0:T(8,128)(2,1)S(1)}, u32[]{:S(2)}, u32[]{:S(2)}) %collective-permute-start.22) | collective-permute-done | bytes 983072 | tf_op jit(solution)/shard_map/ppermute | solution.py:318
  211.0 15.5 %collective-permute-done.14.refs_1_ = bf16[8,64,768]{2,1,0:T(8,128)(2,1)S(1)} collective-permute-done((bf16[8,64,768]{2,1,0:T(8,128)(2,1)S(1)}, bf16[8,64,768]{2,1,0:T(8,128)(2,1)S(1)}, u32[]{:S(2)}, u32[]{:S(2)}) %collective-permute-start.14) | collective-permute-done | bytes 786464 | tf_op jit(solution)/shard_map/ppermute | solution.py:318
  226.5 14.6 %collective-permute-done.16.refs_3_ = bf16[8,64,768]{2,1,0:T(8,128)(2,1)S(1)} collective-permute-done((bf16[8,64,768]{2,1,0:T(8,128)(2,1)S(1)}, bf16[8,64,768]{2,1,0:T(8,128)(2,1)S(1)}, u32[]{:S(2)}, u32[]{:S(2)}) %collective-permute-start.16) | collective-permute-done | bytes 786464 | tf_op jit(solution)/shard_map/ppermute | solution.py:318
  242.7 3.2 convolution_convert_fusion.4
  246.0 3.7 collective-permute-start.24
  250.1 3.3 fusion.47.own
  255.2 3.1 rotate_rows.3
  262.8 21.8 %cached_attention.2 = (bf16[4,6,128,512]{3,2,1,0:T(8,128)(2,1)S(1)}, f32[4,6,128,512]{3,2,1,0:T(8,128)}, f32[4,8,512]{2,1,0:T(8,128)S(1)}, f32[4,8,512]{2,1,0:T(8,128)S(1)}) custom-call(s32[80]{0:T(128)S(1)} %broadcast_add_fusion.1.order, s32[80]{0:T(128)S(1)} %get-tuple-element.80.counts, s32[9]{0:T(128)S(1)} %select_reduce_fusion.4.starts, ...), custom_call_target="tpu_custom_call" | custom-call | flops 402653184 | bytes 786432 | tf_op jit(solution)/shard_map/cached_attention/pallas_call | solution.py:165
  284.7 3.5 add_convert_fusion
  288.2 6.7 %block_attention.2 = (bf16[800,256]{1,0:T(8,128)(2,1)S(1)}, bf16[800,256]{1,0:T(8,128)(2,1)S(1)}, bf16[800,256]{1,0:T(8,128)(2,1)S(1)}, bf16[800,256]{1,0:T(8,12...) custom-call(bf16[4,6,128,512]{3,2,1,0:T(8,128)(2,1)S(1)} %get-tuple-, ...), custom_call_target="tpu_custom_call" | custom-call | flops 100663296 | bytes 1572864 | tf_op jit(solution)/shard_map/block_attention/pallas_call | solution.py:255
  301.5 21.4 %collective-permute-done.26.other = bf16[800,256]{1,0:T(8,128)(2,1)S(1)} collective-permute-done((bf16[800,256]{1,0:T(8,128)(2,1)S(1)}, bf16[800,256]{1,0:T(8,128)(2,1)S(1)}, u32[]{:S(2)}, u32[]{:S(2)}) %collective-permute-start.26) | collective-permute-done | bytes 409632 | tf_op jit(solution)/shard_map/ppermute | solution.py:318
  329.7 22.0 %cached_attention.3 = (bf16[4,6,128,512]{3,2,1,0:T(8,128)(2,1)S(1)}, f32[4,6,128,512]{3,2,1,0:T(8,128)}, f32[4,8,512]{2,1,0:T(8,128)S(1)}, f32[4,8,512]{2,1,0:T(8,128)S(1)}) custom-call(s32[80]{0:T(128)S(1)} %broadcast_add_fusion.1.order, s32[80]{0:T(128)S(1)} %get-tuple-element.80.counts, s32[9]{0:T(128)S(1)} %select_reduce_fusion.4.starts, ...), custom_call_target="tpu_custom_call" | custom-call | flops 402653184 | bytes 786432 | tf_op jit(solution)/shard_map/cached_attention/pallas_call | solution.py:165
  363.7 2.2 constant_dynamic-update-slice_fusion.18
  366.0 2.8 copy-done.2
  368.7 6.7 %block_attention.3 = (bf16[800,256]{1,0:T(8,128)(2,1)S(1)}, bf16[800,256]{1,0:T(8,128)(2,1)S(1)}, bf16[800,256]{1,0:T(8,128)(2,1)S(1)}, bf16[800,256]{1,0:T(8,12...) custom-call(bf16[4,6,128,512]{3,2,1,0:T(8,128)(2,1)S(1)} %copy-done., ...), custom_call_target="tpu_custom_call" | custom-call | flops 100663296 | bytes 1572864 | tf_op jit(solution)/shard_map/block_attention/pallas_call | solution.py:255
  393.0 2.3 constant_dynamic-update-slice_fusion.16
  395.2 2.2 constant_dynamic-update-slice_fusion.15
  400.9 2.2 constant_dynamic-update-slice_fusion.14
  403.1 2.3 constant_dynamic-update-slice_fusion.13
  405.4 2.3 constant_dynamic-update-slice_fusion.12
  419.4 2.6 collective-permute-start.47
  422.0 2.3 convolution_convert_fusion.2
  424.5 3.1 convolution_convert_fusion.3
  438.1 3.3 convolution_convert_fusion
  441.9 2.3 fusion.4
  445.8 2.3 convolution_convert_fusion.1
  448.2 2.4 fusion.5
  451.2 10.7 %collective-permute-done.40 = bf16[256,1280]{1,0:T(8,128)(2,1)S(1)} collective-permute-done((bf16[256,1280]{1,0:T(8,128)(2,1)S(1)}, bf16[256,1280]{1,0:T(8,128)(2,1)S(1)}, u32[]{:S(2)}, u32[]{:S(2)}) %collective-permute-start.40) | collective-permute-done | bytes 655392 | tf_op jit(solution)/shard_map/ppermute | solution.py:610
  461.9 2.4 fusion.6
  464.4 10.6 %collective-permute-done.50 = bf16[256,1280]{1,0:T(8,128)(2,1)S(1)} collective-permute-done((bf16[256,1280]{1,0:T(8,128)(2,1)S(1)}, bf16[256,1280]{1,0:T(8,128)(2,1)S(1)}, u32[]{:S(2)}, u32[]{:S(2)}) %collective-permute-start.50) | collective-permute-done | bytes 655392 | tf_op jit(solution)/shard_map/ppermute | solution.py:610
  475.0 2.3 fusion.7
  (295 shorter events, 118.4 us)
Async XLA Ops:
  0.6 51.2 %collective-permute-start = (bf16[640,768]{1,0:T(8,128)(2,1)}, bf16[640,768]{1,0:T(8,128)(2,1)}, u32[]{:S(2)}, u32[]{:S(2)}) collective-permute-start(bf16[640,768]{1,0:T(8,128)(2,1)} %param.18), channel_id=1, source_target_pairs={{0,4},{4,0},{8,12},{12,8},{16,20},{20,16},{24,28},{28,24},{1,5},{5... | collective-permute-start | bytes 2949128 | tf_op jit(solution)/shard_map/ppermute | solution.py:318
  7.8 31.6 %collective-permute-start.3 = (bf16[512,640]{1,0:T(8,128)(2,1)}, bf16[512,640]{1,0:T(8,128)(2,1)S(1)}, u32[]{:S(2)}, u32[]{:S(2)}) collective-permute-start(bf16[512,640]{1,0:T(8,128)(2,1)} %bitcast.12), channel_id=1, source_target_pairs={{0,16},{4,20},{8,24},{12,28},{16,0},{20,4},{24,8},{28,12},{1,17},{... | collective-permute-start | bytes 1966088 | tf_op jit(solution)/shard_map/ppermute | solution.py:318
  11.6 31.7 %collective-permute-start.7 = (f32[8,64]{1,0:T(8,128)S(1)}, f32[8,64]{1,0:T(8,128)S(1)}, u32[]{:S(2)}, u32[]{:S(2)}) collective-permute-start(f32[8,64]{1,0:T(8,128)S(1)} %rsqrt.16), channel_id=1, source_target_pairs={{0,16},{4,20},{8,24},{12,28},{16,0},{20,4},{24,8},{28,12},{1,17},{... | collective-permute-start | bytes 6152 | tf_op jit(solution)/shard_map/ppermute | solution.py:318
  11.9 38.0 %collective-permute-start.1 = (bf16[640,768]{1,0:T(8,128)(2,1)}, bf16[640,768]{1,0:T(8,128)(2,1)}, u32[]{:S(2)}, u32[]{:S(2)}) collective-permute-start(bf16[640,768]{1,0:T(8,128)(2,1)} %param.18), channel_id=1, source_target_pairs={{0,8},{4,12},{8,0},{12,4},{16,24},{20,28},{24,16},{28,20},{1,9},{5... | collective-permute-start | bytes 2949128 | tf_op jit(solution)/shard_map/ppermute | solution.py:318
  39.3 15.6 %collective-permute-start.5 = (bf16[512,640]{1,0:T(8,128)(2,1)S(1)}, bf16[512,640]{1,0:T(8,128)(2,1)}, u32[]{:S(2)}, u32[]{:S(2)}) collective-permute-start(bf16[512,640]{1,0:T(8,128)(2,1)S(1)} %collective-permute-done.3), channel_id=1, source_target_pairs={{0,2},{1,3},{2,0},{3,1},{4,6},{5,7},{6,4},{7,5},{8,10},{9,11},{10,... | collective-permute-start | bytes 1966088 | tf_op jit(solution)/shard_map/ppermute | solution.py:318
  42.5 43.0 %collective-permute-start.10 = (bf16[640,768]{1,0:T(8,128)(2,1)}, bf16[640,768]{1,0:T(8,128)(2,1)}, u32[]{:S(2)}, u32[]{:S(2)}) collective-permute-start(bf16[640,768]{1,0:T(8,128)(2,1)} %param.19), channel_id=1, source_target_pairs={{0,8},{4,12},{8,0},{12,4},{16,24},{20,28},{24,16},{28,20},{1,9},{5... | collective-permute-start | bytes 2949128 | tf_op jit(solution)/shard_map/ppermute | solution.py:318
  49.9 35.6 %collective-permute-start.2 = (bf16[640,768]{1,0:T(8,128)(2,1)}, bf16[640,768]{1,0:T(8,128)(2,1)}, u32[]{:S(2)}, u32[]{:S(2)}) collective-permute-start(bf16[640,768]{1,0:T(8,128)(2,1)} %collective-permute-done.1), channel_id=1, source_target_pairs={{0,4},{4,0},{8,12},{12,8},{16,20},{20,16},{24,28},{28,24},{1,5},{5... | collective-permute-start | bytes 2949128 | tf_op jit(solution)/shard_map/ppermute | solution.py:318
  51.8 46.9 %collective-permute-start.12 = (bf16[640,768]{1,0:T(8,128)(2,1)}, bf16[640,768]{1,0:T(8,128)(2,1)}, u32[]{:S(2)}, u32[]{:S(2)}) collective-permute-start(bf16[640,768]{1,0:T(8,128)(2,1)} %param.21), channel_id=1, source_target_pairs={{0,16},{4,20},{8,24},{12,28},{16,0},{20,4},{24,8},{28,12},{1,17},{... | collective-permute-start | bytes 2949128 | tf_op jit(solution)/shard_map/ppermute | solution.py:318
  54.9 33.9 %collective-permute-start.6 = (bf16[512,640]{1,0:T(8,128)(2,1)}, bf16[512,640]{1,0:T(8,128)(2,1)S(1)}, u32[]{:S(2)}, u32[]{:S(2)}) collective-permute-start(bf16[512,640]{1,0:T(8,128)(2,1)} %collective-permute-done.5), channel_id=1, source_target_pairs={{0,1},{1,0},{2,3},{3,2},{4,5},{5,4},{6,7},{7,6},{8,9},{9,8},{10,11... | collective-permute-start | bytes 1966088 | tf_op jit(solution)/shard_map/ppermute | solution.py:318
  85.5 43.5 %collective-permute-start.13 = (bf16[640,768]{1,0:T(8,128)(2,1)}, bf16[640,768]{1,0:T(8,128)(2,1)}, u32[]{:S(2)}, u32[]{:S(2)}) collective-permute-start(bf16[640,768]{1,0:T(8,128)(2,1)} %param.20), channel_id=1, source_target_pairs={{0,8},{4,12},{8,0},{12,4},{16,24},{20,28},{24,16},{28,20},{1,9},{5... | collective-permute-start | bytes 2949128 | tf_op jit(solution)/shard_map/ppermute | solution.py:318
  85.5 43.5 %collective-permute-start.11 = (bf16[640,768]{1,0:T(8,128)(2,1)}, bf16[640,768]{1,0:T(8,128)(2,1)}, u32[]{:S(2)}, u32[]{:S(2)}) collective-permute-start(bf16[640,768]{1,0:T(8,128)(2,1)} %collective-permute-done.10), channel_id=1, source_target_pairs={{0,4},{4,0},{8,12},{12,8},{16,20},{20,16},{24,28},{28,24},{1,5},{5... | collective-permute-start | bytes 2949128 | tf_op jit(solution)/shard_map/ppermute | solution.py:318
  85.5 43.5 %collective-permute-start.9 = (bf16[640,768]{1,0:T(8,128)(2,1)}, bf16[640,768]{1,0:T(8,128)(2,1)}, u32[]{:S(2)}, u32[]{:S(2)}) collective-permute-start(bf16[640,768]{1,0:T(8,128)(2,1)} %param.19), channel_id=1, source_target_pairs={{0,4},{4,0},{8,12},{12,8},{16,20},{20,16},{24,28},{28,24},{1,5},{5... | collective-permute-start | bytes 2949128 | tf_op jit(solution)/shard_map/ppermute | solution.py:318
  91.3 37.7 %collective-permute-start.8 = (bf16[512,768]{1,0:T(8,128)(2,1)S(1)}, bf16[512,768]{1,0:T(8,128)(2,1)S(1)}, u32[]{:S(2)}, u32[]{:S(2)}) collective-permute-start(bf16[512,768]{1,0:T(8,128)(2,1)S(1)} %convolution_convert_fusion.6), channel_id=1, source_target_pairs={{0,16},{4,20},{8,24},{12,28},{16,0},{20,4},{24,8},{28,12},{1,17},{... | collective-permute-start | bytes 2359304 | tf_op jit(solution)/shard_map/ppermute | solution.py:318
  133.6 34.5 %collective-permute-start.17 = (bf16[8,64,768]{2,1,0:T(8,128)(2,1)}, bf16[8,64,768]{2,1,0:T(8,128)(2,1)S(1)}, u32[]{:S(2)}, u32[]{:S(2)}) collective-permute-start(bf16[8,64,768]{2,1,0:T(8,128)(2,1)} %bitcast.55), channel_id=1, source_target_pairs={{0,16},{4,20},{8,24},{12,28},{16,0},{20,4},{24,8},{28,12},{1,17},{... | collective-permute-start | bytes 2359304 | tf_op jit(solution)/shard_map/ppermute | solution.py:318
  136.5 41.0 %collective-permute-start.21 = (bf16[640,768]{1,0:T(8,128)(2,1)}, bf16[640,768]{1,0:T(8,128)(2,1)S(1)}, u32[]{:S(2)}, u32[]{:S(2)}) collective-permute-start(bf16[640,768]{1,0:T(8,128)(2,1)} %param.20), channel_id=1, source_target_pairs={{0,4},{4,0},{8,12},{12,8},{16,20},{20,16},{24,28},{28,24},{1,5},{5... | collective-permute-start | bytes 2949128 | tf_op jit(solution)/shard_map/ppermute | solution.py:318
  137.4 40.1 %collective-permute-start.15 = (bf16[8,64,768]{2,1,0:T(8,128)(2,1)}, bf16[8,64,768]{2,1,0:T(8,128)(2,1)S(1)}, u32[]{:S(2)}, u32[]{:S(2)}) collective-permute-start(bf16[8,64,768]{2,1,0:T(8,128)(2,1)} %bitcast.56), channel_id=1, source_target_pairs={{0,8},{4,12},{8,0},{12,4},{16,24},{20,28},{24,16},{28,20},{1,9},{5... | collective-permute-start | bytes 2359304 | tf_op jit(solution)/shard_map/ppermute | solution.py:318
  168.1 20.5 %collective-permute-start.18 = (bf16[8,64,768]{2,1,0:T(8,128)(2,1)S(1)}, bf16[8,64,768]{2,1,0:T(8,128)(2,1)S(1)}, u32[]{:S(2)}, u32[]{:S(2)}) collective-permute-start(bf16[8,64,768]{2,1,0:T(8,128)(2,1)S(1)} %collective-permute-done.17.refs_4_), channel_id=1, source_target_pairs={{0,4},{4,0},{8,12},{12,8},{16,20},{20,16},{24,28},{28,24},{1,5},{5... | collective-permute-start | bytes 2359304 | tf_op jit(solution)/shard_map/ppermute | solution.py:318
  169.9 39.7 %collective-permute-start.22 = (bf16[640,768]{1,0:T(8,128)(2,1)}, bf16[640,768]{1,0:T(8,128)(2,1)S(1)}, u32[]{:S(2)}, u32[]{:S(2)}) collective-permute-start(bf16[640,768]{1,0:T(8,128)(2,1)} %collective-permute-done.13), channel_id=1, source_target_pairs={{0,4},{4,0},{8,12},{12,8},{16,20},{20,16},{24,28},{28,24},{1,5},{5... | collective-permute-start | bytes 2949128 | tf_op jit(solution)/shard_map/ppermute | solution.py:318
  172.9 53.6 %collective-permute-start.14 = (bf16[8,64,768]{2,1,0:T(8,128)(2,1)S(1)}, bf16[8,64,768]{2,1,0:T(8,128)(2,1)S(1)}, u32[]{:S(2)}, u32[]{:S(2)}) collective-permute-start(bf16[8,64,768]{2,1,0:T(8,128)(2,1)S(1)} %bitcast.57), channel_id=1, source_target_pairs={{0,4},{4,0},{8,12},{12,8},{16,20},{20,16},{24,28},{28,24},{1,5},{5... | collective-permute-start | bytes 2359304 | tf_op jit(solution)/shard_map/ppermute | solution.py:318
  177.5 49.1 %collective-permute-start.19 = (bf16[8,64,768]{2,1,0:T(8,128)(2,1)S(1)}, bf16[8,64,768]{2,1,0:T(8,128)(2,1)S(1)}, u32[]{:S(2)}, u32[]{:S(2)}) collective-permute-start(bf16[8,64,768]{2,1,0:T(8,128)(2,1)S(1)} %collective-permute-done.17.refs_4_), channel_id=1, source_target_pairs={{0,8},{4,12},{8,0},{12,4},{16,24},{20,28},{24,16},{28,20},{1,9},{5... | collective-permute-start | bytes 2359304 | tf_op jit(solution)/shard_map/ppermute | solution.py:318
  177.6 63.6 %collective-permute-start.16 = (bf16[8,64,768]{2,1,0:T(8,128)(2,1)S(1)}, bf16[8,64,768]{2,1,0:T(8,128)(2,1)S(1)}, u32[]{:S(2)}, u32[]{:S(2)}) collective-permute-start(bf16[8,64,768]{2,1,0:T(8,128)(2,1)S(1)} %collective-permute-done.15.refs_2_), channel_id=1, source_target_pairs={{0,4},{4,0},{8,12},{12,8},{16,20},{20,16},{24,28},{28,24},{1,5},{5... | collective-permute-start | bytes 2359304 | tf_op jit(solution)/shard_map/ppermute | solution.py:318
  188.6 52.6 %collective-permute-start.20 = (bf16[8,64,768]{2,1,0:T(8,128)(2,1)S(1)}, bf16[8,64,768]{2,1,0:T(8,128)(2,1)S(1)}, u32[]{:S(2)}, u32[]{:S(2)}) collective-permute-start(bf16[8,64,768]{2,1,0:T(8,128)(2,1)S(1)} %collective-permute-done.18.refs_5_), channel_id=1, source_target_pairs={{0,8},{4,12},{8,0},{12,4},{16,24},{20,28},{24,16},{28,20},{1,9},{5... | collective-permute-start | bytes 2359304 | tf_op jit(solution)/shard_map/ppermute | solution.py:318
  209.7 36.3 %collective-permute-start.23 = (bf16[512,768]{1,0:T(8,128)(2,1)S(1)}, bf16[512,768]{1,0:T(8,128)(2,1)S(1)}, u32[]{:S(2)}, u32[]{:S(2)}) collective-permute-start(bf16[512,768]{1,0:T(8,128)(2,1)S(1)} %convolution_convert_fusion.5), channel_id=1, source_target_pairs={{0,16},{4,20},{8,24},{12,28},{16,0},{20,4},{24,8},{28,12},{1,17},{... | collective-permute-start | bytes 2359304 | tf_op jit(solution)/shard_map/ppermute | solution.py:318
  241.2 43.4 %collective-permute-start.33 = (bf16[640,768]{1,0:T(8,128)(2,1)}, bf16[640,768]{1,0:T(8,128)(2,1)}, u32[]{:S(2)}, u32[]{:S(2)}) collective-permute-start(bf16[640,768]{1,0:T(8,128)(2,1)} %param.21), channel_id=1, source_target_pairs={{0,8},{4,12},{8,0},{12,4},{16,24},{20,28},{24,16},{28,20},{1,9},{5... | collective-permute-start | bytes 2949128 | tf_op jit(solution)/shard_map/ppermute | solution.py:318
  246.0 38.7 %collective-permute-start.24 = (bf16[512,768]{1,0:T(8,128)(2,1)}, bf16[512,768]{1,0:T(8,128)(2,1)}, u32[]{:S(2)}, u32[]{:S(2)}) collective-permute-start(bf16[512,768]{1,0:T(8,128)(2,1)} %convolution_convert_fusion.4), channel_id=1, source_target_pairs={{0,16},{4,20},{8,24},{12,28},{16,0},{20,4},{24,8},{28,12},{1,17},{... | collective-permute-start | bytes 2359304 | tf_op jit(solution)/shard_map/ppermute | solution.py:318
  249.7 51.8 %collective-permute-start.35 = (bf16[640,768]{1,0:T(8,128)(2,1)}, bf16[640,768]{1,0:T(8,128)(2,1)}, u32[]{:S(2)}, u32[]{:S(2)}) collective-permute-start(bf16[640,768]{1,0:T(8,128)(2,1)} %collective-permute-done.12), channel_id=1, source_target_pairs={{0,4},{4,0},{8,12},{12,8},{16,20},{20,16},{24,28},{28,24},{1,5},{5... | collective-permute-start | bytes 2949128 | tf_op jit(solution)/shard_map/ppermute | solution.py:318
  253.4 104.7 %collective-permute-start.32 = (bf16[640,768]{1,0:T(8,128)(2,1)}, bf16[640,768]{1,0:T(8,128)(2,1)}, u32[]{:S(2)}, u32[]{:S(2)}) collective-permute-start(bf16[640,768]{1,0:T(8,128)(2,1)} %param.21), channel_id=1, source_target_pairs={{0,4},{4,0},{8,12},{12,8},{16,20},{20,16},{24,28},{28,24},{1,5},{5... | collective-permute-start | bytes 2949128 | tf_op jit(solution)/shard_map/ppermute | solution.py:318
  255.1 102.9 %collective-permute-start.36 = (bf16[640,768]{1,0:T(8,128)(2,1)}, bf16[640,768]{1,0:T(8,128)(2,1)}, u32[]{:S(2)}, u32[]{:S(2)}) collective-permute-start(bf16[640,768]{1,0:T(8,128)(2,1)} %collective-permute-done.12), channel_id=1, source_target_pairs={{0,8},{4,12},{8,0},{12,4},{16,24},{20,28},{24,16},{28,20},{1,9},{5... | collective-permute-start | bytes 2949128 | tf_op jit(solution)/shard_map/ppermute | solution.py:318
  284.6 75.5 %collective-permute-start.34 = (bf16[640,768]{1,0:T(8,128)(2,1)}, bf16[640,768]{1,0:T(8,128)(2,1)}, u32[]{:S(2)}, u32[]{:S(2)}) collective-permute-start(bf16[640,768]{1,0:T(8,128)(2,1)} %collective-permute-done.33), channel_id=1, source_target_pairs={{0,4},{4,0},{8,12},{12,8},{16,20},{20,16},{24,28},{28,24},{1,5},{5... | collective-permute-start | bytes 2949128 | tf_op jit(solution)/shard_map/ppermute | solution.py:318
  299.5 23.4 %collective-permute-start.26 = (bf16[800,256]{1,0:T(8,128)(2,1)S(1)}, bf16[800,256]{1,0:T(8,128)(2,1)S(1)}, u32[]{:S(2)}, u32[]{:S(2)}) collective-permute-start(bf16[800,256]{1,0:T(8,128)(2,1)S(1)} %get-tuple-element.60), channel_id=1, source_target_pairs={{0,4},{4,0},{8,12},{12,8},{16,20},{20,16},{24,28},{28,24},{1,5},{5... | collective-permute-start | bytes 1228808 | tf_op jit(solution)/shard_map/ppermute | solution.py:318
  301.5 64.4 %collective-permute-start.37 = (bf16[640,768]{1,0:T(8,128)(2,1)}, bf16[640,768]{1,0:T(8,128)(2,1)}, u32[]{:S(2)}, u32[]{:S(2)}) collective-permute-start(bf16[640,768]{1,0:T(8,128)(2,1)} %collective-permute-done.35), channel_id=1, source_target_pairs={{0,8},{4,12},{8,0},{12,4},{16,24},{20,28},{24,16},{28,20},{1,9},{5... | collective-permute-start | bytes 2949128 | tf_op jit(solution)/shard_map/ppermute | solution.py:318
  323.7 31.7 %collective-permute-start.29 = (bf16[800,256]{1,0:T(8,128)(2,1)}, bf16[800,256]{1,0:T(8,128)(2,1)}, u32[]{:S(2)}, u32[]{:S(2)}) collective-permute-start(bf16[800,256]{1,0:T(8,128)(2,1)} %get-tuple-element.64), channel_id=1, source_target_pairs={{0,8},{4,12},{8,0},{12,4},{16,24},{20,28},{24,16},{28,20},{1,9},{5... | collective-permute-start | bytes 1228808 | tf_op jit(solution)/shard_map/ppermute | solution.py:318
  355.4 25.4 %collective-permute-start.25 = (bf16[800,256]{1,0:T(8,128)(2,1)}, bf16[800,256]{1,0:T(8,128)(2,1)}, u32[]{:S(2)}, u32[]{:S(2)}) collective-permute-start(bf16[800,256]{1,0:T(8,128)(2,1)} %copy-done.31), channel_id=1, source_target_pairs={{0,4},{4,0},{8,12},{12,8},{16,20},{20,16},{24,28},{28,24},{1,5},{5... | collective-permute-start | bytes 1228808 | tf_op jit(solution)/shard_map/ppermute | solution.py:318
  358.1 24.8 %collective-permute-start.28 = (bf16[800,256]{1,0:T(8,128)(2,1)}, bf16[800,256]{1,0:T(8,128)(2,1)}, u32[]{:S(2)}, u32[]{:S(2)}) collective-permute-start(bf16[800,256]{1,0:T(8,128)(2,1)} %copy-done.30), channel_id=1, source_target_pairs={{0,8},{4,12},{8,0},{12,4},{16,24},{20,28},{24,16},{28,20},{1,9},{5... | collective-permute-start | bytes 1228808 | tf_op jit(solution)/shard_map/ppermute | solution.py:318
  358.1 29.8 %collective-permute-start.27 = (bf16[800,256]{1,0:T(8,128)(2,1)}, bf16[800,256]{1,0:T(8,128)(2,1)}, u32[]{:S(2)}, u32[]{:S(2)}) collective-permute-start(bf16[800,256]{1,0:T(8,128)(2,1)} %merge_partials.15), channel_id=1, source_target_pairs={{0,8},{4,12},{8,0},{12,4},{16,24},{20,28},{24,16},{28,20},{1,9},{5... | collective-permute-start | bytes 1228808 | tf_op jit(solution)/shard_map/ppermute | solution.py:318
  360.1 24.8 %collective-permute-start.30 = (bf16[800,256]{1,0:T(8,128)(2,1)}, bf16[800,256]{1,0:T(8,128)(2,1)}, u32[]{:S(2)}, u32[]{:S(2)}) collective-permute-start(bf16[800,256]{1,0:T(8,128)(2,1)} %merge_partials.18), channel_id=1, source_target_pairs={{0,4},{4,0},{8,12},{12,8},{16,20},{20,16},{24,28},{28,24},{1,5},{5... | collective-permute-start | bytes 1228808 | tf_op jit(solution)/shard_map/ppermute | solution.py:318
  378.5 19.0 %collective-permute-start.45 = (bf16[800,256]{1,0:T(8,128)(2,1)}, bf16[800,256]{1,0:T(8,128)(2,1)S(1)}, u32[]{:S(2)}, u32[]{:S(2)}) collective-permute-start(bf16[800,256]{1,0:T(8,128)(2,1)} %get-tuple-element.79), channel_id=1, source_target_pairs={{0,8},{4,12},{8,0},{12,4},{16,24},{20,28},{24,16},{28,20},{1,9},{5... | collective-permute-start | bytes 1228808 | tf_op jit(solution)/shard_map/ppermute | solution.py:318
  387.0 20.7 %collective-permute-start.31 = (bf16[800,256]{1,0:T(8,128)(2,1)}, bf16[800,256]{1,0:T(8,128)(2,1)S(1)}, u32[]{:S(2)}, u32[]{:S(2)}) collective-permute-start(bf16[800,256]{1,0:T(8,128)(2,1)} %merge_partials.19), channel_id=1, source_target_pairs={{0,16},{4,20},{8,24},{12,28},{16,0},{20,4},{24,8},{28,12},{1,17},{... | collective-permute-start | bytes 1228808 | tf_op jit(solution)/shard_map/ppermute | solution.py:318
  389.9 37.7 %collective-permute-start.41 = (bf16[800,256]{1,0:T(8,128)(2,1)S(1)}, bf16[800,256]{1,0:T(8,128)(2,1)S(1)}, u32[]{:S(2)}, u32[]{:S(2)}) collective-permute-start(bf16[800,256]{1,0:T(8,128)(2,1)S(1)} %get-tuple-element.73), channel_id=1, source_target_pairs={{0,4},{4,0},{8,12},{12,8},{16,20},{20,16},{24,28},{28,24},{1,5},{5... | collective-permute-start | bytes 1228808 | tf_op jit(solution)/shard_map/ppermute | solution.py:318
  390.0 20.5 %collective-permute-start.42 = (bf16[800,256]{1,0:T(8,128)(2,1)S(1)}, bf16[800,256]{1,0:T(8,128)(2,1)S(1)}, u32[]{:S(2)}, u32[]{:S(2)}) collective-permute-start(bf16[800,256]{1,0:T(8,128)(2,1)S(1)} %get-tuple-element.75), channel_id=1, source_target_pairs={{0,4},{4,0},{8,12},{12,8},{16,20},{20,16},{24,28},{28,24},{1,5},{5... | collective-permute-start | bytes 1228808 | tf_op jit(solution)/shard_map/ppermute | solution.py:318
  392.0 22.5 %collective-permute-start.44 = (bf16[800,256]{1,0:T(8,128)(2,1)S(1)}, bf16[800,256]{1,0:T(8,128)(2,1)S(1)}, u32[]{:S(2)}, u32[]{:S(2)}) collective-permute-start(bf16[800,256]{1,0:T(8,128)(2,1)S(1)} %get-tuple-element.77), channel_id=1, source_target_pairs={{0,8},{4,12},{8,0},{12,4},{16,24},{20,28},{24,16},{28,20},{1,9},{5... | collective-permute-start | bytes 1228808 | tf_op jit(solution)/shard_map/ppermute | solution.py:318
  400.3 17.0 %collective-permute-start.46 = (bf16[800,256]{1,0:T(8,128)(2,1)}, bf16[800,256]{1,0:T(8,128)(2,1)}, u32[]{:S(2)}, u32[]{:S(2)}) collective-permute-start(bf16[800,256]{1,0:T(8,128)(2,1)} %merge_partials.25), channel_id=1, source_target_pairs={{0,4},{4,0},{8,12},{12,8},{16,20},{20,16},{24,28},{28,24},{1,5},{5... | collective-permute-start | bytes 1228808 | tf_op jit(solution)/shard_map/ppermute | solution.py:318
  413.3 17.1 %collective-permute-start.43 = (bf16[800,256]{1,0:T(8,128)(2,1)}, bf16[800,256]{1,0:T(8,128)(2,1)S(1)}, u32[]{:S(2)}, u32[]{:S(2)}) collective-permute-start(bf16[800,256]{1,0:T(8,128)(2,1)} %merge_partials.22), channel_id=1, source_target_pairs={{0,8},{4,12},{8,0},{12,4},{16,24},{20,28},{24,16},{28,20},{1,9},{5... | collective-permute-start | bytes 1228808 | tf_op jit(solution)/shard_map/ppermute | solution.py:318
  419.4 16.0 %collective-permute-start.47 = (bf16[800,256]{1,0:T(8,128)(2,1)}, bf16[800,256]{1,0:T(8,128)(2,1)S(1)}, u32[]{:S(2)}, u32[]{:S(2)}) collective-permute-start(bf16[800,256]{1,0:T(8,128)(2,1)} %merge_partials.26), channel_id=1, source_target_pairs={{0,16},{4,20},{8,24},{12,28},{16,0},{20,4},{24,8},{28,12},{1,17},{... | collective-permute-start | bytes 1228808 | tf_op jit(solution)/shard_map/ppermute | solution.py:318
  424.3 17.7 %collective-permute-start.39 = (bf16[256,1280]{1,0:T(8,128)(2,1)S(1)}, bf16[256,1280]{1,0:T(8,128)(2,1)S(1)}, u32[]{:S(2)}, u32[]{:S(2)}) collective-permute-start(bf16[256,1280]{1,0:T(8,128)(2,1)S(1)} %convolution_convert_fusion.2), channel_id=1, source_target_pairs={{0,1},{1,0},{2,3},{3,2},{4,5},{5,4},{6,7},{7,6},{8,9},{9,8},{10,11... | collective-permute-start | bytes 1966088 | tf_op jit(solution)/shard_map/ppermute | solution.py:610
  444.2 17.7 %collective-permute-start.40 = (bf16[256,1280]{1,0:T(8,128)(2,1)S(1)}, bf16[256,1280]{1,0:T(8,128)(2,1)S(1)}, u32[]{:S(2)}, u32[]{:S(2)}) collective-permute-start(bf16[256,1280]{1,0:T(8,128)(2,1)S(1)} %fusion.4), channel_id=1, source_target_pairs={{0,2},{1,3},{2,0},{3,1},{4,6},{5,7},{6,4},{7,5},{8,10},{9,11},{10,... | collective-permute-start | bytes 1966088 | tf_op jit(solution)/shard_map/ppermute | solution.py:610
  448.1 16.3 %collective-permute-start.48 = (bf16[256,1280]{1,0:T(8,128)(2,1)S(1)}, bf16[256,1280]{1,0:T(8,128)(2,1)S(1)}, u32[]{:S(2)}, u32[]{:S(2)}) collective-permute-start(bf16[256,1280]{1,0:T(8,128)(2,1)S(1)} %convolution_convert_fusion.1), channel_id=1, source_target_pairs={{0,1},{1,0},{2,3},{3,2},{4,5},{5,4},{6,7},{7,6},{8,9},{9,8},{10,11... | collective-permute-start | bytes 1966088 | tf_op jit(solution)/shard_map/ppermute | solution.py:610
  450.6 24.4 %collective-permute-start.50 = (bf16[256,1280]{1,0:T(8,128)(2,1)S(1)}, bf16[256,1280]{1,0:T(8,128)(2,1)S(1)}, u32[]{:S(2)}, u32[]{:S(2)}) collective-permute-start(bf16[256,1280]{1,0:T(8,128)(2,1)S(1)} %fusion.5), channel_id=1, source_target_pairs={{0,2},{1,3},{2,0},{3,1},{4,6},{5,7},{6,4},{7,5},{8,10},{9,11},{10,... | collective-permute-start | bytes 1966088 | tf_op jit(solution)/shard_map/ppermute | solution.py:610
  (73 other events, 804.8 us)
where the time goes:
time: 481 us; the launch traced here: 479 us
  waiting for transfers between devices  217 us (45%)
  Pallas kernels  92.1 us (19%)
  local copies, waits for them, and re-layouts  63.8 us (13%)
  starting transfers between devices  54.1 us (11%)
  matrix products  38.2 us (8%)
  other arithmetic  11.8 us (2%)
    ppermute x45, waiting for transfers between devices, step(): return lax.ppermute(value, self.mesh_axis, pairs)  196 us
    unnamed x156, local copies, waits for them, and re-layouts  54.2 us
    ppermute x45, starting transfers between devices, step(): return lax.ppermute(value, self.mesh_axis, pairs)  51.3 us
    pallas_call x2, Pallas kernels, cached_attention(): pl.pallas_call(functools.partial(cached_kernel, sources, first), out_shap...  43.7 us
    pallas_call x14, Pallas kernels, merge(): pl.pallas_call(merge_kernel, out_shape=jax.ShapeDtypeStruct(own.shape, ow...  28.7 us
    ppermute x6, waiting for transfers between devices, per_device(): lax.ppermute(sent, 'head', pairs).astype(jnp.float32)  21.3 us
    dot_general x8, matrix products, per_device(): lax.dot_general(context, features_of(target), (((0,), (1,)), ((), ())), p...  20.3 us
    dot_general x6, matrix products, product(): return jnp.dot(left, weight, preferred_element_type=jnp.float32)  17.9 us
  transfers between devices with their start and end apart: 51, of which 14 were waited for; matrix products, arithmetic and copies ran while one was open for 17% of the time, Pallas kernels for 19%

commit v1 on v0

--- a/solution.py
+++ b/solution.py
@@ -56,14 +56,13 @@
     )
 
 
-def cached_kernel(sources, first, order, counts, starts, lives, fulls, *refs):
+def cached_kernel(sources, order, counts, starts, lives, fulls, *refs):
     q_refs = refs[:sources]
     k_hbm, v_hbm, q_t, acc, peak, total, kbuf, vbuf, sem = refs[sources:]
-    requests = acc.shape[0]
-    _, rows, width = q_refs[0].shape
+    requests, rows, width = q_refs[0].shape
     heads = width // HD
     columns = sources * rows
-    end = starts[first + requests]
+    end = starts[requests]
 
     def copies(item):
         slot = lax.rem(item, SLOTS)
@@ -109,19 +108,18 @@
                 vbuf[place, head_span(head)], weights
             )
 
-    begin = starts[first]
     for item in range(SLOTS - 2):
-        fetch(begin + item)
+        fetch(item)
 
     def request(r, carry):
         for head in range(heads):
-            query = jnp.concatenate([ref[first + r, :, head_span(head)] for ref in q_refs], axis=0)
+            query = jnp.concatenate([ref[r, :, head_span(head)] for ref in q_refs], axis=0)
             q_t[r, head] = query.T
             acc[r, head] = jnp.zeros((HD, columns), jnp.float32)
         peak[r] = jnp.full((8, columns), MASKED, jnp.float32)
         total[r] = jnp.zeros((8, columns), jnp.float32)
-        start = starts[first + r]
-        pairs = fulls[first + r] // 2
+        start = starts[r]
+        pairs = fulls[r] // 2
 
         def pair(step, inner):
             item = start + 2 * step
@@ -135,7 +133,7 @@
 
         lax.fori_loop(0, pairs, pair, 0)
         rest = start + 2 * pairs
-        after_rest = start + lives[first + r]
+        after_rest = start + lives[r]
 
         @pl.when(rest < after_rest)
         def _():
@@ -155,15 +153,14 @@
     lax.fori_loop(0, requests, request, 0)
 
 
-def cached_attention(first, queries, key_cache, value_cache, plan):
+def cached_attention(queries, key_cache, value_cache, plan):
     sources = len(queries)
-    whole, rows, width = queries[0].shape
-    requests = whole // CHUNKS
+    requests, rows, width = queries[0].shape
     heads = width // HD
     columns = sources * rows
-    touched = key_cache.shape[0] * PAGE // CHUNKS
+    touched = key_cache.shape[0] * PAGE
     return pl.pallas_call(
-        functools.partial(cached_kernel, sources, first),
+        functools.partial(cached_kernel, sources),
         out_shape=[
             jax.ShapeDtypeStruct((requests, heads, HD, columns), jnp.bfloat16),
             jax.ShapeDtypeStruct((requests, heads, HD, columns), jnp.float32),
@@ -193,30 +190,30 @@
     return jnp.concatenate([high, middle, values - high - middle, jnp.zeros_like(values)], axis=0)
 
 
-def block_kernel(sources, first, q_t, acc, peak, total, kblk, vblk, *refs):
-    o_refs = refs[:sources]
-    sums = refs[sources]
+def block_kernel(sources, q_t, acc, peak, total, kblk, vblk, *refs):
+    sums = refs[-1]
     requests, heads, _, columns = q_t.shape
     rows = kblk.shape[1]
     width = heads * HD
-    lanes = min(HD, requests * rows)
+    chunk = requests // CHUNKS
+    lanes = min(HD, chunk * rows)
     together = lanes // rows
     key_pass = lax.broadcasted_iota(jnp.int32, (rows, columns), 0) // (rows // 2)
     query_pass = (lax.broadcasted_iota(jnp.int32, (rows, columns), 1) // (rows // 2)) % 2
     same_pass = key_pass == query_pass
     sums[...] = jnp.zeros_like(sums)
 
-    def group(g, carry):
-        if requests == together:
+    def group(first, o_refs, g, carry):
+        if chunk == together:
             place = slice(0, lanes)
         else:
             place = pl.ds(pl.multiple_of(g * lanes, lanes), lanes)
         for head in range(heads):
             means = []
             for item in range(together):
-                r = g * together + item
+                r = first + g * together + item
                 scores = jnp.dot(
-                    kblk[first + r, :, head_span(head)], q_t[r, head], preferred_element_type=jnp.float32
+                    kblk[r, :, head_span(head)], q_t[r, head], preferred_element_type=jnp.float32
                 )
                 scores = jnp.where(same_pass, scores, MASKED)
                 before = peak[r, head : head + 1, :]
@@ -227,7 +224,7 @@
                     weights, axis=0, keepdims=True
                 )
                 summed = acc[r, head] * shrink + values_by_weights(
-                    vblk[first + r, :, head_span(head)], weights
+                    vblk[r, :, head_span(head)], weights
                 )
                 means.append(summed * (1.0 / weight_sum))
                 sums[item, head : head + 1, :] = top * EXP2_SCALE + jnp.log2(weight_sum)
@@ -244,19 +241,23 @@
             ).astype(jnp.bfloat16)
         return carry
 
-    lax.fori_loop(0, requests // together, group, 0)
-
-
-def block_attention(sources, first, state, kblk, vblk):
+    for number in range(CHUNKS):
+        o_refs = refs[number * sources : (number + 1) * sources]
+        body = functools.partial(group, number * chunk, o_refs)
+        lax.fori_loop(0, chunk // together, body, 0)
+
+
+def block_attention(sources, state, kblk, vblk):
     requests, heads, _, columns = state[0].shape
     rows = kblk.shape[1]
-    together = min(HD, requests * rows) // rows
-    piece = jax.ShapeDtypeStruct((heads * HD + SUM_ROWS, requests * rows), jnp.bfloat16)
-    return pl.pallas_call(
-        functools.partial(block_kernel, sources, first),
-        out_shape=[piece] * sources,
+    chunk = requests // CHUNKS
+    together = min(HD, chunk * rows) // rows
+    piece = jax.ShapeDtypeStruct((heads * HD + SUM_ROWS, chunk * rows), jnp.bfloat16)
+    pieces = pl.pallas_call(
+        functools.partial(block_kernel, sources),
+        out_shape=[piece] * (CHUNKS * sources),
         in_specs=[IN_VMEM] * 6,
-        out_specs=[IN_VMEM] * sources,
+        out_specs=[IN_VMEM] * (CHUNKS * sources),
         scratch_shapes=[pltpu.VMEM((together, 8, columns), jnp.float32)],
         compiler_params=pltpu.CompilerParams(vmem_limit_bytes=VMEM_BYTES),
         cost_estimate=pl.CostEstimate(
@@ -266,6 +267,7 @@
         ),
         name="block_attention",
     )(*state, kblk, vblk)
+    return [list(pieces[number * sources : (number + 1) * sources]) for number in range(CHUNKS)]
 
 
 def merge_kernel(own, other, out):
@@ -301,6 +303,34 @@
         ),
         name="merge_partials",
     )(own, other)
+
+
+def join_kernel(count, *refs):
+    whole, sem = refs[count], refs[count + 1]
+    rows = refs[0].shape[0]
+    copies = [
+        pltpu.make_async_copy(refs[place], whole.at[pl.ds(place * rows, rows)], sem.at[place])
+        for place in range(count)
+    ]
+    for copy in copies:
+        copy.start()
+    for copy in copies:
+        copy.wait()
+
+
+def join_rows(shards):
+    count, (rows, width) = len(shards), shards[0].shape
+    return pl.pallas_call(
+        functools.partial(join_kernel, count),
+        out_shape=jax.ShapeDtypeStruct((count * rows, width), shards[0].dtype),
+        in_specs=[IN_HBM] * count,
+        out_specs=IN_HBM,
+        scratch_shapes=[pltpu.SemaphoreType.DMA((count,))],
+        cost_estimate=pl.CostEstimate(
+            flops=0, bytes_accessed=4 * count * rows * width, transcendentals=0
+        ),
+        name="join_rows",
+    )(*shards)
 
 
 class Axis:
@@ -432,9 +462,10 @@
     picked = raw_rows([place_of(1, flat // x_size, flat % x_size) for flat in flats])
     fetched = half_axis.step(picked)
     query_shards = gather_plane(w_query, picked, None)
-    key_shards = gather_plane(w_key, fetched, query_shards[half_order[-1]])
+    key_shards = gather_plane(w_key, fetched, picked)
+    fetched = after(fetched, key_shards[(0, 0, 1)])
     value_shards = gather_plane(
-        w_value, key_shards[(0, 1, 0)], key_shards[half_order[-1]]
+        w_value, query_shards[(0, 1, 0)], query_shards[half_order[-1]]
     )
     far_out = half_axis.step(after(w_out, (fetched, query_shards[(0, 1, 0)])))
 
@@ -499,13 +530,14 @@
     chunk = requests // CHUNKS
 
     sent_query = product(other_rows, query_weight).astype(jnp.bfloat16)
-    received_query = after(
-        half_axis.step(sent_query), (key_shards, far_out, value_shards[(0, 1, 0)])
-    )
+    received_query = half_axis.step(sent_query)
     near = rotated_sum(
         product(own_rows, query_weight), received_query, cosine, sine
     ).reshape(piece)
-    far = half_axis.step(near)
+    near = after(
+        near, (key_shards, far_out, value_shards[(0, 1, 0)], value_shards[(0, 0, 1)])
+    )
+    far = after(half_axis.step(near), value_shards)
     trees = [gather_tree(near, (z_axis, x_axis)), gather_tree(far, (x_axis, z_axis))]
     every_query = [trees[key[0]][with_entry(key, 0, 0)] for key in full_order]
 
@@ -557,20 +589,17 @@
     own_out = gather_tree(after(w_out, every_query), (z_axis, x_axis))
     far_out = gather_tree(after(far_out, every_query), (x_axis, z_axis))
     out_shards = [(own_out, far_out)[key[0]][with_entry(key, 0, 0)] for key in full_order]
-    out_weight = jnp.concatenate(out_shards, axis=0)
+    out_weight = join_rows(out_shards)
     out_width = model_width // head_size
-    states = [
-        cached_attention(number * chunk, every_query, key_cache, value_cache, plan)
-        for number in range(CHUNKS)
-    ]
+    state = cached_attention(every_query, key_cache, value_cache, plan)
+    first_steps = [tree[key] for tree in (own_out, far_out) for key in ((0, 1, 0), (0, 0, 1))]
+    pieces_of = block_attention(seq_size, state, new_keys, after(new_values, first_steps))
     results = []
     for number in range(CHUNKS):
-        block_values = new_values
-        if number == CHUNKS - 1:
-            block_values = after(block_values, out_shards)
-        pieces = block_attention(
-            seq_size, number * chunk, states[number], new_keys, block_values
-        )
+        pieces = pieces_of[number]
+        if number == 0:
+            for mine in (0, half_size):
+                pieces[mine] = after(pieces[mine], out_shards)
 
         def parts_for(half_steps):
             return {

time: 481 us -> 744 us (1.55)
  Pallas kernels: 92.1 us -> 333 us
  waiting for transfers between devices: 217 us -> 273 us
  local copies, waits for them, and re-layouts: 63.8 us -> 40.3 us
  starting transfers between devices: 54.1 us -> 44.3 us
    pallas_call x4 -> x3, Pallas kernels: 57.2 us -> 298 us  [the longest x1 239 us: join_rows(): pl.pallas_call(functools.partial(join_kernel, count), out_shape=jax.Shape...]
    ppermute x45, waiting for transfers between devices: 196 us -> 251 us  [step(): return lax.ppermute(value, self.mesh_axis, pairs)]
    unnamed x156 -> x127, local copies, waits for them, and re-layouts: 54.2 us -> 31.7 us
    ppermute x45, starting transfers between devices: 51.3 us -> 41.4 us  [step(): return lax.ppermute(value, self.mesh_axis, pairs)]
  transfers between devices with their start and end apart: 51 -> 51, of which waited for: 14 -> 20; matrix products, arithmetic and copies ran while one was open for 17% -> 9% of each run, Pallas kernels for 19% -> 42%
where the time goes in v1:
time: 744 us; the launch traced here: 743 us
  Pallas kernels  333 us (45%)
  waiting for transfers between devices  273 us (37%)
  starting transfers between devices  44.3 us (6%)
  local copies, waits for them, and re-layouts  40.3 us (5%)
  matrix products  38.1 us (5%)
  other arithmetic  12.6 us (2%)
    ppermute x45, waiting for transfers between devices, step(): return lax.ppermute(value, self.mesh_axis, pairs)  251 us
    pallas_call x1, Pallas kernels, join_rows(): pl.pallas_call(functools.partial(join_kernel, count), out_shape=jax.Shape...  239 us
    ppermute x45, starting transfers between devices, step(): return lax.ppermute(value, self.mesh_axis, pairs)  41.4 us
    pallas_call x1, Pallas kernels, cached_attention(): pl.pallas_call(functools.partial(cached_kernel, sources), out_shape=[jax....  40.2 us
    unnamed x127, local copies, waits for them, and re-layouts  31.7 us
    pallas_call x14, Pallas kernels, merge(): pl.pallas_call(merge_kernel, out_shape=jax.ShapeDtypeStruct(own.shape, ow...  28.8 us
    ppermute x6, waiting for transfers between devices, per_device(): lax.ppermute(sent, 'head', pairs).astype(jnp.float32)  21.6 us
    dot_general x8, matrix products, per_device(): lax.dot_general(context, features_of(target), (((0,), (1,)), ((), ())), p...  19.6 us
  transfers between devices with their start and end apart: 51, of which 20 were waited for; matrix products, arithmetic and copies ran while one was open for 9% of the time, Pallas kernels for 42%

profile of v1, /device:TPU:0, one launch (start us, length us, event | category | flops | bytes accessed | tf_op | source)
XLA Modules:
  0.0 743.0 jit_solution(14260488255964833107)
XLA Ops:
  1.5 2.5 dynamic-slice_bitcast_fusion.4
  5.0 4.0 collective-permute-start.3
  19.0 19.2 %collective-permute-done.3 = bf16[512,640]{1,0:T(8,128)(2,1)S(1)} collective-permute-done((bf16[512,640]{1,0:T(8,128)(2,1)}, bf16[512,640]{1,0:T(8,128)(2,1)S(1)}, u32[]{:S(2)}, u32[]{:S(2)}) %collective-permute-start.3) | collective-permute-done | bytes 655392 | tf_op jit(solution)/shard_map/ppermute | solution.py:348
  38.9 14.7 %collective-permute-done.4 = bf16[640,768]{1,0:T(8,128)(2,1)} collective-permute-done((bf16[640,768]{1,0:T(8,128)(2,1)}, bf16[640,768]{1,0:T(8,128)(2,1)}, u32[]{:S(2)}, u32[]{:S(2)}) %collective-permute-start.4) | collective-permute-done | bytes 983072 | tf_op jit(solution)/shard_map/ppermute | solution.py:348
  55.7 2.2 constant_dynamic-update-slice_fusion.3
  62.4 2.2 constant_dynamic-update-slice_fusion.2
  64.6 4.4 collective-permute-done.6
  74.9 7.9 %collective-permute-done.2 = bf16[640,768]{1,0:T(8,128)(2,1)} collective-permute-done((bf16[640,768]{1,0:T(8,128)(2,1)}, bf16[640,768]{1,0:T(8,128)(2,1)}, u32[]{:S(2)}, u32[]{:S(2)}) %collective-permute-start.2) | collective-permute-done | bytes 983072 | tf_op jit(solution)/shard_map/ppermute | solution.py:348
  85.8 2.3 convolution_convert_fusion.6
  88.7 13.7 %collective-permute-done.13 = bf16[640,768]{1,0:T(8,128)(2,1)} collective-permute-done((bf16[640,768]{1,0:T(8,128)(2,1)}, bf16[640,768]{1,0:T(8,128)(2,1)}, u32[]{:S(2)}, u32[]{:S(2)}) %collective-permute-start.13) | collective-permute-done | bytes 983072 | tf_op jit(solution)/shard_map/ppermute | solution.py:348
  103.0 3.4 fusion.46.own
  106.4 44.4 %collective-permute-done.9.received = bf16[512,768]{1,0:T(8,128)(2,1)S(1)} collective-permute-done((bf16[512,768]{1,0:T(8,128)(2,1)S(1)}, bf16[512,768]{1,0:T(8,128)(2,1)S(1)}, u32[]{:S(2)}, u32[]{:S(2)}) %collective-permute-start.9) | collective-permute-done | bytes 786464 | tf_op jit(solution)/shard_map/ppermute | solution.py:348
  152.3 3.1 rotate_rows.2
  161.2 30.1 %collective-permute-done.18.refs_4_ = bf16[8,64,768]{2,1,0:T(8,128)(2,1)S(1)} collective-permute-done((bf16[8,64,768]{2,1,0:T(8,128)(2,1)}, bf16[8,64,768]{2,1,0:T(8,128)(2,1)S(1)}, u32[]{:S(2)}, u32[]{:S(2)}) %collective-permute-start.18) | collective-permute-done | bytes 786464 | tf_op jit(solution)/shard_map/ppermute | solution.py:348
  194.2 2.3 convolution_convert_fusion.5
  197.7 13.0 %collective-permute-done.20.refs_5_ = bf16[8,64,768]{2,1,0:T(8,128)(2,1)S(1)} collective-permute-done((bf16[8,64,768]{2,1,0:T(8,128)(2,1)S(1)}, bf16[8,64,768]{2,1,0:T(8,128)(2,1)S(1)}, u32[]{:S(2)}, u32[]{:S(2)}) %collective-permute-start.20) | collective-permute-done | bytes 786464 | tf_op jit(solution)/shard_map/ppermute | solution.py:348
  214.9 3.0 collective-permute-start.21
  218.4 3.2 convolution_convert_fusion.4
  221.6 25.6 %collective-permute-done.23.received = bf16[512,768]{1,0:T(8,128)(2,1)S(1)} collective-permute-done((bf16[512,768]{1,0:T(8,128)(2,1)S(1)}, bf16[512,768]{1,0:T(8,128)(2,1)S(1)}, u32[]{:S(2)}, u32[]{:S(2)}) %collective-permute-start.23) | collective-permute-done | bytes 786464 | tf_op jit(solution)/shard_map/ppermute | solution.py:348
  248.1 18.9 %collective-permute-done.21.refs_6_ = bf16[8,64,768]{2,1,0:T(8,128)(2,1)S(1)} collective-permute-done((bf16[8,64,768]{2,1,0:T(8,128)(2,1)S(1)}, bf16[8,64,768]{2,1,0:T(8,128)(2,1)S(1)}, u32[]{:S(2)}, u32[]{:S(2)}) %collective-permute-start.21) | collective-permute-done | bytes 786464 | tf_op jit(solution)/shard_map/ppermute | solution.py:348
  268.8 15.2 %collective-permute-done.22.refs_7_ = bf16[8,64,768]{2,1,0:T(8,128)(2,1)S(1)} collective-permute-done((bf16[8,64,768]{2,1,0:T(8,128)(2,1)S(1)}, bf16[8,64,768]{2,1,0:T(8,128)(2,1)S(1)}, u32[]{:S(2)}, u32[]{:S(2)}) %collective-permute-start.22) | collective-permute-done | bytes 786464 | tf_op jit(solution)/shard_map/ppermute | solution.py:348
  289.0 3.3 fusion.47.own
  292.3 3.1 rotate_rows.3
  300.0 40.2 %cached_attention.1 = (bf16[8,6,128,512]{3,2,1,0:T(8,128)(2,1)S(1)}, f32[8,6,128,512]{3,2,1,0:T(8,128)}, f32[8,8,512]{2,1,0:T(8,128)S(1)}, f32[8,8,512]{2,1,0:T(8,128)S(1)}) custom-call(s32[80]{0:T(128)S(1)} %broadcast_add_fusion.1.order, s32[80]{0:T(128)S(1)} %get-tuple-element.80.counts, s32[9]{0:T(128)S(1)} %select_reduce_fusion.4.starts, ...), custom_call_target="tpu_custom_call" | custom-call | flops 805306368 | bytes 1572864 | tf_op jit(solution)/shard_map/cached_attention/pallas_call | solution.py:162
  340.2 4.1 add_convert_fusion
  344.4 18.6 %block_attention.1 = (bf16[800,256]{1,0:T(8,128)(2,1)S(1)}, bf16[800,256]{1,0:T(8,128)(2,1)S(1)}, bf16[800,256]{1,0:T(8,128)(2,1)S(1)}, bf16[800,256]{1,0:T(8,12...) custom-call(bf16[8,6,128,512]{3,2,1,0:T(8,128)(2,1)} %copy-done, ...), custom_call_target="tpu_custom_call" | custom-call | flops 201326592 | bytes 3145728 | tf_op jit(solution)/shard_map/block_attention/pallas_call | solution.py:256
  373.1 8.3 %collective-permute-done.35.other = bf16[800,256]{1,0:T(8,128)(2,1)S(1)} collective-permute-done((bf16[800,256]{1,0:T(8,128)(2,1)S(1)}, bf16[800,256]{1,0:T(8,128)(2,1)S(1)}, u32[]{:S(2)}, u32[]{:S(2)}) %collective-permute-start.35) | collective-permute-done | bytes 409632 | tf_op jit(solution)/shard_map/ppermute | solution.py:348
  381.5 8.7 %collective-permute-done.45.other = bf16[800,256]{1,0:T(8,128)(2,1)S(1)} collective-permute-done((bf16[800,256]{1,0:T(8,128)(2,1)S(1)}, bf16[800,256]{1,0:T(8,128)(2,1)S(1)}, u32[]{:S(2)}, u32[]{:S(2)}) %collective-permute-start.45) | collective-permute-done | bytes 409632 | tf_op jit(solution)/shard_map/ppermute | solution.py:348
  391.0 2.1 merge_partials.25
  396.4 2.7 collective-permute-done.44.other
  399.1 2.1 merge_partials.18
  401.2 16.9 %collective-permute-done.41.other = bf16[800,256]{1,0:T(8,128)(2,1)S(1)} collective-permute-done((bf16[800,256]{1,0:T(8,128)(2,1)S(1)}, bf16[800,256]{1,0:T(8,128)(2,1)S(1)}, u32[]{:S(2)}, u32[]{:S(2)}) %collective-permute-start.41) | collective-permute-done | bytes 409632 | tf_op jit(solution)/shard_map/ppermute | solution.py:348
  419.8 6.1 collective-permute-done.46.other
  426.0 2.1 merge_partials.24.own
  432.2 2.1 merge_partials.15
  443.1 2.1 merge_partials.19
  445.2 2.2 collective-permute-start.37
  447.4 239.4 %join_rows.1 = bf16[5120,768]{1,0:T(8,128)(2,1)} custom-call(bf16[640,768]{1,0:T(8,128)(2,1)} %refs_0_, bf16[640,768]{1,0:T(8,128)(2,1)} %collective-permute-done.26.refs_1_, bf16[640,768]{1,0:T(8,128)(2,1)} %collective-permute-done.25.refs_2_, bf16[640,768]{1,0:T(8,128)(2,1)} %collective-permute-done.29.refs_3_, ...), custom_call_target="tpu_custom_call" | custom-call | bytes 15728640 | tf_op jit(solution)/shard_map/join_rows/pallas_call | solution.py:323
  688.8 2.4 convolution_convert_fusion
  697.1 2.3 convolution_convert_fusion.1
  702.2 3.2 convolution_convert_fusion.2
  706.0 2.3 fusion.5
  709.8 2.3 convolution_convert_fusion.3
  712.2 2.4 fusion.4
  715.2 10.6 %collective-permute-done.50 = bf16[256,1280]{1,0:T(8,128)(2,1)S(1)} collective-permute-done((bf16[256,1280]{1,0:T(8,128)(2,1)S(1)}, bf16[256,1280]{1,0:T(8,128)(2,1)S(1)}, u32[]{:S(2)}, u32[]{:S(2)}) %collective-permute-start.50) | collective-permute-done | bytes 655392 | tf_op jit(solution)/shard_map/ppermute | solution.py:639
  725.9 2.4 fusion.7
  728.4 10.9 %collective-permute-done.40 = bf16[256,1280]{1,0:T(8,128)(2,1)S(1)} collective-permute-done((bf16[256,1280]{1,0:T(8,128)(2,1)S(1)}, bf16[256,1280]{1,0:T(8,128)(2,1)S(1)}, u32[]{:S(2)}, u32[]{:S(2)}) %collective-permute-start.40) | collective-permute-done | bytes 655392 | tf_op jit(solution)/shard_map/ppermute | solution.py:639
  739.3 2.3 fusion.6
  (264 shorter events, 100.8 us)
Async XLA Ops:
  5.0 33.2 %collective-permute-start.3 = (bf16[512,640]{1,0:T(8,128)(2,1)}, bf16[512,640]{1,0:T(8,128)(2,1)S(1)}, u32[]{:S(2)}, u32[]{:S(2)}) collective-permute-start(bf16[512,640]{1,0:T(8,128)(2,1)} %bitcast.12), channel_id=1, source_target_pairs={{0,16},{4,20},{8,24},{12,28},{16,0},{20,4},{24,8},{28,12},{1,17},{... | collective-permute-start | bytes 1966088 | tf_op jit(solution)/shard_map/ppermute | solution.py:348
  9.0 51.8 %collective-permute-start = (bf16[640,768]{1,0:T(8,128)(2,1)}, bf16[640,768]{1,0:T(8,128)(2,1)}, u32[]{:S(2)}, u32[]{:S(2)}) collective-permute-start(bf16[640,768]{1,0:T(8,128)(2,1)} %param.18), channel_id=1, source_target_pairs={{0,4},{4,0},{8,12},{12,8},{16,20},{20,16},{24,28},{28,24},{1,5},{5... | collective-permute-start | bytes 2949128 | tf_op jit(solution)/shard_map/ppermute | solution.py:348
  10.5 47.4 %collective-permute-start.1 = (bf16[640,768]{1,0:T(8,128)(2,1)}, bf16[640,768]{1,0:T(8,128)(2,1)}, u32[]{:S(2)}, u32[]{:S(2)}) collective-permute-start(bf16[640,768]{1,0:T(8,128)(2,1)} %param.18), channel_id=1, source_target_pairs={{0,8},{4,12},{8,0},{12,4},{16,24},{20,28},{24,16},{28,20},{1,9},{5... | collective-permute-start | bytes 2949128 | tf_op jit(solution)/shard_map/ppermute | solution.py:348
  12.1 41.5 %collective-permute-start.4 = (bf16[640,768]{1,0:T(8,128)(2,1)}, bf16[640,768]{1,0:T(8,128)(2,1)}, u32[]{:S(2)}, u32[]{:S(2)}) collective-permute-start(bf16[640,768]{1,0:T(8,128)(2,1)} %param.19), channel_id=1, source_target_pairs={{0,4},{4,0},{8,12},{12,8},{16,20},{20,16},{24,28},{28,24},{1,5},{5... | collective-permute-start | bytes 2949128 | tf_op jit(solution)/shard_map/ppermute | solution.py:348
  13.8 44.1 %collective-permute-start.8 = (f32[8,64]{1,0:T(8,128)S(1)}, f32[8,64]{1,0:T(8,128)S(1)}, u32[]{:S(2)}, u32[]{:S(2)}) collective-permute-start(f32[8,64]{1,0:T(8,128)S(1)} %rsqrt.16), channel_id=1, source_target_pairs={{0,16},{4,20},{8,24},{12,28},{16,0},{20,4},{24,8},{28,12},{1,17},{... | collective-permute-start | bytes 6152 | tf_op jit(solution)/shard_map/ppermute | solution.py:348
  38.1 33.2 %collective-permute-start.10 = (bf16[640,768]{1,0:T(8,128)(2,1)}, bf16[640,768]{1,0:T(8,128)(2,1)}, u32[]{:S(2)}, u32[]{:S(2)}) collective-permute-start(bf16[640,768]{1,0:T(8,128)(2,1)} %param.19), channel_id=1, source_target_pairs={{0,8},{4,12},{8,0},{12,4},{16,24},{20,28},{24,16},{28,20},{1,9},{5... | collective-permute-start | bytes 2949128 | tf_op jit(solution)/shard_map/ppermute | solution.py:348
  53.6 15.4 %collective-permute-start.6 = (bf16[512,640]{1,0:T(8,128)(2,1)S(1)}, bf16[512,640]{1,0:T(8,128)(2,1)}, u32[]{:S(2)}, u32[]{:S(2)}) collective-permute-start(bf16[512,640]{1,0:T(8,128)(2,1)S(1)} %collective-permute-done.3), channel_id=1, source_target_pairs={{0,2},{1,3},{2,0},{3,1},{4,6},{5,7},{6,4},{7,5},{8,10},{9,11},{10,... | collective-permute-start | bytes 1966088 | tf_op jit(solution)/shard_map/ppermute | solution.py:348
  57.9 12.7 %collective-permute-start.5 = (bf16[512,640]{1,0:T(8,128)(2,1)S(1)}, bf16[512,640]{1,0:T(8,128)(2,1)}, u32[]{:S(2)}, u32[]{:S(2)}) collective-permute-start(bf16[512,640]{1,0:T(8,128)(2,1)S(1)} %collective-permute-done.3), channel_id=1, source_target_pairs={{0,1},{1,0},{2,3},{3,2},{4,5},{5,4},{6,7},{7,6},{8,9},{9,8},{10,11... | collective-permute-start | bytes 1966088 | tf_op jit(solution)/shard_map/ppermute | solution.py:348
  57.9 24.9 %collective-permute-start.2 = (bf16[640,768]{1,0:T(8,128)(2,1)}, bf16[640,768]{1,0:T(8,128)(2,1)}, u32[]{:S(2)}, u32[]{:S(2)}) collective-permute-start(bf16[640,768]{1,0:T(8,128)(2,1)} %collective-permute-done.1), channel_id=1, source_target_pairs={{0,4},{4,0},{8,12},{12,8},{16,20},{20,16},{24,28},{28,24},{1,5},{5... | collective-permute-start | bytes 2949128 | tf_op jit(solution)/shard_map/ppermute | solution.py:348
  60.8 41.6 %collective-permute-start.13 = (bf16[640,768]{1,0:T(8,128)(2,1)}, bf16[640,768]{1,0:T(8,128)(2,1)}, u32[]{:S(2)}, u32[]{:S(2)}) collective-permute-start(bf16[640,768]{1,0:T(8,128)(2,1)} %param.20), channel_id=1, source_target_pairs={{0,8},{4,12},{8,0},{12,4},{16,24},{20,28},{24,16},{28,20},{1,9},{5... | collective-permute-start | bytes 2949128 | tf_op jit(solution)/shard_map/ppermute | solution.py:348
  69.0 16.6 %collective-permute-start.7 = (bf16[512,640]{1,0:T(8,128)(2,1)}, bf16[512,640]{1,0:T(8,128)(2,1)S(1)}, u32[]{:S(2)}, u32[]{:S(2)}) collective-permute-start(bf16[512,640]{1,0:T(8,128)(2,1)} %collective-permute-done.6), channel_id=1, source_target_pairs={{0,1},{1,0},{2,3},{3,2},{4,5},{5,4},{6,7},{7,6},{8,9},{9,8},{10,11... | collective-permute-start | bytes 1966088 | tf_op jit(solution)/shard_map/ppermute | solution.py:348
  70.6 84.8 %collective-permute-start.12 = (bf16[640,768]{1,0:T(8,128)(2,1)}, bf16[640,768]{1,0:T(8,128)(2,1)}, u32[]{:S(2)}, u32[]{:S(2)}) collective-permute-start(bf16[640,768]{1,0:T(8,128)(2,1)} %refs_0_), channel_id=1, source_target_pairs={{0,16},{4,20},{8,24},{12,28},{16,0},{20,4},{24,8},{28,12},{1,17},{... | collective-permute-start | bytes 2949128 | tf_op jit(solution)/shard_map/ppermute | solution.py:348
  71.3 84.0 %collective-permute-start.11 = (bf16[640,768]{1,0:T(8,128)(2,1)}, bf16[640,768]{1,0:T(8,128)(2,1)}, u32[]{:S(2)}, u32[]{:S(2)}) collective-permute-start(bf16[640,768]{1,0:T(8,128)(2,1)} %collective-permute-done.10), channel_id=1, source_target_pairs={{0,4},{4,0},{8,12},{12,8},{16,20},{20,16},{24,28},{28,24},{1,5},{5... | collective-permute-start | bytes 2949128 | tf_op jit(solution)/shard_map/ppermute | solution.py:348
  82.8 72.5 %collective-permute-start.14 = (bf16[640,768]{1,0:T(8,128)(2,1)}, bf16[640,768]{1,0:T(8,128)(2,1)}, u32[]{:S(2)}, u32[]{:S(2)}) collective-permute-start(bf16[640,768]{1,0:T(8,128)(2,1)} %param.20), channel_id=1, source_target_pairs={{0,4},{4,0},{8,12},{12,8},{16,20},{20,16},{24,28},{28,24},{1,5},{5... | collective-permute-start | bytes 2949128 | tf_op jit(solution)/shard_map/ppermute | solution.py:348
  88.0 62.7 %collective-permute-start.9 = (bf16[512,768]{1,0:T(8,128)(2,1)S(1)}, bf16[512,768]{1,0:T(8,128)(2,1)S(1)}, u32[]{:S(2)}, u32[]{:S(2)}) collective-permute-start(bf16[512,768]{1,0:T(8,128)(2,1)S(1)} %convolution_convert_fusion.6), channel_id=1, source_target_pairs={{0,16},{4,20},{8,24},{12,28},{16,0},{20,4},{24,8},{28,12},{1,17},{... | collective-permute-start | bytes 2359304 | tf_op jit(solution)/shard_map/ppermute | solution.py:348
  102.4 58.8 %collective-permute-start.19 = (bf16[640,768]{1,0:T(8,128)(2,1)}, bf16[640,768]{1,0:T(8,128)(2,1)}, u32[]{:S(2)}, u32[]{:S(2)}) collective-permute-start(bf16[640,768]{1,0:T(8,128)(2,1)} %collective-permute-done.13), channel_id=1, source_target_pairs={{0,4},{4,0},{8,12},{12,8},{16,20},{20,16},{24,28},{28,24},{1,5},{5... | collective-permute-start | bytes 2949128 | tf_op jit(solution)/shard_map/ppermute | solution.py:348
  155.4 35.9 %collective-permute-start.18 = (bf16[8,64,768]{2,1,0:T(8,128)(2,1)}, bf16[8,64,768]{2,1,0:T(8,128)(2,1)S(1)}, u32[]{:S(2)}, u32[]{:S(2)}) collective-permute-start(bf16[8,64,768]{2,1,0:T(8,128)(2,1)} %bitcast.56), channel_id=1, source_target_pairs={{0,16},{4,20},{8,24},{12,28},{16,0},{20,4},{24,8},{28,12},{1,17},{... | collective-permute-start | bytes 2359304 | tf_op jit(solution)/shard_map/ppermute | solution.py:348
  191.3 19.5 %collective-permute-start.20 = (bf16[8,64,768]{2,1,0:T(8,128)(2,1)S(1)}, bf16[8,64,768]{2,1,0:T(8,128)(2,1)S(1)}, u32[]{:S(2)}, u32[]{:S(2)}) collective-permute-start(bf16[8,64,768]{2,1,0:T(8,128)(2,1)S(1)} %collective-permute-done.18.refs_4_), channel_id=1, source_target_pairs={{0,4},{4,0},{8,12},{12,8},{16,20},{20,16},{24,28},{28,24},{1,5},{5... | collective-permute-start | bytes 2359304 | tf_op jit(solution)/shard_map/ppermute | solution.py:348
  194.1 23.8 %collective-permute-start.16 = (bf16[8,64,768]{2,1,0:T(8,128)(2,1)S(1)}, bf16[8,64,768]{2,1,0:T(8,128)(2,1)S(1)}, u32[]{:S(2)}, u32[]{:S(2)}) collective-permute-start(bf16[8,64,768]{2,1,0:T(8,128)(2,1)S(1)} %bitcast.57), channel_id=1, source_target_pairs={{0,8},{4,12},{8,0},{12,4},{16,24},{20,28},{24,16},{28,20},{1,9},{5... | collective-permute-start | bytes 2359304 | tf_op jit(solution)/shard_map/ppermute | solution.py:348
  210.8 36.4 %collective-permute-start.23 = (bf16[512,768]{1,0:T(8,128)(2,1)S(1)}, bf16[512,768]{1,0:T(8,128)(2,1)S(1)}, u32[]{:S(2)}, u32[]{:S(2)}) collective-permute-start(bf16[512,768]{1,0:T(8,128)(2,1)S(1)} %convolution_convert_fusion.5), channel_id=1, source_target_pairs={{0,16},{4,20},{8,24},{12,28},{16,0},{20,4},{24,8},{28,12},{1,17},{... | collective-permute-start | bytes 2359304 | tf_op jit(solution)/shard_map/ppermute | solution.py:348
  213.3 33.9 %collective-permute-start.15 = (bf16[8,64,768]{2,1,0:T(8,128)(2,1)S(1)}, bf16[8,64,768]{2,1,0:T(8,128)(2,1)S(1)}, u32[]{:S(2)}, u32[]{:S(2)}) collective-permute-start(bf16[8,64,768]{2,1,0:T(8,128)(2,1)S(1)} %bitcast.58), channel_id=1, source_target_pairs={{0,4},{4,0},{8,12},{12,8},{16,20},{20,16},{24,28},{28,24},{1,5},{5... | collective-permute-start | bytes 2359304 | tf_op jit(solution)/shard_map/ppermute | solution.py:348
  214.9 52.1 %collective-permute-start.21 = (bf16[8,64,768]{2,1,0:T(8,128)(2,1)S(1)}, bf16[8,64,768]{2,1,0:T(8,128)(2,1)S(1)}, u32[]{:S(2)}, u32[]{:S(2)}) collective-permute-start(bf16[8,64,768]{2,1,0:T(8,128)(2,1)S(1)} %collective-permute-done.18.refs_4_), channel_id=1, source_target_pairs={{0,8},{4,12},{8,0},{12,4},{16,24},{20,28},{24,16},{28,20},{1,9},{5... | collective-permute-start | bytes 2359304 | tf_op jit(solution)/shard_map/ppermute | solution.py:348
  217.9 50.0 %collective-permute-start.17 = (bf16[8,64,768]{2,1,0:T(8,128)(2,1)S(1)}, bf16[8,64,768]{2,1,0:T(8,128)(2,1)S(1)}, u32[]{:S(2)}, u32[]{:S(2)}) collective-permute-start(bf16[8,64,768]{2,1,0:T(8,128)(2,1)S(1)} %collective-permute-done.16.refs_2_), channel_id=1, source_target_pairs={{0,4},{4,0},{8,12},{12,8},{16,20},{20,16},{24,28},{28,24},{1,5},{5... | collective-permute-start | bytes 2359304 | tf_op jit(solution)/shard_map/ppermute | solution.py:348
  218.4 65.6 %collective-permute-start.22 = (bf16[8,64,768]{2,1,0:T(8,128)(2,1)S(1)}, bf16[8,64,768]{2,1,0:T(8,128)(2,1)S(1)}, u32[]{:S(2)}, u32[]{:S(2)}) collective-permute-start(bf16[8,64,768]{2,1,0:T(8,128)(2,1)S(1)} %collective-permute-done.20.refs_5_), channel_id=1, source_target_pairs={{0,8},{4,12},{8,0},{12,4},{16,24},{20,28},{24,16},{28,20},{1,9},{5... | collective-permute-start | bytes 2359304 | tf_op jit(solution)/shard_map/ppermute | solution.py:348
  247.2 93.0 %collective-permute-start.24 = (bf16[512,768]{1,0:T(8,128)(2,1)}, bf16[512,768]{1,0:T(8,128)(2,1)}, u32[]{:S(2)}, u32[]{:S(2)}) collective-permute-start(bf16[512,768]{1,0:T(8,128)(2,1)} %convolution_convert_fusion.4), channel_id=1, source_target_pairs={{0,16},{4,20},{8,24},{12,28},{16,0},{20,4},{24,8},{28,12},{1,17},{... | collective-permute-start | bytes 2359304 | tf_op jit(solution)/shard_map/ppermute | solution.py:348
  284.9 59.4 %collective-permute-start.27 = (bf16[640,768]{1,0:T(8,128)(2,1)}, bf16[640,768]{1,0:T(8,128)(2,1)}, u32[]{:S(2)}, u32[]{:S(2)}) collective-permute-start(bf16[640,768]{1,0:T(8,128)(2,1)} %collective-permute-done.12.refs_4_), channel_id=1, source_target_pairs={{0,8},{4,12},{8,0},{12,4},{16,24},{20,28},{24,16},{28,20},{1,9},{5... | collective-permute-start | bytes 2949128 | tf_op jit(solution)/shard_map/ppermute | solution.py:348
  284.9 59.4 %collective-permute-start.28 = (bf16[640,768]{1,0:T(8,128)(2,1)}, bf16[640,768]{1,0:T(8,128)(2,1)}, u32[]{:S(2)}, u32[]{:S(2)}) collective-permute-start(bf16[640,768]{1,0:T(8,128)(2,1)} %collective-permute-done.12.refs_4_), channel_id=1, source_target_pairs={{0,4},{4,0},{8,12},{12,8},{16,20},{20,16},{24,28},{28,24},{1,5},{5... | collective-permute-start | bytes 2949128 | tf_op jit(solution)/shard_map/ppermute | solution.py:348
  285.0 59.4 %collective-permute-start.25 = (bf16[640,768]{1,0:T(8,128)(2,1)}, bf16[640,768]{1,0:T(8,128)(2,1)}, u32[]{:S(2)}, u32[]{:S(2)}) collective-permute-start(bf16[640,768]{1,0:T(8,128)(2,1)} %refs_0_), channel_id=1, source_target_pairs={{0,8},{4,12},{8,0},{12,4},{16,24},{20,28},{24,16},{28,20},{1,9},{5... | collective-permute-start | bytes 2949128 | tf_op jit(solution)/shard_map/ppermute | solution.py:348
  287.0 57.4 %collective-permute-start.26 = (bf16[640,768]{1,0:T(8,128)(2,1)}, bf16[640,768]{1,0:T(8,128)(2,1)}, u32[]{:S(2)}, u32[]{:S(2)}) collective-permute-start(bf16[640,768]{1,0:T(8,128)(2,1)} %refs_0_), channel_id=1, source_target_pairs={{0,4},{4,0},{8,12},{12,8},{16,20},{20,16},{24,28},{28,24},{1,5},{5... | collective-permute-start | bytes 2949128 | tf_op jit(solution)/shard_map/ppermute | solution.py:348
  369.0 12.4 %collective-permute-start.32 = (bf16[800,256]{1,0:T(8,128)(2,1)S(1)}, bf16[800,256]{1,0:T(8,128)(2,1)S(1)}, u32[]{:S(2)}, u32[]{:S(2)}) collective-permute-start(bf16[800,256]{1,0:T(8,128)(2,1)S(1)} %get-tuple-element.66), channel_id=1, source_target_pairs={{0,4},{4,0},{8,12},{12,8},{16,20},{20,16},{24,28},{28,24},{1,5},{5... | collective-permute-start | bytes 1228808 | tf_op jit(solution)/shard_map/ppermute | solution.py:348
  369.0 21.2 %collective-permute-start.45 = (bf16[800,256]{1,0:T(8,128)(2,1)S(1)}, bf16[800,256]{1,0:T(8,128)(2,1)S(1)}, u32[]{:S(2)}, u32[]{:S(2)}) collective-permute-start(bf16[800,256]{1,0:T(8,128)(2,1)S(1)} %get-tuple-element.79), channel_id=1, source_target_pairs={{0,8},{4,12},{8,0},{12,4},{16,24},{20,28},{24,16},{28,20},{1,9},{5... | collective-permute-start | bytes 1228808 | tf_op jit(solution)/shard_map/ppermute | solution.py:348
  371.1 22.0 %collective-permute-start.42 = (bf16[800,256]{1,0:T(8,128)(2,1)S(1)}, bf16[800,256]{1,0:T(8,128)(2,1)}, u32[]{:S(2)}, u32[]{:S(2)}) collective-permute-start(bf16[800,256]{1,0:T(8,128)(2,1)S(1)} %get-tuple-element.75), channel_id=1, source_target_pairs={{0,4},{4,0},{8,12},{12,8},{16,20},{20,16},{24,28},{28,24},{1,5},{5... | collective-permute-start | bytes 1228808 | tf_op jit(solution)/shard_map/ppermute | solution.py:348
  373.1 26.0 %collective-permute-start.44 = (bf16[800,256]{1,0:T(8,128)(2,1)S(1)}, bf16[800,256]{1,0:T(8,128)(2,1)}, u32[]{:S(2)}, u32[]{:S(2)}) collective-permute-start(bf16[800,256]{1,0:T(8,128)(2,1)S(1)} %get-tuple-element.77), channel_id=1, source_target_pairs={{0,8},{4,12},{8,0},{12,4},{16,24},{20,28},{24,16},{28,20},{1,9},{5... | collective-permute-start | bytes 1228808 | tf_op jit(solution)/shard_map/ppermute | solution.py:348
  381.4 49.3 %collective-permute-start.30 = (bf16[640,768]{1,0:T(8,128)(2,1)}, bf16[640,768]{1,0:T(8,128)(2,1)S(1)}, u32[]{:S(2)}, u32[]{:S(2)}) collective-permute-start(bf16[640,768]{1,0:T(8,128)(2,1)} %collective-permute-done.28.refs_5_), channel_id=1, source_target_pairs={{0,8},{4,12},{8,0},{12,4},{16,24},{20,28},{24,16},{28,20},{1,9},{5... | collective-permute-start | bytes 2949128 | tf_op jit(solution)/shard_map/ppermute | solution.py:348
  381.5 52.8 %collective-permute-start.29 = (bf16[640,768]{1,0:T(8,128)(2,1)}, bf16[640,768]{1,0:T(8,128)(2,1)}, u32[]{:S(2)}, u32[]{:S(2)}) collective-permute-start(bf16[640,768]{1,0:T(8,128)(2,1)} %collective-permute-done.25.refs_2_), channel_id=1, source_target_pairs={{0,4},{4,0},{8,12},{12,8},{16,20},{20,16},{24,28},{28,24},{1,5},{5... | collective-permute-start | bytes 2949128 | tf_op jit(solution)/shard_map/ppermute | solution.py:348
  390.2 27.9 %collective-permute-start.41 = (bf16[800,256]{1,0:T(8,128)(2,1)S(1)}, bf16[800,256]{1,0:T(8,128)(2,1)S(1)}, u32[]{:S(2)}, u32[]{:S(2)}) collective-permute-start(bf16[800,256]{1,0:T(8,128)(2,1)S(1)} %get-tuple-element.73), channel_id=1, source_target_pairs={{0,4},{4,0},{8,12},{12,8},{16,20},{20,16},{24,28},{28,24},{1,5},{5... | collective-permute-start | bytes 1228808 | tf_op jit(solution)/shard_map/ppermute | solution.py:348
  393.1 32.9 %collective-permute-start.46 = (bf16[800,256]{1,0:T(8,128)(2,1)}, bf16[800,256]{1,0:T(8,128)(2,1)}, u32[]{:S(2)}, u32[]{:S(2)}) collective-permute-start(bf16[800,256]{1,0:T(8,128)(2,1)} %merge_partials.25), channel_id=1, source_target_pairs={{0,4},{4,0},{8,12},{12,8},{16,20},{20,16},{24,28},{28,24},{1,5},{5... | collective-permute-start | bytes 1228808 | tf_op jit(solution)/shard_map/ppermute | solution.py:348
  399.1 31.6 %collective-permute-start.43 = (bf16[800,256]{1,0:T(8,128)(2,1)}, bf16[800,256]{1,0:T(8,128)(2,1)S(1)}, u32[]{:S(2)}, u32[]{:S(2)}) collective-permute-start(bf16[800,256]{1,0:T(8,128)(2,1)} %merge_partials.22), channel_id=1, source_target_pairs={{0,8},{4,12},{8,0},{12,4},{16,24},{20,28},{24,16},{28,20},{1,9},{5... | collective-permute-start | bytes 1228808 | tf_op jit(solution)/shard_map/ppermute | solution.py:348
  418.1 23.0 %collective-permute-start.34 = (bf16[800,256]{1,0:T(8,128)(2,1)S(1)}, bf16[800,256]{1,0:T(8,128)(2,1)}, u32[]{:S(2)}, u32[]{:S(2)}) collective-permute-start(bf16[800,256]{1,0:T(8,128)(2,1)S(1)} %get-tuple-element.69), channel_id=1, source_target_pairs={{0,8},{4,12},{8,0},{12,4},{16,24},{20,28},{24,16},{28,20},{1,9},{5... | collective-permute-start | bytes 1228808 | tf_op jit(solution)/shard_map/ppermute | solution.py:348
  426.0 17.2 %collective-permute-start.36 = (bf16[800,256]{1,0:T(8,128)(2,1)}, bf16[800,256]{1,0:T(8,128)(2,1)}, u32[]{:S(2)}, u32[]{:S(2)}) collective-permute-start(bf16[800,256]{1,0:T(8,128)(2,1)} %merge_partials.18), channel_id=1, source_target_pairs={{0,4},{4,0},{8,12},{12,8},{16,20},{20,16},{24,28},{28,24},{1,5},{5... | collective-permute-start | bytes 1228808 | tf_op jit(solution)/shard_map/ppermute | solution.py:348
  430.7 256.1 %collective-permute-start.47 = (bf16[800,256]{1,0:T(8,128)(2,1)}, bf16[800,256]{1,0:T(8,128)(2,1)}, u32[]{:S(2)}, u32[]{:S(2)}) collective-permute-start(bf16[800,256]{1,0:T(8,128)(2,1)} %merge_partials.26), channel_id=1, source_target_pairs={{0,16},{4,20},{8,24},{12,28},{16,0},{20,4},{24,8},{28,12},{1,17},{... | collective-permute-start | bytes 1228808 | tf_op jit(solution)/shard_map/ppermute | solution.py:348
  430.7 260.8 %collective-permute-start.31 = (bf16[800,256]{1,0:T(8,128)(2,1)S(1)}, bf16[800,256]{1,0:T(8,128)(2,1)S(1)}, u32[]{:S(2)}, u32[]{:S(2)}) collective-permute-start(bf16[800,256]{1,0:T(8,128)(2,1)S(1)} %get-tuple-element.64), channel_id=1, source_target_pairs={{0,4},{4,0},{8,12},{12,8},{16,20},{20,16},{24,28},{28,24},{1,5},{5... | collective-permute-start | bytes 1228808 | tf_op jit(solution)/shard_map/ppermute | solution.py:348
  434.3 260.1 %collective-permute-start.33 = (bf16[800,256]{1,0:T(8,128)(2,1)}, bf16[800,256]{1,0:T(8,128)(2,1)S(1)}, u32[]{:S(2)}, u32[]{:S(2)}) collective-permute-start(bf16[800,256]{1,0:T(8,128)(2,1)} %merge_partials.15), channel_id=1, source_target_pairs={{0,8},{4,12},{8,0},{12,4},{16,24},{20,28},{24,16},{28,20},{1,9},{5... | collective-permute-start | bytes 1228808 | tf_op jit(solution)/shard_map/ppermute | solution.py:348
  445.2 254.2 %collective-permute-start.37 = (bf16[800,256]{1,0:T(8,128)(2,1)}, bf16[800,256]{1,0:T(8,128)(2,1)S(1)}, u32[]{:S(2)}, u32[]{:S(2)}) collective-permute-start(bf16[800,256]{1,0:T(8,128)(2,1)} %merge_partials.19), channel_id=1, source_target_pairs={{0,16},{4,20},{8,24},{12,28},{16,0},{20,4},{24,8},{28,12},{1,17},{... | collective-permute-start | bytes 1228808 | tf_op jit(solution)/shard_map/ppermute | solution.py:348
  691.3 14.7 %collective-permute-start.49 = (bf16[256,1280]{1,0:T(8,128)(2,1)S(1)}, bf16[256,1280]{1,0:T(8,128)(2,1)S(1)}, u32[]{:S(2)}, u32[]{:S(2)}) collective-permute-start(bf16[256,1280]{1,0:T(8,128)(2,1)S(1)} %convolution_convert_fusion), channel_id=1, source_target_pairs={{0,1},{1,0},{2,3},{3,2},{4,5},{5,4},{6,7},{7,6},{8,9},{9,8},{10,11... | collective-permute-start | bytes 1966088 | tf_op jit(solution)/shard_map/ppermute | solution.py:639
  708.3 17.6 %collective-permute-start.50 = (bf16[256,1280]{1,0:T(8,128)(2,1)S(1)}, bf16[256,1280]{1,0:T(8,128)(2,1)S(1)}, u32[]{:S(2)}, u32[]{:S(2)}) collective-permute-start(bf16[256,1280]{1,0:T(8,128)(2,1)S(1)} %fusion.5), channel_id=1, source_target_pairs={{0,2},{1,3},{2,0},{3,1},{4,6},{5,7},{6,4},{7,5},{8,10},{9,11},{10,... | collective-permute-start | bytes 1966088 | tf_op jit(solution)/shard_map/ppermute | solution.py:639
  712.1 16.3 %collective-permute-start.38 = (bf16[256,1280]{1,0:T(8,128)(2,1)S(1)}, bf16[256,1280]{1,0:T(8,128)(2,1)S(1)}, u32[]{:S(2)}, u32[]{:S(2)}) collective-permute-start(bf16[256,1280]{1,0:T(8,128)(2,1)S(1)} %convolution_convert_fusion.3), channel_id=1, source_target_pairs={{0,1},{1,0},{2,3},{3,2},{4,5},{5,4},{6,7},{7,6},{8,9},{9,8},{10,11... | collective-permute-start | bytes 1966088 | tf_op jit(solution)/shard_map/ppermute | solution.py:639
  714.6 24.7 %collective-permute-start.40 = (bf16[256,1280]{1,0:T(8,128)(2,1)S(1)}, bf16[256,1280]{1,0:T(8,128)(2,1)S(1)}, u32[]{:S(2)}, u32[]{:S(2)}) collective-permute-start(bf16[256,1280]{1,0:T(8,128)(2,1)S(1)} %fusion.4), channel_id=1, source_target_pairs={{0,2},{1,3},{2,0},{3,1},{4,6},{5,7},{6,4},{7,5},{8,10},{9,11},{10,... | collective-permute-start | bytes 1966088 | tf_op jit(solution)/shard_map/ppermute | solution.py:639
  (62 other events, 966.0 us)

commit v2 on v1

--- a/solution.py
+++ b/solution.py
@@ -305,32 +305,49 @@
     )(own, other)
 
 
-def join_kernel(count, *refs):
-    whole, sem = refs[count], refs[count + 1]
-    rows = refs[0].shape[0]
-    copies = [
-        pltpu.make_async_copy(refs[place], whole.at[pl.ds(place * rows, rows)], sem.at[place])
-        for place in range(count)
-    ]
-    for copy in copies:
-        copy.start()
-    for copy in copies:
-        copy.wait()
-
-
-def join_rows(shards):
-    count, (rows, width) = len(shards), shards[0].shape
+def project_kernel(heads, line, places, context, *refs):
+    shards, (even, odd) = refs[: heads * line], refs[heads * line :]
+    width = shards[0].shape[1]
+    turned = context[:width, :].T
+    for number in range(heads):
+        target = places[number]
+        for step in range(line):
+            product = lax.dot_general(
+                turned,
+                shards[number * line + step][...],
+                (((1,), (1,)), ((), ())),
+                preferred_element_type=jnp.float32,
+            )
+            block = places[heads + step]
+
+            @pl.when(target % 2 == 0)
+            def _():
+                even[target // 2, block] = product
+
+            @pl.when(target % 2 == 1)
+            def _():
+                odd[target // 2, block] = product.astype(jnp.bfloat16)
+
+
+def project_out(places, context, shards, heads, line):
+    depth, width = shards[0].shape
+    shape = (heads // 2, line, context.shape[1], depth)
     return pl.pallas_call(
-        functools.partial(join_kernel, count),
-        out_shape=jax.ShapeDtypeStruct((count * rows, width), shards[0].dtype),
-        in_specs=[IN_HBM] * count,
-        out_specs=IN_HBM,
-        scratch_shapes=[pltpu.SemaphoreType.DMA((count,))],
+        functools.partial(project_kernel, heads, line),
+        out_shape=[
+            jax.ShapeDtypeStruct(shape, jnp.float32),
+            jax.ShapeDtypeStruct(shape, jnp.bfloat16),
+        ],
+        in_specs=[IN_SMEM] + [IN_VMEM] * (1 + heads * line),
+        out_specs=[IN_VMEM] * 2,
+        compiler_params=pltpu.CompilerParams(vmem_limit_bytes=VMEM_BYTES),
         cost_estimate=pl.CostEstimate(
-            flops=0, bytes_accessed=4 * count * rows * width, transcendentals=0
+            flops=2 * context.shape[1] * heads * line * depth * width,
+            bytes_accessed=2 * heads * line * depth * width,
+            transcendentals=0,
         ),
-        name="join_rows",
-    )(*shards)
+        name="project_out",
+    )(places, context, *shards)
 
 
 class Axis:
@@ -530,15 +547,18 @@
     chunk = requests // CHUNKS
 
     sent_query = product(other_rows, query_weight).astype(jnp.bfloat16)
-    received_query = half_axis.step(sent_query)
+    received_query = after(
+        half_axis.step(sent_query),
+        (key_shards, far_out, value_shards[(0, 1, 0)], value_shards[(0, 0, 1)]),
+    )
     near = rotated_sum(
         product(own_rows, query_weight), received_query, cosine, sine
     ).reshape(piece)
-    near = after(
-        near, (key_shards, far_out, value_shards[(0, 1, 0)], value_shards[(0, 0, 1)])
-    )
-    far = after(half_axis.step(near), value_shards)
-    trees = [gather_tree(near, (z_axis, x_axis)), gather_tree(far, (x_axis, z_axis))]
+    near_tree = gather_tree(near, (z_axis, x_axis))
+    far = after(
+        half_axis.step(near), (value_shards, near_tree[(0, 1, 0)], near_tree[(0, 0, 1)])
+    )
+    trees = [near_tree, gather_tree(far, (x_axis, z_axis))]
     every_query = [trees[key[0]][with_entry(key, 0, 0)] for key in full_order]
 
     sent_key = product(other_rows, key_weight).astype(jnp.bfloat16)
@@ -586,20 +606,37 @@
     counts = jnp.sum(jnp.where(at_item, page_count[None, :], 0), axis=1)
     plan = (order, counts, starts, lives, fulls)
 
-    own_out = gather_tree(after(w_out, every_query), (z_axis, x_axis))
-    far_out = gather_tree(after(far_out, every_query), (x_axis, z_axis))
+    def gather_gated(value, first, second):
+        found = {}
+        for steps, line in enumerate(first.gather(value)):
+            line = after(line, state) if steps else line
+            for more, item in enumerate(second.gather(line)):
+                key = with_entry((0, 0, 0), first.rank, steps)
+                found[with_entry(key, second.rank, more)] = item
+        return found
+
+    ready = (every_query, received_key)
+    state = cached_attention(
+        after(every_query, received_key), key_cache, value_cache, plan
+    )
+    own_out = gather_gated(after(w_out, ready), z_axis, x_axis)
+    far_out = gather_gated(after(far_out, ready), x_axis, z_axis)
     out_shards = [(own_out, far_out)[key[0]][with_entry(key, 0, 0)] for key in full_order]
-    out_weight = join_rows(out_shards)
     out_width = model_width // head_size
-    state = cached_attention(every_query, key_cache, value_cache, plan)
+    lines = [
+        half_axis.before(half) * z_size + z_axis.before(z)
+        for half in range(2)
+        for z in range(z_size)
+    ]
+    places = jnp.stack(
+        [line ^ head_place for line in lines] + [x_axis.before(x) for x in range(x_size)]
+    ).astype(jnp.int32)
     first_steps = [tree[key] for tree in (own_out, far_out) for key in ((0, 1, 0), (0, 0, 1))]
     pieces_of = block_attention(seq_size, state, new_keys, after(new_values, first_steps))
+    pieces_of = after(pieces_of, out_shards)
     results = []
     for number in range(CHUNKS):
         pieces = pieces_of[number]
-        if number == 0:
-            for mine in (0, half_size):
-                pieces[mine] = after(pieces[mine], out_shards)
 
         def parts_for(half_steps):
             return {
@@ -612,42 +649,23 @@
 
         far_sum = reduce_tree(parts_for(1), (z_axis, x_axis), merge)
         near_sum = reduce_tree(parts_for(0), (x_axis, z_axis), merge)
-        context = half_axis.reduce([near_sum, far_sum], merge)[:local_width]
-
-        def features_of(target):
-            line = target ^ head_place
-            half_steps = (half_axis.coord - line // z_size + 2) % 2
-            z_steps = (z_axis.coord - line % z_size + z_size) % z_size
-            return lax.dynamic_slice_in_dim(
-                out_weight, (half_steps * z_size + z_steps) * out_width, out_width, axis=0
-            )
-
-        outputs = {
-            target: lax.dot_general(
-                context,
-                features_of(target),
-                (((0,), (1,)), ((), ())),
-                preferred_element_type=jnp.float32,
-            )
-            for target in range(head_size)
-        }
+        context = half_axis.reduce([near_sum, far_sum], merge)
+        even, odd = project_out(places, context, out_shards, head_size, x_size)
+
+        outputs = {2 * place: even[place] for place in range(head_size // 2)}
+        sending = {2 * place + 1: odd[place] for place in range(head_size // 2)}
         bit = 1
         while bit < head_size:
             pairs = [(index, index ^ bit) for index in range(head_size)]
-            for target in [place for place in outputs if place & bit]:
-                sent = outputs.pop(target).astype(jnp.bfloat16)
-                outputs[target ^ bit] += lax.ppermute(sent, "head", pairs).astype(jnp.float32)
+            for target, value in sending.items():
+                outputs[target ^ bit] += lax.ppermute(value, "head", pairs).astype(jnp.float32)
             bit *= 2
+            sending = {
+                target: outputs.pop(target).astype(jnp.bfloat16)
+                for target in [place for place in outputs if place & bit]
+            }
         summed = outputs[0].astype(jnp.bfloat16)
-        in_order = jnp.concatenate(
-            [
-                lax.dynamic_slice_in_dim(
-                    summed, (x_axis.coord - x + x_size) % x_size * depth, depth, axis=1
-                )
-                for x in range(x_size)
-            ],
-            axis=1,
-        )
+        in_order = jnp.concatenate([summed[x] for x in range(x_size)], axis=1)
         results.append(in_order.reshape(chunk, 2, part_len, out_width))
     result = jnp.concatenate(results, axis=0)
     return (result[:, 0], result[:, 1])

time: 744 us -> 475 us (0.64)
  Pallas kernels: 333 us -> 108 us
  waiting for transfers between devices: 273 us -> 204 us
  starting transfers between devices: 44.3 us -> 81.3 us
  matrix products: 38.1 us -> 22.9 us
    pallas_call x1 -> x2, Pallas kernels: 239 us -> 15.1 us  [project_out(): pl.pallas_call(functools.partial(project_kernel, heads, line), out_shape=...]
    ppermute x45, waiting for transfers between devices: 251 us -> 175 us  [step(): return lax.ppermute(value, self.mesh_axis, pairs)]
    ppermute x45, starting transfers between devices: 41.4 us -> 78.3 us  [step(): return lax.ppermute(value, self.mesh_axis, pairs)]
    dot_general x8 -> x0, matrix products: 19.6 us -> none  [per_device(): lax.dot_general(context, features_of(target), (((0,), (1,)), ((), ())), p...]
    unnamed x127 -> x85, local copies, waits for them, and re-layouts: 31.7 us -> 28.6 us
  transfers between devices with their start and end apart: 51 -> 51, of which waited for: 20 -> 19; matrix products, arithmetic and copies ran while one was open for 9% -> 12% of each run, Pallas kernels for 42% -> 23%
where the time goes in v2:
time: 475 us; the launch traced here: 471 us
  waiting for transfers between devices  204 us (43%)
  Pallas kernels  108 us (23%)
  starting transfers between devices  81.3 us (17%)
  local copies, waits for them, and re-layouts  41.6 us (9%)
  matrix products  22.9 us (5%)
  other arithmetic  12.2 us (3%)
    ppermute x45, waiting for transfers between devices, step(): return lax.ppermute(value, self.mesh_axis, pairs)  175 us
    ppermute x45, starting transfers between devices, step(): return lax.ppermute(value, self.mesh_axis, pairs)  78.3 us
    pallas_call x1, Pallas kernels, cached_attention(): pl.pallas_call(functools.partial(cached_kernel, sources), out_shape=[jax....  38.7 us
    pallas_call x14, Pallas kernels, merge(): pl.pallas_call(merge_kernel, out_shape=jax.ShapeDtypeStruct(own.shape, ow...  28.8 us
    unnamed x85, local copies, waits for them, and re-layouts  28.6 us
    ppermute x6, waiting for transfers between devices, per_device(): lax.ppermute(value, 'head', pairs).astype(jnp.float32)  28.4 us
    dot_general x6, matrix products, product(): return jnp.dot(left, weight, preferred_element_type=jnp.float32)  22.9 us
    pallas_call x1, Pallas kernels, block_attention(): pl.pallas_call(functools.partial(block_kernel, sources), out_shape=[piece...  19.3 us
  transfers between devices with their start and end apart: 51, of which 19 were waited for; matrix products, arithmetic and copies ran while one was open for 12% of the time, Pallas kernels for 23%

profile of v2, /device:TPU:0, one launch (start us, length us, event | category | flops | bytes accessed | tf_op | source)
XLA Modules:
  0.0 471.4 jit_solution(1405409215549446707)
XLA Ops:
  0.6 3.0 collective-permute-start
  4.3 2.5 dynamic-slice_bitcast_fusion.4
  7.8 2.6 collective-permute-start.3
  15.3 2.2 fusion.1
  17.9 21.6 %collective-permute-done.3 = bf16[512,640]{1,0:T(8,128)(2,1)} collective-permute-done((bf16[512,640]{1,0:T(8,128)(2,1)}, bf16[512,640]{1,0:T(8,128)(2,1)}, u32[]{:S(2)}, u32[]{:S(2)}) %collective-permute-start.3) | collective-permute-done | bytes 655392 | tf_op jit(solution)/shard_map/ppermute | solution.py:365
  40.1 6.7 %collective-permute-done.4 = bf16[640,768]{1,0:T(8,128)(2,1)} collective-permute-done((bf16[640,768]{1,0:T(8,128)(2,1)}, bf16[640,768]{1,0:T(8,128)(2,1)}, u32[]{:S(2)}, u32[]{:S(2)}) %collective-permute-start.4) | collective-permute-done | bytes 983072 | tf_op jit(solution)/shard_map/ppermute | solution.py:365
  53.6 2.2 constant_dynamic-update-slice_fusion.2
  55.8 7.2 %collective-permute-done.6 = bf16[512,640]{1,0:T(8,128)(2,1)} collective-permute-done((bf16[512,640]{1,0:T(8,128)(2,1)}, bf16[512,640]{1,0:T(8,128)(2,1)}, u32[]{:S(2)}, u32[]{:S(2)}) %collective-permute-start.6) | collective-permute-done | bytes 655392 | tf_op jit(solution)/shard_map/ppermute | solution.py:365
  64.4 2.2 constant_dynamic-update-slice_fusion.1
  66.6 14.9 %collective-permute-done.10 = bf16[640,768]{1,0:T(8,128)(2,1)} collective-permute-done((bf16[640,768]{1,0:T(8,128)(2,1)S(1)}, bf16[640,768]{1,0:T(8,128)(2,1)}, u32[]{:S(2)}, u32[]{:S(2)}) %collective-permute-start.10) | collective-permute-done | bytes 983072 | tf_op jit(solution)/shard_map/ppermute | solution.py:365
  84.0 2.1 collective-permute-start.14
  86.1 2.2 constant_dynamic-update-slice_fusion
  88.5 5.4 %convolution_convert_fusion.2 = bf16[512,768]{1,0:T(8,128)(2,1)S(1)} fusion(bf16[2560,768]{1,0:T(8,128)(2,1)} %constant_dynamic-update-slice_fusion, bf16[512,2560]{1,0:T(8,128)(2,1)S(1)} %constant_dynamic-update-slice_fusion.15, f32[512]{0:T(512)S(1)} %mul.213, f32[2560]{0:T(1024)S(1)} %pad_maximum_fusion.2), kind=kOutput, calls=%fused_computation.10 | convolution fusion | flops 2018902016 | bytes 7352320 | tf_op jit(solution)/shard_map/dot_general | solution.py:530
  93.8 2.9 collective-permute-start.9
  96.9 7.1 %collective-permute-done.13 = bf16[640,768]{1,0:T(8,128)(2,1)} collective-permute-done((bf16[640,768]{1,0:T(8,128)(2,1)}, bf16[640,768]{1,0:T(8,128)(2,1)}, u32[]{:S(2)}, u32[]{:S(2)}) %collective-permute-start.13) | collective-permute-done | bytes 983072 | tf_op jit(solution)/shard_map/ppermute | solution.py:365
  104.1 4.5 collective-permute-start.19
  108.5 3.4 fusion.21.own
  111.9 31.0 %collective-permute-done.12.refs_4_ = bf16[640,768]{1,0:T(8,128)(2,1)S(1)} collective-permute-done((bf16[640,768]{1,0:T(8,128)(2,1)S(1)}, bf16[640,768]{1,0:T(8,128)(2,1)S(1)}, u32[]{:S(2)}, u32[]{:S(2)}) %collective-permute-start.12) | collective-permute-done | bytes 983072 | tf_op jit(solution)/shard_map/ppermute | solution.py:365
  142.9 18.8 %collective-permute-done.9.received = bf16[512,768]{1,0:T(8,128)(2,1)} collective-permute-done((bf16[512,768]{1,0:T(8,128)(2,1)S(1)}, bf16[512,768]{1,0:T(8,128)(2,1)}, u32[]{:S(2)}, u32[]{:S(2)}) %collective-permute-start.9) | collective-permute-done | bytes 786464 | tf_op jit(solution)/shard_map/ppermute | solution.py:365
  163.2 3.1 rotate_rows.2
  166.4 6.7 %collective-permute-start.16 = (bf16[8,64,768]{2,1,0:T(8,128)(2,1)}, bf16[8,64,768]{2,1,0:T(8,128)(2,1)S(1)}, u32[]{:S(2)}, u32[]{:S(2)}) collective-permute-start(bf16[8,64,768]{2,1,0:T(8,128)(2,1)} %bitcast.93), channel_id=1, source_target_pairs={{0,8},{4,12},{8,0},{12,4},{16,24},{20,28},{24,16},{28,20},{1,9},{5... | collective-permute-start | bytes 2359304 | tf_op jit(solution)/shard_map/ppermute | solution.py:365
  173.1 7.4 %collective-permute-start.15 = (bf16[8,64,768]{2,1,0:T(8,128)(2,1)}, bf16[8,64,768]{2,1,0:T(8,128)(2,1)S(1)}, u32[]{:S(2)}, u32[]{:S(2)}) collective-permute-start(bf16[8,64,768]{2,1,0:T(8,128)(2,1)} %bitcast.94), channel_id=1, source_target_pairs={{0,4},{4,0},{8,12},{12,8},{16,20},{20,16},{24,28},{28,24},{1,5},{5... | collective-permute-start | bytes 2359304 | tf_op jit(solution)/shard_map/ppermute | solution.py:365
  182.2 5.8 %collective-permute-done.18.refs_4_ = bf16[8,64,768]{2,1,0:T(8,128)(2,1)S(1)} collective-permute-done((bf16[8,64,768]{2,1,0:T(8,128)(2,1)}, bf16[8,64,768]{2,1,0:T(8,128)(2,1)S(1)}, u32[]{:S(2)}, u32[]{:S(2)}) %collective-permute-start.18) | collective-permute-done | bytes 786464 | tf_op jit(solution)/shard_map/ppermute | solution.py:365
  188.7 10.5 %collective-permute-done.15.refs_1_ = bf16[8,64,768]{2,1,0:T(8,128)(2,1)S(1)} collective-permute-done((bf16[8,64,768]{2,1,0:T(8,128)(2,1)}, bf16[8,64,768]{2,1,0:T(8,128)(2,1)S(1)}, u32[]{:S(2)}, u32[]{:S(2)}) %collective-permute-start.15) | collective-permute-done | bytes 786464 | tf_op jit(solution)/shard_map/ppermute | solution.py:365
  199.2 6.2 %collective-permute-start.20 = (bf16[8,64,768]{2,1,0:T(8,128)(2,1)S(1)}, bf16[8,64,768]{2,1,0:T(8,128)(2,1)S(1)}, u32[]{:S(2)}, u32[]{:S(2)}) collective-permute-start(bf16[8,64,768]{2,1,0:T(8,128)(2,1)S(1)} %collective-permute-done.18.refs_4_), channel_id=1, source_target_pairs={{0,4},{4,0},{8,12},{12,8},{16,20},{20,16},{24,28},{28,24},{1,5},{5... | collective-permute-start | bytes 2359304 | tf_op jit(solution)/shard_map/ppermute | solution.py:365
  208.0 2.3 convolution_convert_fusion.1
  210.4 5.0 %collective-permute-done.20.refs_5_ = bf16[8,64,768]{2,1,0:T(8,128)(2,1)S(1)} collective-permute-done((bf16[8,64,768]{2,1,0:T(8,128)(2,1)S(1)}, bf16[8,64,768]{2,1,0:T(8,128)(2,1)S(1)}, u32[]{:S(2)}, u32[]{:S(2)}) %collective-permute-start.20) | collective-permute-done | bytes 786464 | tf_op jit(solution)/shard_map/ppermute | solution.py:365
  215.4 6.0 %collective-permute-start.23 = (bf16[512,768]{1,0:T(8,128)(2,1)S(1)}, bf16[512,768]{1,0:T(8,128)(2,1)S(1)}, u32[]{:S(2)}, u32[]{:S(2)}) collective-permute-start(bf16[512,768]{1,0:T(8,128)(2,1)S(1)} %convolution_convert_fusion.1), channel_id=1, source_target_pairs={{0,16},{4,20},{8,24},{12,28},{16,0},{20,4},{24,8},{28,12},{1,17},{... | collective-permute-start | bytes 2359304 | tf_op jit(solution)/shard_map/ppermute | solution.py:365
  225.8 10.9 %collective-permute-done.21.refs_6_ = bf16[8,64,768]{2,1,0:T(8,128)(2,1)S(1)} collective-permute-done((bf16[8,64,768]{2,1,0:T(8,128)(2,1)S(1)}, bf16[8,64,768]{2,1,0:T(8,128)(2,1)S(1)}, u32[]{:S(2)}, u32[]{:S(2)}) %collective-permute-start.21) | collective-permute-done | bytes 786464 | tf_op jit(solution)/shard_map/ppermute | solution.py:365
  236.6 2.2 collective-permute-done.23.received
  238.8 18.1 %collective-permute-done.22.refs_7_ = bf16[8,64,768]{2,1,0:T(8,128)(2,1)S(1)} collective-permute-done((bf16[8,64,768]{2,1,0:T(8,128)(2,1)S(1)}, bf16[8,64,768]{2,1,0:T(8,128)(2,1)S(1)}, u32[]{:S(2)}, u32[]{:S(2)}) %collective-permute-start.22) | collective-permute-done | bytes 786464 | tf_op jit(solution)/shard_map/ppermute | solution.py:365
  256.9 3.4 collective-permute-start.28
  261.6 3.2 convolution_convert_fusion
  264.8 8.5 %collective-permute-start.24 = (bf16[512,768]{1,0:T(8,128)(2,1)}, bf16[512,768]{1,0:T(8,128)(2,1)}, u32[]{:S(2)}, u32[]{:S(2)}) collective-permute-start(bf16[512,768]{1,0:T(8,128)(2,1)} %convolution_convert_fusion), channel_id=1, source_target_pairs={{0,16},{4,20},{8,24},{12,28},{16,0},{20,4},{24,8},{28,12},{1,17},{... | collective-permute-start | bytes 2359304 | tf_op jit(solution)/shard_map/ppermute | solution.py:365
  275.3 38.7 %cached_attention.1 = (bf16[8,6,128,512]{3,2,1,0:T(8,128)(2,1)S(1)}, f32[8,6,128,512]{3,2,1,0:T(8,128)}, f32[8,8,512]{2,1,0:T(8,128)S(1)}, f32[8,8,512]{2,1,0:T(8,128)S(1)}) custom-call(s32[80]{0:T(128)S(1)} %broadcast_add_fusion.1.order, s32[80]{0:T(128)S(1)} %get-tuple-element.136.counts, s32[9]{0:T(128)S(1)} %select_reduce_fusion.4.starts, ...), custom_call_target="tpu_custom_call" | custom-call | flops 805306368 | bytes 1572864 | tf_op jit(solution)/shard_map/cached_attention/pallas_call | solution.py:162
  314.0 2.6 copy-done
  317.3 3.3 fusion.22.own
  320.6 3.1 rotate_rows.3
  323.7 5.3 %add_convert_fusion = bf16[512,768]{1,0:T(8,128)(2,1)S(1)} fusion(bf16[512,768]{1,0:T(8,128)(2,1)} %collective-permute-done.24, bf16[512,2560]{1,0:T(8,128)(2,1)} %fusion.1, bf16[2560,768]{1,0:T(8,128)(2,1)} %copy-done.33), kind=kOutput, calls=%fused_computation.7 | convolution fusion | flops 2014445568 | bytes 8126464 | tf_op jit(solution)/shard_map/dot_general | solution.py:530
  329.1 19.3 %block_attention.1 = (bf16[800,256]{1,0:T(8,128)(2,1)S(1)}, bf16[800,256]{1,0:T(8,128)(2,1)S(1)}, bf16[800,256]{1,0:T(8,128)(2,1)S(1)}, bf16[800,256]{1,0:T(8,12...) custom-call(bf16[8,6,128,512]{3,2,1,0:T(8,128)(2,1)} %copy-done, ...), custom_call_target="tpu_custom_call" | custom-call | flops 201326592 | bytes 3145728 | tf_op jit(solution)/shard_map/block_attention/pallas_call | solution.py:256
  362.9 13.8 %collective-permute-done.35.other = bf16[800,256]{1,0:T(8,128)(2,1)} collective-permute-done((bf16[800,256]{1,0:T(8,128)(2,1)S(1)}, bf16[800,256]{1,0:T(8,128)(2,1)}, u32[]{:S(2)}, u32[]{:S(2)}) %collective-permute-start.35) | collective-permute-done | bytes 409632 | tf_op jit(solution)/shard_map/ppermute | solution.py:365
  383.6 2.1 merge_partials.25
  391.0 2.1 merge_partials.19
  402.4 2.7 collective-permute-start.47
  410.2 7.5 %project_out.2 = (f32[2,2,256,640]{3,2,1,0:T(8,128)S(1)}, bf16[2,2,256,640]{3,2,1,0:T(8,128)(2,1)S(1)}) custom-call(s32[6]{0:T(128)S(1)} %stack.50.places, bf16[800,256]{1,0:T(8,128)(2,1)S(1)} %copy-done.7, bf16[640,768]{1,0:T(8,128)(2,1)S(1)} %copy-done.1, bf16[640,768]{1,0:T(8,128)(2,1)} %collective-permute-done.26.refs_1_, ...), custom_call_target="tpu_custom_call" | custom-call | flops 2013265920 | bytes 7864320 | tf_op jit(solution)/shard_map/project_out/pallas_call | solution.py:335
  427.6 7.6 %project_out.3 = (f32[2,2,256,640]{3,2,1,0:T(8,128)S(1)}, bf16[2,2,256,640]{3,2,1,0:T(8,128)(2,1)S(1)}) custom-call(s32[6]{0:T(128)S(1)} %stack.50.places, bf16[800,256]{1,0:T(8,128)(2,1)S(1)} %copy-done.6, bf16[640,768]{1,0:T(8,128)(2,1)S(1)} %copy-done.1, bf16[640,768]{1,0:T(8,128)(2,1)} %collective-permute-done.26.refs_1_, ...), custom_call_target="tpu_custom_call" | custom-call | flops 2013265920 | bytes 7864320 | tf_op jit(solution)/shard_map/project_out/pallas_call | solution.py:335
  440.7 15.1 %collective-permute-done.40 = bf16[2,256,640]{2,1,0:T(8,128)(2,1)S(1)} collective-permute-done((bf16[2,256,640]{2,1,0:T(8,128)(2,1)S(1)}, bf16[2,256,640]{2,1,0:T(8,128)(2,1)S(1)}, u32[]{:S(2)}, u32[]{:S(2)}) %collective-permute-start.40) | collective-permute-done | bytes 655392 | tf_op jit(solution)/shard_map/ppermute | solution.py:661
  456.1 13.3 %collective-permute-done.50 = bf16[2,256,640]{2,1,0:T(8,128)(2,1)S(1)} collective-permute-done((bf16[2,256,640]{2,1,0:T(8,128)(2,1)S(1)}, bf16[2,256,640]{2,1,0:T(8,128)(2,1)S(1)}, u32[]{:S(2)}, u32[]{:S(2)}) %collective-permute-start.50) | collective-permute-done | bytes 655392 | tf_op jit(solution)/shard_map/ppermute | solution.py:661
  (221 shorter events, 91.3 us)
Async XLA Ops:
  0.6 51.3 %collective-permute-start = (bf16[640,768]{1,0:T(8,128)(2,1)}, bf16[640,768]{1,0:T(8,128)(2,1)}, u32[]{:S(2)}, u32[]{:S(2)}) collective-permute-start(bf16[640,768]{1,0:T(8,128)(2,1)} %param.18), channel_id=1, source_target_pairs={{0,4},{4,0},{8,12},{12,8},{16,20},{20,16},{24,28},{28,24},{1,5},{5... | collective-permute-start | bytes 2949128 | tf_op jit(solution)/shard_map/ppermute | solution.py:365
  7.8 31.7 %collective-permute-start.3 = (bf16[512,640]{1,0:T(8,128)(2,1)}, bf16[512,640]{1,0:T(8,128)(2,1)}, u32[]{:S(2)}, u32[]{:S(2)}) collective-permute-start(bf16[512,640]{1,0:T(8,128)(2,1)} %bitcast.18), channel_id=1, source_target_pairs={{0,16},{4,20},{8,24},{12,28},{16,0},{20,4},{24,8},{28,12},{1,17},{... | collective-permute-start | bytes 1966088 | tf_op jit(solution)/shard_map/ppermute | solution.py:365
  11.6 38.1 %collective-permute-start.8 = (f32[8,64]{1,0:T(8,128)S(1)}, f32[8,64]{1,0:T(8,128)S(1)}, u32[]{:S(2)}, u32[]{:S(2)}) collective-permute-start(f32[8,64]{1,0:T(8,128)S(1)} %rsqrt.16), channel_id=1, source_target_pairs={{0,16},{4,20},{8,24},{12,28},{16,0},{20,4},{24,8},{28,12},{1,17},{... | collective-permute-start | bytes 6152 | tf_op jit(solution)/shard_map/ppermute | solution.py:365
  11.9 38.0 %collective-permute-start.1 = (bf16[640,768]{1,0:T(8,128)(2,1)}, bf16[640,768]{1,0:T(8,128)(2,1)}, u32[]{:S(2)}, u32[]{:S(2)}) collective-permute-start(bf16[640,768]{1,0:T(8,128)(2,1)} %param.18), channel_id=1, source_target_pairs={{0,8},{4,12},{8,0},{12,4},{16,24},{20,28},{24,16},{28,20},{1,9},{5... | collective-permute-start | bytes 2949128 | tf_op jit(solution)/shard_map/ppermute | solution.py:365
  13.5 33.3 %collective-permute-start.4 = (bf16[640,768]{1,0:T(8,128)(2,1)}, bf16[640,768]{1,0:T(8,128)(2,1)}, u32[]{:S(2)}, u32[]{:S(2)}) collective-permute-start(bf16[640,768]{1,0:T(8,128)(2,1)} %param.19), channel_id=1, source_target_pairs={{0,4},{4,0},{8,12},{12,8},{16,20},{20,16},{24,28},{28,24},{1,5},{5... | collective-permute-start | bytes 2949128 | tf_op jit(solution)/shard_map/ppermute | solution.py:365
  39.5 42.1 %collective-permute-start.10 = (bf16[640,768]{1,0:T(8,128)(2,1)S(1)}, bf16[640,768]{1,0:T(8,128)(2,1)}, u32[]{:S(2)}, u32[]{:S(2)}) collective-permute-start(bf16[640,768]{1,0:T(8,128)(2,1)S(1)} %copy-done.28), channel_id=1, source_target_pairs={{0,8},{4,12},{8,0},{12,4},{16,24},{20,28},{24,16},{28,20},{1,9},{5... | collective-permute-start | bytes 2949128 | tf_op jit(solution)/shard_map/ppermute | solution.py:365
  46.8 16.2 %collective-permute-start.6 = (bf16[512,640]{1,0:T(8,128)(2,1)}, bf16[512,640]{1,0:T(8,128)(2,1)}, u32[]{:S(2)}, u32[]{:S(2)}) collective-permute-start(bf16[512,640]{1,0:T(8,128)(2,1)} %collective-permute-done.3), channel_id=1, source_target_pairs={{0,2},{1,3},{2,0},{3,1},{4,6},{5,7},{6,4},{7,5},{8,10},{9,11},{10,... | collective-permute-start | bytes 1966088 | tf_op jit(solution)/shard_map/ppermute | solution.py:365
  49.7 31.9 %collective-permute-start.5 = (bf16[512,640]{1,0:T(8,128)(2,1)}, bf16[512,640]{1,0:T(8,128)(2,1)}, u32[]{:S(2)}, u32[]{:S(2)}) collective-permute-start(bf16[512,640]{1,0:T(8,128)(2,1)} %collective-permute-done.3), channel_id=1, source_target_pairs={{0,1},{1,0},{2,3},{3,2},{4,5},{5,4},{6,7},{7,6},{8,9},{9,8},{10,11... | collective-permute-start | bytes 1966088 | tf_op jit(solution)/shard_map/ppermute | solution.py:365
  49.9 34.1 %collective-permute-start.2 = (bf16[640,768]{1,0:T(8,128)(2,1)}, bf16[640,768]{1,0:T(8,128)(2,1)}, u32[]{:S(2)}, u32[]{:S(2)}) collective-permute-start(bf16[640,768]{1,0:T(8,128)(2,1)} %collective-permute-done.1), channel_id=1, source_target_pairs={{0,4},{4,0},{8,12},{12,8},{16,20},{20,16},{24,28},{28,24},{1,5},{5... | collective-permute-start | bytes 2949128 | tf_op jit(solution)/shard_map/ppermute | solution.py:365
  52.0 52.1 %collective-permute-start.13 = (bf16[640,768]{1,0:T(8,128)(2,1)}, bf16[640,768]{1,0:T(8,128)(2,1)}, u32[]{:S(2)}, u32[]{:S(2)}) collective-permute-start(bf16[640,768]{1,0:T(8,128)(2,1)} %param.20), channel_id=1, source_target_pairs={{0,8},{4,12},{8,0},{12,4},{16,24},{20,28},{24,16},{28,20},{1,9},{5... | collective-permute-start | bytes 2949128 | tf_op jit(solution)/shard_map/ppermute | solution.py:365
  63.0 25.3 %collective-permute-start.7 = (bf16[512,640]{1,0:T(8,128)(2,1)}, bf16[512,640]{1,0:T(8,128)(2,1)S(1)}, u32[]{:S(2)}, u32[]{:S(2)}) collective-permute-start(bf16[512,640]{1,0:T(8,128)(2,1)} %collective-permute-done.6), channel_id=1, source_target_pairs={{0,1},{1,0},{2,3},{3,2},{4,5},{5,4},{6,7},{7,6},{8,9},{9,8},{10,11... | collective-permute-start | bytes 1966088 | tf_op jit(solution)/shard_map/ppermute | solution.py:365
  81.5 61.4 %collective-permute-start.12 = (bf16[640,768]{1,0:T(8,128)(2,1)S(1)}, bf16[640,768]{1,0:T(8,128)(2,1)S(1)}, u32[]{:S(2)}, u32[]{:S(2)}) collective-permute-start(bf16[640,768]{1,0:T(8,128)(2,1)S(1)} %copy-done.1), channel_id=1, source_target_pairs={{0,16},{4,20},{8,24},{12,28},{16,0},{20,4},{24,8},{28,12},{1,17},{... | collective-permute-start | bytes 2949128 | tf_op jit(solution)/shard_map/ppermute | solution.py:365
  81.6 61.4 %collective-permute-start.11 = (bf16[640,768]{1,0:T(8,128)(2,1)}, bf16[640,768]{1,0:T(8,128)(2,1)}, u32[]{:S(2)}, u32[]{:S(2)}) collective-permute-start(bf16[640,768]{1,0:T(8,128)(2,1)} %collective-permute-done.10), channel_id=1, source_target_pairs={{0,4},{4,0},{8,12},{12,8},{16,20},{20,16},{24,28},{28,24},{1,5},{5... | collective-permute-start | bytes 2949128 | tf_op jit(solution)/shard_map/ppermute | solution.py:365
  84.0 58.9 %collective-permute-start.14 = (bf16[640,768]{1,0:T(8,128)(2,1)}, bf16[640,768]{1,0:T(8,128)(2,1)}, u32[]{:S(2)}, u32[]{:S(2)}) collective-permute-start(bf16[640,768]{1,0:T(8,128)(2,1)} %param.20), channel_id=1, source_target_pairs={{0,4},{4,0},{8,12},{12,8},{16,20},{20,16},{24,28},{28,24},{1,5},{5... | collective-permute-start | bytes 2949128 | tf_op jit(solution)/shard_map/ppermute | solution.py:365
  93.8 67.9 %collective-permute-start.9 = (bf16[512,768]{1,0:T(8,128)(2,1)S(1)}, bf16[512,768]{1,0:T(8,128)(2,1)}, u32[]{:S(2)}, u32[]{:S(2)}) collective-permute-start(bf16[512,768]{1,0:T(8,128)(2,1)S(1)} %convolution_convert_fusion.2), channel_id=1, source_target_pairs={{0,16},{4,20},{8,24},{12,28},{16,0},{20,4},{24,8},{28,12},{1,17},{... | collective-permute-start | bytes 2359304 | tf_op jit(solution)/shard_map/ppermute | solution.py:365
  104.1 78.1 %collective-permute-start.19 = (bf16[640,768]{1,0:T(8,128)(2,1)}, bf16[640,768]{1,0:T(8,128)(2,1)}, u32[]{:S(2)}, u32[]{:S(2)}) collective-permute-start(bf16[640,768]{1,0:T(8,128)(2,1)} %collective-permute-done.13), channel_id=1, source_target_pairs={{0,4},{4,0},{8,12},{12,8},{16,20},{20,16},{24,28},{28,24},{1,5},{5... | collective-permute-start | bytes 2949128 | tf_op jit(solution)/shard_map/ppermute | solution.py:365
  166.3 21.6 %collective-permute-start.18 = (bf16[8,64,768]{2,1,0:T(8,128)(2,1)}, bf16[8,64,768]{2,1,0:T(8,128)(2,1)S(1)}, u32[]{:S(2)}, u32[]{:S(2)}) collective-permute-start(bf16[8,64,768]{2,1,0:T(8,128)(2,1)} %bitcast.92), channel_id=1, source_target_pairs={{0,16},{4,20},{8,24},{12,28},{16,0},{20,4},{24,8},{28,12},{1,17},{... | collective-permute-start | bytes 2359304 | tf_op jit(solution)/shard_map/ppermute | solution.py:365
  166.4 22.3 %collective-permute-start.16 = (bf16[8,64,768]{2,1,0:T(8,128)(2,1)}, bf16[8,64,768]{2,1,0:T(8,128)(2,1)S(1)}, u32[]{:S(2)}, u32[]{:S(2)}) collective-permute-start(bf16[8,64,768]{2,1,0:T(8,128)(2,1)} %bitcast.93), channel_id=1, source_target_pairs={{0,8},{4,12},{8,0},{12,4},{16,24},{20,28},{24,16},{28,20},{1,9},{5... | collective-permute-start | bytes 2359304 | tf_op jit(solution)/shard_map/ppermute | solution.py:365
  173.1 26.1 %collective-permute-start.15 = (bf16[8,64,768]{2,1,0:T(8,128)(2,1)}, bf16[8,64,768]{2,1,0:T(8,128)(2,1)S(1)}, u32[]{:S(2)}, u32[]{:S(2)}) collective-permute-start(bf16[8,64,768]{2,1,0:T(8,128)(2,1)} %bitcast.94), channel_id=1, source_target_pairs={{0,4},{4,0},{8,12},{12,8},{16,20},{20,16},{24,28},{28,24},{1,5},{5... | collective-permute-start | bytes 2359304 | tf_op jit(solution)/shard_map/ppermute | solution.py:365
  199.2 16.2 %collective-permute-start.20 = (bf16[8,64,768]{2,1,0:T(8,128)(2,1)S(1)}, bf16[8,64,768]{2,1,0:T(8,128)(2,1)S(1)}, u32[]{:S(2)}, u32[]{:S(2)}) collective-permute-start(bf16[8,64,768]{2,1,0:T(8,128)(2,1)S(1)} %collective-permute-done.18.refs_4_), channel_id=1, source_target_pairs={{0,4},{4,0},{8,12},{12,8},{16,20},{20,16},{24,28},{28,24},{1,5},{5... | collective-permute-start | bytes 2359304 | tf_op jit(solution)/shard_map/ppermute | solution.py:365
  210.3 26.4 %collective-permute-start.21 = (bf16[8,64,768]{2,1,0:T(8,128)(2,1)S(1)}, bf16[8,64,768]{2,1,0:T(8,128)(2,1)S(1)}, u32[]{:S(2)}, u32[]{:S(2)}) collective-permute-start(bf16[8,64,768]{2,1,0:T(8,128)(2,1)S(1)} %collective-permute-done.18.refs_4_), channel_id=1, source_target_pairs={{0,8},{4,12},{8,0},{12,4},{16,24},{20,28},{24,16},{28,20},{1,9},{5... | collective-permute-start | bytes 2359304 | tf_op jit(solution)/shard_map/ppermute | solution.py:365
  210.3 15.4 %collective-permute-start.17 = (bf16[8,64,768]{2,1,0:T(8,128)(2,1)S(1)}, bf16[8,64,768]{2,1,0:T(8,128)(2,1)S(1)}, u32[]{:S(2)}, u32[]{:S(2)}) collective-permute-start(bf16[8,64,768]{2,1,0:T(8,128)(2,1)S(1)} %collective-permute-done.16.refs_2_), channel_id=1, source_target_pairs={{0,4},{4,0},{8,12},{12,8},{16,20},{20,16},{24,28},{28,24},{1,5},{5... | collective-permute-start | bytes 2359304 | tf_op jit(solution)/shard_map/ppermute | solution.py:365
  215.4 23.4 %collective-permute-start.23 = (bf16[512,768]{1,0:T(8,128)(2,1)S(1)}, bf16[512,768]{1,0:T(8,128)(2,1)S(1)}, u32[]{:S(2)}, u32[]{:S(2)}) collective-permute-start(bf16[512,768]{1,0:T(8,128)(2,1)S(1)} %convolution_convert_fusion.1), channel_id=1, source_target_pairs={{0,16},{4,20},{8,24},{12,28},{16,0},{20,4},{24,8},{28,12},{1,17},{... | collective-permute-start | bytes 2359304 | tf_op jit(solution)/shard_map/ppermute | solution.py:365
  221.4 35.5 %collective-permute-start.22 = (bf16[8,64,768]{2,1,0:T(8,128)(2,1)S(1)}, bf16[8,64,768]{2,1,0:T(8,128)(2,1)S(1)}, u32[]{:S(2)}, u32[]{:S(2)}) collective-permute-start(bf16[8,64,768]{2,1,0:T(8,128)(2,1)S(1)} %collective-permute-done.20.refs_5_), channel_id=1, source_target_pairs={{0,8},{4,12},{8,0},{12,4},{16,24},{20,28},{24,16},{28,20},{1,9},{5... | collective-permute-start | bytes 2359304 | tf_op jit(solution)/shard_map/ppermute | solution.py:365
  256.9 59.6 %collective-permute-start.25 = (bf16[640,768]{1,0:T(8,128)(2,1)S(1)}, bf16[640,768]{1,0:T(8,128)(2,1)S(1)}, u32[]{:S(2)}, u32[]{:S(2)}) collective-permute-start(bf16[640,768]{1,0:T(8,128)(2,1)S(1)} %copy-done.1), channel_id=1, source_target_pairs={{0,8},{4,12},{8,0},{12,4},{16,24},{20,28},{24,16},{28,20},{1,9},{5... | collective-permute-start | bytes 2949128 | tf_op jit(solution)/shard_map/ppermute | solution.py:365
  256.9 59.6 %collective-permute-start.28 = (bf16[640,768]{1,0:T(8,128)(2,1)S(1)}, bf16[640,768]{1,0:T(8,128)(2,1)}, u32[]{:S(2)}, u32[]{:S(2)}) collective-permute-start(bf16[640,768]{1,0:T(8,128)(2,1)S(1)} %collective-permute-done.12.refs_4_), channel_id=1, source_target_pairs={{0,4},{4,0},{8,12},{12,8},{16,20},{20,16},{24,28},{28,24},{1,5},{5... | collective-permute-start | bytes 2949128 | tf_op jit(solution)/shard_map/ppermute | solution.py:365
  264.8 58.9 %collective-permute-start.24 = (bf16[512,768]{1,0:T(8,128)(2,1)}, bf16[512,768]{1,0:T(8,128)(2,1)}, u32[]{:S(2)}, u32[]{:S(2)}) collective-permute-start(bf16[512,768]{1,0:T(8,128)(2,1)} %convolution_convert_fusion), channel_id=1, source_target_pairs={{0,16},{4,20},{8,24},{12,28},{16,0},{20,4},{24,8},{28,12},{1,17},{... | collective-permute-start | bytes 2359304 | tf_op jit(solution)/shard_map/ppermute | solution.py:365
  273.3 55.8 %collective-permute-start.26 = (bf16[640,768]{1,0:T(8,128)(2,1)S(1)}, bf16[640,768]{1,0:T(8,128)(2,1)}, u32[]{:S(2)}, u32[]{:S(2)}) collective-permute-start(bf16[640,768]{1,0:T(8,128)(2,1)S(1)} %copy-done.1), channel_id=1, source_target_pairs={{0,4},{4,0},{8,12},{12,8},{16,20},{20,16},{24,28},{28,24},{1,5},{5... | collective-permute-start | bytes 2949128 | tf_op jit(solution)/shard_map/ppermute | solution.py:365
  275.1 54.0 %collective-permute-start.27 = (bf16[640,768]{1,0:T(8,128)(2,1)S(1)}, bf16[640,768]{1,0:T(8,128)(2,1)}, u32[]{:S(2)}, u32[]{:S(2)}) collective-permute-start(bf16[640,768]{1,0:T(8,128)(2,1)S(1)} %collective-permute-done.12.refs_4_), channel_id=1, source_target_pairs={{0,8},{4,12},{8,0},{12,4},{16,24},{20,28},{24,16},{28,20},{1,9},{5... | collective-permute-start | bytes 2949128 | tf_op jit(solution)/shard_map/ppermute | solution.py:365
  316.6 41.0 %collective-permute-start.29 = (bf16[640,768]{1,0:T(8,128)(2,1)S(1)}, bf16[640,768]{1,0:T(8,128)(2,1)}, u32[]{:S(2)}, u32[]{:S(2)}) collective-permute-start(bf16[640,768]{1,0:T(8,128)(2,1)S(1)} %collective-permute-done.25.refs_2_), channel_id=1, source_target_pairs={{0,4},{4,0},{8,12},{12,8},{16,20},{20,16},{24,28},{28,24},{1,5},{5... | collective-permute-start | bytes 2949128 | tf_op jit(solution)/shard_map/ppermute | solution.py:365
  316.6 41.0 %collective-permute-start.30 = (bf16[640,768]{1,0:T(8,128)(2,1)}, bf16[640,768]{1,0:T(8,128)(2,1)}, u32[]{:S(2)}, u32[]{:S(2)}) collective-permute-start(bf16[640,768]{1,0:T(8,128)(2,1)} %collective-permute-done.28.refs_5_), channel_id=1, source_target_pairs={{0,8},{4,12},{8,0},{12,4},{16,24},{20,28},{24,16},{28,20},{1,9},{5... | collective-permute-start | bytes 2949128 | tf_op jit(solution)/shard_map/ppermute | solution.py:365
  357.6 19.1 %collective-permute-start.35 = (bf16[800,256]{1,0:T(8,128)(2,1)S(1)}, bf16[800,256]{1,0:T(8,128)(2,1)}, u32[]{:S(2)}, u32[]{:S(2)}) collective-permute-start(bf16[800,256]{1,0:T(8,128)(2,1)S(1)} %get-tuple-element.123), channel_id=1, source_target_pairs={{0,8},{4,12},{8,0},{12,4},{16,24},{20,28},{24,16},{28,20},{1,9},{5... | collective-permute-start | bytes 1228808 | tf_op jit(solution)/shard_map/ppermute | solution.py:365
  358.9 21.9 %collective-permute-start.32 = (bf16[800,256]{1,0:T(8,128)(2,1)}, bf16[800,256]{1,0:T(8,128)(2,1)S(1)}, u32[]{:S(2)}, u32[]{:S(2)}) collective-permute-start(bf16[800,256]{1,0:T(8,128)(2,1)} %get-tuple-element.119), channel_id=1, source_target_pairs={{0,4},{4,0},{8,12},{12,8},{16,20},{20,16},{24,28},{28,24},{1,5},{5... | collective-permute-start | bytes 1228808 | tf_op jit(solution)/shard_map/ppermute | solution.py:365
  360.9 22.7 %collective-permute-start.45 = (bf16[800,256]{1,0:T(8,128)(2,1)}, bf16[800,256]{1,0:T(8,128)(2,1)}, u32[]{:S(2)}, u32[]{:S(2)}) collective-permute-start(bf16[800,256]{1,0:T(8,128)(2,1)} %get-tuple-element.133), channel_id=1, source_target_pairs={{0,8},{4,12},{8,0},{12,4},{16,24},{20,28},{24,16},{28,20},{1,9},{5... | collective-permute-start | bytes 1228808 | tf_op jit(solution)/shard_map/ppermute | solution.py:365
  361.0 24.8 %collective-permute-start.34 = (bf16[800,256]{1,0:T(8,128)(2,1)}, bf16[800,256]{1,0:T(8,128)(2,1)}, u32[]{:S(2)}, u32[]{:S(2)}) collective-permute-start(bf16[800,256]{1,0:T(8,128)(2,1)} %get-tuple-element.121), channel_id=1, source_target_pairs={{0,8},{4,12},{8,0},{12,4},{16,24},{20,28},{24,16},{28,20},{1,9},{5... | collective-permute-start | bytes 1228808 | tf_op jit(solution)/shard_map/ppermute | solution.py:365
  379.2 13.9 %collective-permute-start.31 = (bf16[800,256]{1,0:T(8,128)(2,1)}, bf16[800,256]{1,0:T(8,128)(2,1)}, u32[]{:S(2)}, u32[]{:S(2)}) collective-permute-start(bf16[800,256]{1,0:T(8,128)(2,1)} %copy-done.20), channel_id=1, source_target_pairs={{0,4},{4,0},{8,12},{12,8},{16,20},{20,16},{24,28},{28,24},{1,5},{5... | collective-permute-start | bytes 1228808 | tf_op jit(solution)/shard_map/ppermute | solution.py:365
  380.8 15.0 %collective-permute-start.42 = (bf16[800,256]{1,0:T(8,128)(2,1)}, bf16[800,256]{1,0:T(8,128)(2,1)}, u32[]{:S(2)}, u32[]{:S(2)}) collective-permute-start(bf16[800,256]{1,0:T(8,128)(2,1)} %copy-done.19), channel_id=1, source_target_pairs={{0,4},{4,0},{8,12},{12,8},{16,20},{20,16},{24,28},{28,24},{1,5},{5... | collective-permute-start | bytes 1228808 | tf_op jit(solution)/shard_map/ppermute | solution.py:365
  383.6 14.7 %collective-permute-start.44 = (bf16[800,256]{1,0:T(8,128)(2,1)}, bf16[800,256]{1,0:T(8,128)(2,1)}, u32[]{:S(2)}, u32[]{:S(2)}) collective-permute-start(bf16[800,256]{1,0:T(8,128)(2,1)} %copy-done.18), channel_id=1, source_target_pairs={{0,8},{4,12},{8,0},{12,4},{16,24},{20,28},{24,16},{28,20},{1,9},{5... | collective-permute-start | bytes 1228808 | tf_op jit(solution)/shard_map/ppermute | solution.py:365
  385.7 14.6 %collective-permute-start.46 = (bf16[800,256]{1,0:T(8,128)(2,1)}, bf16[800,256]{1,0:T(8,128)(2,1)}, u32[]{:S(2)}, u32[]{:S(2)}) collective-permute-start(bf16[800,256]{1,0:T(8,128)(2,1)} %merge_partials.25), channel_id=1, source_target_pairs={{0,4},{4,0},{8,12},{12,8},{16,20},{20,16},{24,28},{28,24},{1,5},{5... | collective-permute-start | bytes 1228808 | tf_op jit(solution)/shard_map/ppermute | solution.py:365
  389.1 16.1 %collective-permute-start.33 = (bf16[800,256]{1,0:T(8,128)(2,1)}, bf16[800,256]{1,0:T(8,128)(2,1)}, u32[]{:S(2)}, u32[]{:S(2)}) collective-permute-start(bf16[800,256]{1,0:T(8,128)(2,1)} %merge_partials.15), channel_id=1, source_target_pairs={{0,8},{4,12},{8,0},{12,4},{16,24},{20,28},{24,16},{28,20},{1,9},{5... | collective-permute-start | bytes 1228808 | tf_op jit(solution)/shard_map/ppermute | solution.py:365
  393.1 14.1 %collective-permute-start.37 = (bf16[800,256]{1,0:T(8,128)(2,1)}, bf16[800,256]{1,0:T(8,128)(2,1)}, u32[]{:S(2)}, u32[]{:S(2)}) collective-permute-start(bf16[800,256]{1,0:T(8,128)(2,1)} %merge_partials.19), channel_id=1, source_target_pairs={{0,16},{4,20},{8,24},{12,28},{16,0},{20,4},{24,8},{28,12},{1,17},{... | collective-permute-start | bytes 1228808 | tf_op jit(solution)/shard_map/ppermute | solution.py:365
  395.8 24.6 %collective-permute-start.41 = (bf16[800,256]{1,0:T(8,128)(2,1)S(1)}, bf16[800,256]{1,0:T(8,128)(2,1)}, u32[]{:S(2)}, u32[]{:S(2)}) collective-permute-start(bf16[800,256]{1,0:T(8,128)(2,1)S(1)} %copy-done.17), channel_id=1, source_target_pairs={{0,4},{4,0},{8,12},{12,8},{16,20},{20,16},{24,28},{28,24},{1,5},{5... | collective-permute-start | bytes 1228808 | tf_op jit(solution)/shard_map/ppermute | solution.py:365
  398.3 24.2 %collective-permute-start.43 = (bf16[800,256]{1,0:T(8,128)(2,1)}, bf16[800,256]{1,0:T(8,128)(2,1)}, u32[]{:S(2)}, u32[]{:S(2)}) collective-permute-start(bf16[800,256]{1,0:T(8,128)(2,1)} %merge_partials.22), channel_id=1, source_target_pairs={{0,8},{4,12},{8,0},{12,4},{16,24},{20,28},{24,16},{28,20},{1,9},{5... | collective-permute-start | bytes 1228808 | tf_op jit(solution)/shard_map/ppermute | solution.py:365
  402.4 22.1 %collective-permute-start.47 = (bf16[800,256]{1,0:T(8,128)(2,1)}, bf16[800,256]{1,0:T(8,128)(2,1)}, u32[]{:S(2)}, u32[]{:S(2)}) collective-permute-start(bf16[800,256]{1,0:T(8,128)(2,1)} %merge_partials.26), channel_id=1, source_target_pairs={{0,16},{4,20},{8,24},{12,28},{16,0},{20,4},{24,8},{28,12},{1,17},{... | collective-permute-start | bytes 1228808 | tf_op jit(solution)/shard_map/ppermute | solution.py:365
  420.4 15.6 %collective-permute-start.39 = (bf16[2,256,640]{2,1,0:T(8,128)(2,1)}, bf16[2,256,640]{2,1,0:T(8,128)(2,1)}, u32[]{:S(2)}, u32[]{:S(2)}) collective-permute-start(bf16[2,256,640]{2,1,0:T(8,128)(2,1)} %get-tuple-element.155), channel_id=1, source_target_pairs={{0,1},{1,0},{2,3},{3,2},{4,5},{5,4},{6,7},{7,6},{8,9},{9,8},{10,11... | collective-permute-start | bytes 1966088 | tf_op jit(solution)/shard_map/ppermute | solution.py:661
  438.2 17.6 %collective-permute-start.40 = (bf16[2,256,640]{2,1,0:T(8,128)(2,1)S(1)}, bf16[2,256,640]{2,1,0:T(8,128)(2,1)S(1)}, u32[]{:S(2)}, u32[]{:S(2)}) collective-permute-start(bf16[2,256,640]{2,1,0:T(8,128)(2,1)S(1)} %fusion.5), channel_id=1, source_target_pairs={{0,2},{1,3},{2,0},{3,1},{4,6},{5,7},{6,4},{7,5},{8,10},{9,11},{10,... | collective-permute-start | bytes 1966088 | tf_op jit(solution)/shard_map/ppermute | solution.py:661
  438.3 17.9 %collective-permute-start.48 = (bf16[2,256,640]{2,1,0:T(8,128)(2,1)S(1)}, bf16[2,256,640]{2,1,0:T(8,128)(2,1)S(1)}, u32[]{:S(2)}, u32[]{:S(2)}) collective-permute-start(bf16[2,256,640]{2,1,0:T(8,128)(2,1)S(1)} %get-tuple-element.156), channel_id=1, source_target_pairs={{0,1},{1,0},{2,3},{3,2},{4,5},{5,4},{6,7},{7,6},{8,9},{9,8},{10,11... | collective-permute-start | bytes 1966088 | tf_op jit(solution)/shard_map/ppermute | solution.py:661
  439.0 30.5 %collective-permute-start.50 = (bf16[2,256,640]{2,1,0:T(8,128)(2,1)S(1)}, bf16[2,256,640]{2,1,0:T(8,128)(2,1)S(1)}, u32[]{:S(2)}, u32[]{:S(2)}) collective-permute-start(bf16[2,256,640]{2,1,0:T(8,128)(2,1)S(1)} %fusion.2), channel_id=1, source_target_pairs={{0,2},{1,3},{2,0},{3,1},{4,6},{5,7},{6,4},{7,5},{8,10},{9,11},{10,... | collective-permute-start | bytes 1966088 | tf_op jit(solution)/shard_map/ppermute | solution.py:661
  (41 other events, 325.4 us)

commit v3 on v2

--- a/solution.py
+++ b/solution.py
@@ -484,7 +484,6 @@
     value_shards = gather_plane(
         w_value, query_shards[(0, 1, 0)], query_shards[half_order[-1]]
     )
-    far_out = half_axis.step(after(w_out, (fetched, query_shards[(0, 1, 0)])))
 
     def joined(shards):
         return jnp.concatenate([shards[key] for key in half_order], axis=0)
@@ -549,7 +548,7 @@
     sent_query = product(other_rows, query_weight).astype(jnp.bfloat16)
     received_query = after(
         half_axis.step(sent_query),
-        (key_shards, far_out, value_shards[(0, 1, 0)], value_shards[(0, 0, 1)]),
+        (key_shards, value_shards[(0, 1, 0)], value_shards[(0, 0, 1)]),
     )
     near = rotated_sum(
         product(own_rows, query_weight), received_query, cosine, sine
@@ -558,7 +557,7 @@
     far = after(
         half_axis.step(near), (value_shards, near_tree[(0, 1, 0)], near_tree[(0, 0, 1)])
     )
-    trees = [near_tree, gather_tree(far, (x_axis, z_axis))]
+    trees = [near_tree, gather_tree(far, (z_axis, x_axis))]
     every_query = [trees[key[0]][with_entry(key, 0, 0)] for key in full_order]
 
     sent_key = product(other_rows, key_weight).astype(jnp.bfloat16)
@@ -566,7 +565,7 @@
     new_keys = rotated_sum(product(own_rows, key_weight), received_key, cosine, sine)
     new_keys = new_keys.reshape(piece)
     sent_value = product(other_rows, value_weight).astype(jnp.bfloat16)
-    received_value = half_axis.step(after(sent_value, received_key))
+    received_value = half_axis.step(after(sent_value, (trees[1][(0, 0, 1)], value_shards)))
     new_values = (
         (product(own_rows, value_weight) + received_value.astype(jnp.float32))
         .astype(jnp.bfloat16)
@@ -617,10 +616,13 @@
 
     ready = (every_query, received_key)
     state = cached_attention(
-        after(every_query, received_key), key_cache, value_cache, plan
-    )
-    own_out = gather_gated(after(w_out, ready), z_axis, x_axis)
-    far_out = gather_gated(after(far_out, ready), x_axis, z_axis)
+        after(every_query, (received_key, received_value)), key_cache, value_cache, plan
+    )
+    ready_out = after(w_out, ready)
+    crossed_out = half_axis.step(ready_out)
+    own_out = gather_gated(ready_out, z_axis, x_axis)
+    near_steps = (own_out[(0, 1, 0)], own_out[(0, 0, 1)])
+    far_out = gather_gated(after(crossed_out, (state, near_steps)), z_axis, x_axis)
     out_shards = [(own_out, far_out)[key[0]][with_entry(key, 0, 0)] for key in full_order]
     out_width = model_width // head_size
     lines = [
@@ -631,7 +633,7 @@
     places = jnp.stack(
         [line ^ head_place for line in lines] + [x_axis.before(x) for x in range(x_size)]
     ).astype(jnp.int32)
-    first_steps = [tree[key] for tree in (own_out, far_out) for key in ((0, 1, 0), (0, 0, 1))]
+    first_steps = (near_steps, crossed_out)
     pieces_of = block_attention(seq_size, state, new_keys, after(new_values, first_steps))
     pieces_of = after(pieces_of, out_shards)
     results = []

time: 475 us -> 511 us (1.076)
  waiting for transfers between devices: 204 us -> 262 us
  starting transfers between devices: 81.3 us -> 64.7 us
    ppermute x45, waiting for transfers between devices: 175 us -> 234 us  [step(): return lax.ppermute(value, self.mesh_axis, pairs)]
    ppermute x45, starting transfers between devices: 78.3 us -> 61.6 us  [step(): return lax.ppermute(value, self.mesh_axis, pairs)]
    unnamed x85 -> x107, local copies, waits for them, and re-layouts: 28.6 us -> 29.9 us
  transfers between devices with their start and end apart: 51 -> 51, of which waited for: 19 -> 25; matrix products, arithmetic and copies ran while one was open for 12% -> 11% of each run, Pallas kernels for 23% -> 21%
where the time goes in v3:
time: 511 us; the launch traced here: 506 us
  waiting for transfers between devices  262 us (51%)
  Pallas kernels  104 us (20%)
  starting transfers between devices  64.7 us (13%)
  local copies, waits for them, and re-layouts  40.9 us (8%)
  matrix products  18.8 us (4%)
  other arithmetic  14 us (3%)
    ppermute x45, waiting for transfers between devices, step(): return lax.ppermute(value, self.mesh_axis, pairs)  234 us
    ppermute x45, starting transfers between devices, step(): return lax.ppermute(value, self.mesh_axis, pairs)  61.6 us
    pallas_call x1, Pallas kernels, cached_attention(): pl.pallas_call(functools.partial(cached_kernel, sources), out_shape=[jax....  34.7 us
    unnamed x107, local copies, waits for them, and re-layouts  29.9 us
    pallas_call x14, Pallas kernels, merge(): pl.pallas_call(merge_kernel, out_shape=jax.ShapeDtypeStruct(own.shape, ow...  28.8 us
    ppermute x6, waiting for transfers between devices, per_device(): lax.ppermute(value, 'head', pairs).astype(jnp.float32)  28.4 us
    pallas_call x1, Pallas kernels, block_attention(): pl.pallas_call(functools.partial(block_kernel, sources), out_shape=[piece...  19.3 us
    dot_general x6, matrix products, product(): return jnp.dot(left, weight, preferred_element_type=jnp.float32)  18.8 us
  transfers between devices with their start and end apart: 51, of which 25 were waited for; matrix products, arithmetic and copies ran while one was open for 11% of the time, Pallas kernels for 21%

profile of v3, /device:TPU:0, one launch (start us, length us, event | category | flops | bytes accessed | tf_op | source)
XLA Modules:
  0.0 506.5 jit_solution(5680513178881219863)
XLA Ops:
  0.6 3.0 collective-permute-start
  4.3 2.5 dynamic-slice_bitcast_fusion.4
  7.8 2.6 collective-permute-start.3
  15.3 2.2 fusion.1
  17.9 21.5 %collective-permute-done.3 = bf16[512,640]{1,0:T(8,128)(2,1)S(1)} collective-permute-done((bf16[512,640]{1,0:T(8,128)(2,1)}, bf16[512,640]{1,0:T(8,128)(2,1)S(1)}, u32[]{:S(2)}, u32[]{:S(2)}) %collective-permute-start.3) | collective-permute-done | bytes 655392 | tf_op jit(solution)/shard_map/ppermute | solution.py:365
  40.1 6.7 %collective-permute-done.4 = bf16[640,768]{1,0:T(8,128)(2,1)} collective-permute-done((bf16[640,768]{1,0:T(8,128)(2,1)}, bf16[640,768]{1,0:T(8,128)(2,1)}, u32[]{:S(2)}, u32[]{:S(2)}) %collective-permute-start.4) | collective-permute-done | bytes 983072 | tf_op jit(solution)/shard_map/ppermute | solution.py:365
  54.6 2.2 constant_dynamic-update-slice_fusion.2
  56.8 5.9 %collective-permute-done.6 = bf16[512,640]{1,0:T(8,128)(2,1)} collective-permute-done((bf16[512,640]{1,0:T(8,128)(2,1)S(1)}, bf16[512,640]{1,0:T(8,128)(2,1)}, u32[]{:S(2)}, u32[]{:S(2)}) %collective-permute-start.6) | collective-permute-done | bytes 655392 | tf_op jit(solution)/shard_map/ppermute | solution.py:365
  64.4 6.6 %collective-permute-done.10 = bf16[640,768]{1,0:T(8,128)(2,1)} collective-permute-done((bf16[640,768]{1,0:T(8,128)(2,1)}, bf16[640,768]{1,0:T(8,128)(2,1)}, u32[]{:S(2)}, u32[]{:S(2)}) %collective-permute-start.10) | collective-permute-done | bytes 983072 | tf_op jit(solution)/shard_map/ppermute | solution.py:365
  78.1 2.3 convolution_convert_fusion.2
  80.3 2.7 collective-permute-start.9
  83.7 13.0 %collective-permute-done.12 = bf16[640,768]{1,0:T(8,128)(2,1)} collective-permute-done((bf16[640,768]{1,0:T(8,128)(2,1)}, bf16[640,768]{1,0:T(8,128)(2,1)}, u32[]{:S(2)}, u32[]{:S(2)}) %collective-permute-start.12) | collective-permute-done | bytes 983072 | tf_op jit(solution)/shard_map/ppermute | solution.py:365
  97.2 3.3 fusion.21.own
  100.6 16.7 %collective-permute-done.13 = bf16[640,768]{1,0:T(8,128)(2,1)} collective-permute-done((bf16[640,768]{1,0:T(8,128)(2,1)}, bf16[640,768]{1,0:T(8,128)(2,1)}, u32[]{:S(2)}, u32[]{:S(2)}) %collective-permute-start.13) | collective-permute-done | bytes 983072 | tf_op jit(solution)/shard_map/ppermute | solution.py:365
  118.8 3.1 rotate_rows.2
  121.9 2.6 collective-permute-start.17
  124.5 2.4 collective-permute-start.15
  132.8 5.5 %collective-permute-done.18 = bf16[640,768]{1,0:T(8,128)(2,1)} collective-permute-done((bf16[640,768]{1,0:T(8,128)(2,1)}, bf16[640,768]{1,0:T(8,128)(2,1)}, u32[]{:S(2)}, u32[]{:S(2)}) %collective-permute-start.18) | collective-permute-done | bytes 983072 | tf_op jit(solution)/shard_map/ppermute | solution.py:365
  138.3 20.3 %collective-permute-done.17.refs_4_ = bf16[8,64,768]{2,1,0:T(8,128)(2,1)S(1)} collective-permute-done((bf16[8,64,768]{2,1,0:T(8,128)(2,1)}, bf16[8,64,768]{2,1,0:T(8,128)(2,1)S(1)}, u32[]{:S(2)}, u32[]{:S(2)}) %collective-permute-start.17) | collective-permute-done | bytes 786464 | tf_op jit(solution)/shard_map/ppermute | solution.py:365
  163.0 2.3 convolution_convert_fusion.1
  167.3 13.4 %collective-permute-done.19.refs_5_ = bf16[8,64,768]{2,1,0:T(8,128)(2,1)S(1)} collective-permute-done((bf16[8,64,768]{2,1,0:T(8,128)(2,1)S(1)}, bf16[8,64,768]{2,1,0:T(8,128)(2,1)S(1)}, u32[]{:S(2)}, u32[]{:S(2)}) %collective-permute-start.19) | collective-permute-done | bytes 786464 | tf_op jit(solution)/shard_map/ppermute | solution.py:365
  182.4 2.1 collective-permute-start.21
  187.1 2.3 convolution_convert_fusion
  190.1 7.5 %collective-permute-done.16.refs_3_ = bf16[8,64,768]{2,1,0:T(8,128)(2,1)S(1)} collective-permute-done((bf16[8,64,768]{2,1,0:T(8,128)(2,1)S(1)}, bf16[8,64,768]{2,1,0:T(8,128)(2,1)S(1)}, u32[]{:S(2)}, u32[]{:S(2)}) %collective-permute-start.16) | collective-permute-done | bytes 786464 | tf_op jit(solution)/shard_map/ppermute | solution.py:365
  197.6 14.4 %collective-permute-done.21.refs_7_ = bf16[8,64,768]{2,1,0:T(8,128)(2,1)S(1)} collective-permute-done((bf16[8,64,768]{2,1,0:T(8,128)(2,1)S(1)}, bf16[8,64,768]{2,1,0:T(8,128)(2,1)S(1)}, u32[]{:S(2)}, u32[]{:S(2)}) %collective-permute-start.21) | collective-permute-done | bytes 786464 | tf_op jit(solution)/shard_map/ppermute | solution.py:365
  211.9 20.3 %collective-permute-done.22.received = bf16[512,768]{1,0:T(8,128)(2,1)S(1)} collective-permute-done((bf16[512,768]{1,0:T(8,128)(2,1)S(1)}, bf16[512,768]{1,0:T(8,128)(2,1)S(1)}, u32[]{:S(2)}, u32[]{:S(2)}) %collective-permute-start.22) | collective-permute-done | bytes 786464 | tf_op jit(solution)/shard_map/ppermute | solution.py:365
  233.8 4.0 collective-permute-start.24
  238.3 31.9 %collective-permute-done.23 = bf16[512,768]{1,0:T(8,128)(2,1)S(1)} collective-permute-done((bf16[512,768]{1,0:T(8,128)(2,1)S(1)}, bf16[512,768]{1,0:T(8,128)(2,1)S(1)}, u32[]{:S(2)}, u32[]{:S(2)}) %collective-permute-start.23) | collective-permute-done | bytes 786464 | tf_op jit(solution)/shard_map/ppermute | solution.py:365
  271.4 34.7 %cached_attention.1 = (bf16[8,6,128,512]{3,2,1,0:T(8,128)(2,1)S(1)}, f32[8,6,128,512]{3,2,1,0:T(8,128)}, f32[8,8,512]{2,1,0:T(8,128)S(1)}, f32[8,8,512]{2,1,0:T(8,128)S(1)}) custom-call(s32[80]{0:T(128)S(1)} %broadcast_add_fusion.1.order, s32[80]{0:T(128)S(1)} %get-tuple-element.134.counts, s32[9]{0:T(128)S(1)} %select_reduce_fusion.4.starts, ...), custom_call_target="tpu_custom_call" | custom-call | flops 805306368 | bytes 1572864 | tf_op jit(solution)/shard_map/cached_attention/pallas_call | solution.py:162
  306.1 2.6 copy-done
  308.7 4.5 collective-permute-start.29
  315.1 18.1 %collective-permute-done.29.refs_6_ = bf16[640,768]{1,0:T(8,128)(2,1)} collective-permute-done((bf16[640,768]{1,0:T(8,128)(2,1)S(1)}, bf16[640,768]{1,0:T(8,128)(2,1)}, u32[]{:S(2)}, u32[]{:S(2)}) %collective-permute-start.29) | collective-permute-done | bytes 983072 | tf_op jit(solution)/shard_map/ppermute | solution.py:365
  333.2 3.3 fusion.22.own
  336.6 3.1 rotate_rows.3
  339.7 5.3 %add_convert_fusion = bf16[512,768]{1,0:T(8,128)(2,1)S(1)} fusion(bf16[512,768]{1,0:T(8,128)(2,1)} %copy-done.47, bf16[512,2560]{1,0:T(8,128)(2,1)} %fusion.1, bf16[2560,768]{1,0:T(8,128)(2,1)} %copy-done.35), kind=kOutput, calls=%fused_computation.7 | convolution fusion | flops 2014445568 | bytes 8126464 | tf_op jit(solution)/shard_map/dot_general | solution.py:529
  345.0 19.3 %block_attention.1 = (bf16[800,256]{1,0:T(8,128)(2,1)S(1)}, bf16[800,256]{1,0:T(8,128)(2,1)S(1)}, bf16[800,256]{1,0:T(8,128)(2,1)S(1)}, bf16[800,256]{1,0:T(8,12...) custom-call(bf16[8,6,128,512]{3,2,1,0:T(8,128)(2,1)} %copy-done, ...), custom_call_target="tpu_custom_call" | custom-call | flops 201326592 | bytes 3145728 | tf_op jit(solution)/shard_map/block_attention/pallas_call | solution.py:256
  373.5 3.3 collective-permute-done.30.refs_7_
  379.5 9.8 %collective-permute-done.35.other = bf16[800,256]{1,0:T(8,128)(2,1)} collective-permute-done((bf16[800,256]{1,0:T(8,128)(2,1)S(1)}, bf16[800,256]{1,0:T(8,128)(2,1)}, u32[]{:S(2)}, u32[]{:S(2)}) %collective-permute-start.35) | collective-permute-done | bytes 409632 | tf_op jit(solution)/shard_map/ppermute | solution.py:365
  394.2 2.1 merge_partials.15
  398.5 2.1 merge_partials.25
  400.6 6.3 %collective-permute-done.34.other = bf16[800,256]{1,0:T(8,128)(2,1)} collective-permute-done((bf16[800,256]{1,0:T(8,128)(2,1)}, bf16[800,256]{1,0:T(8,128)(2,1)}, u32[]{:S(2)}, u32[]{:S(2)}) %collective-permute-start.34) | collective-permute-done | bytes 409632 | tf_op jit(solution)/shard_map/ppermute | solution.py:365
  412.5 4.3 collective-permute-start.37
  428.1 5.5 %collective-permute-start.47 = (bf16[800,256]{1,0:T(8,128)(2,1)}, bf16[800,256]{1,0:T(8,128)(2,1)}, u32[]{:S(2)}, u32[]{:S(2)}) collective-permute-start(bf16[800,256]{1,0:T(8,128)(2,1)} %merge_partials.26), channel_id=1, source_target_pairs={{0,16},{4,20},{8,24},{12,28},{16,0},{20,4},{24,8},{28,12},{1,17},{... | collective-permute-start | bytes 1228808 | tf_op jit(solution)/shard_map/ppermute | solution.py:365
  433.6 6.6 %collective-permute-done.33.other = bf16[800,256]{1,0:T(8,128)(2,1)} collective-permute-done((bf16[800,256]{1,0:T(8,128)(2,1)}, bf16[800,256]{1,0:T(8,128)(2,1)}, u32[]{:S(2)}, u32[]{:S(2)}) %collective-permute-start.33) | collective-permute-done | bytes 409632 | tf_op jit(solution)/shard_map/ppermute | solution.py:365
  445.3 7.5 %project_out.2 = (f32[2,2,256,640]{3,2,1,0:T(8,128)S(1)}, bf16[2,2,256,640]{3,2,1,0:T(8,128)(2,1)S(1)}) custom-call(s32[6]{0:T(128)S(1)} %stack.50.places, bf16[800,256]{1,0:T(8,128)(2,1)S(1)} %copy-done.7, bf16[640,768]{1,0:T(8,128)(2,1)S(1)} %copy-done.1, bf16[640,768]{1,0:T(8,128)(2,1)S(1)} %collective-permute-done.25.refs_1_, ...), custom_call_target="tpu_custom_call" | custom-call | flops 2013265920 | bytes 7864320 | tf_op jit(solution)/shard_map/project_out/pallas_call | solution.py:335
  462.7 7.6 %project_out.3 = (f32[2,2,256,640]{3,2,1,0:T(8,128)S(1)}, bf16[2,2,256,640]{3,2,1,0:T(8,128)(2,1)S(1)}) custom-call(s32[6]{0:T(128)S(1)} %stack.50.places, bf16[800,256]{1,0:T(8,128)(2,1)S(1)} %copy-done.6, bf16[640,768]{1,0:T(8,128)(2,1)S(1)} %copy-done.1, bf16[640,768]{1,0:T(8,128)(2,1)S(1)} %collective-permute-done.25.refs_1_, ...), custom_call_target="tpu_custom_call" | custom-call | flops 2013265920 | bytes 7864320 | tf_op jit(solution)/shard_map/project_out/pallas_call | solution.py:335
  475.8 15.1 %collective-permute-done.40 = bf16[2,256,640]{2,1,0:T(8,128)(2,1)S(1)} collective-permute-done((bf16[2,256,640]{2,1,0:T(8,128)(2,1)S(1)}, bf16[2,256,640]{2,1,0:T(8,128)(2,1)S(1)}, u32[]{:S(2)}, u32[]{:S(2)}) %collective-permute-start.40) | collective-permute-done | bytes 655392 | tf_op jit(solution)/shard_map/ppermute | solution.py:663
  491.2 13.3 %collective-permute-done.50 = bf16[2,256,640]{2,1,0:T(8,128)(2,1)S(1)} collective-permute-done((bf16[2,256,640]{2,1,0:T(8,128)(2,1)S(1)}, bf16[2,256,640]{2,1,0:T(8,128)(2,1)S(1)}, u32[]{:S(2)}, u32[]{:S(2)}) %collective-permute-start.50) | collective-permute-done | bytes 655392 | tf_op jit(solution)/shard_map/ppermute | solution.py:663
  (243 shorter events, 107.0 us)
Async XLA Ops:
  0.6 52.4 %collective-permute-start = (bf16[640,768]{1,0:T(8,128)(2,1)}, bf16[640,768]{1,0:T(8,128)(2,1)}, u32[]{:S(2)}, u32[]{:S(2)}) collective-permute-start(bf16[640,768]{1,0:T(8,128)(2,1)} %param.18), channel_id=1, source_target_pairs={{0,4},{4,0},{8,12},{12,8},{16,20},{20,16},{24,28},{28,24},{1,5},{5... | collective-permute-start | bytes 2949128 | tf_op jit(solution)/shard_map/ppermute | solution.py:365
  7.8 31.6 %collective-permute-start.3 = (bf16[512,640]{1,0:T(8,128)(2,1)}, bf16[512,640]{1,0:T(8,128)(2,1)S(1)}, u32[]{:S(2)}, u32[]{:S(2)}) collective-permute-start(bf16[512,640]{1,0:T(8,128)(2,1)} %bitcast.18), channel_id=1, source_target_pairs={{0,16},{4,20},{8,24},{12,28},{16,0},{20,4},{24,8},{28,12},{1,17},{... | collective-permute-start | bytes 1966088 | tf_op jit(solution)/shard_map/ppermute | solution.py:365
  11.6 38.6 %collective-permute-start.8 = (f32[8,64]{1,0:T(8,128)S(1)}, f32[8,64]{1,0:T(8,128)S(1)}, u32[]{:S(2)}, u32[]{:S(2)}) collective-permute-start(f32[8,64]{1,0:T(8,128)S(1)} %rsqrt.16), channel_id=1, source_target_pairs={{0,16},{4,20},{8,24},{12,28},{16,0},{20,4},{24,8},{28,12},{1,17},{... | collective-permute-start | bytes 6152 | tf_op jit(solution)/shard_map/ppermute | solution.py:365
  11.9 38.3 %collective-permute-start.1 = (bf16[640,768]{1,0:T(8,128)(2,1)}, bf16[640,768]{1,0:T(8,128)(2,1)}, u32[]{:S(2)}, u32[]{:S(2)}) collective-permute-start(bf16[640,768]{1,0:T(8,128)(2,1)} %param.18), channel_id=1, source_target_pairs={{0,8},{4,12},{8,0},{12,4},{16,24},{20,28},{24,16},{28,20},{1,9},{5... | collective-permute-start | bytes 2949128 | tf_op jit(solution)/shard_map/ppermute | solution.py:365
  13.5 33.3 %collective-permute-start.4 = (bf16[640,768]{1,0:T(8,128)(2,1)}, bf16[640,768]{1,0:T(8,128)(2,1)}, u32[]{:S(2)}, u32[]{:S(2)}) collective-permute-start(bf16[640,768]{1,0:T(8,128)(2,1)} %param.19), channel_id=1, source_target_pairs={{0,4},{4,0},{8,12},{12,8},{16,20},{20,16},{24,28},{28,24},{1,5},{5... | collective-permute-start | bytes 2949128 | tf_op jit(solution)/shard_map/ppermute | solution.py:365
  39.3 31.7 %collective-permute-start.10 = (bf16[640,768]{1,0:T(8,128)(2,1)}, bf16[640,768]{1,0:T(8,128)(2,1)}, u32[]{:S(2)}, u32[]{:S(2)}) collective-permute-start(bf16[640,768]{1,0:T(8,128)(2,1)} %param.19), channel_id=1, source_target_pairs={{0,8},{4,12},{8,0},{12,4},{16,24},{20,28},{24,16},{28,20},{1,9},{5... | collective-permute-start | bytes 2949128 | tf_op jit(solution)/shard_map/ppermute | solution.py:365
  46.8 16.0 %collective-permute-start.6 = (bf16[512,640]{1,0:T(8,128)(2,1)S(1)}, bf16[512,640]{1,0:T(8,128)(2,1)}, u32[]{:S(2)}, u32[]{:S(2)}) collective-permute-start(bf16[512,640]{1,0:T(8,128)(2,1)S(1)} %collective-permute-done.3), channel_id=1, source_target_pairs={{0,2},{1,3},{2,0},{3,1},{4,6},{5,7},{6,4},{7,5},{8,10},{9,11},{10,... | collective-permute-start | bytes 1966088 | tf_op jit(solution)/shard_map/ppermute | solution.py:365
  50.2 21.1 %collective-permute-start.5 = (bf16[512,640]{1,0:T(8,128)(2,1)S(1)}, bf16[512,640]{1,0:T(8,128)(2,1)}, u32[]{:S(2)}, u32[]{:S(2)}) collective-permute-start(bf16[512,640]{1,0:T(8,128)(2,1)S(1)} %collective-permute-done.3), channel_id=1, source_target_pairs={{0,1},{1,0},{2,3},{3,2},{4,5},{5,4},{6,7},{7,6},{8,9},{9,8},{10,11... | collective-permute-start | bytes 1966088 | tf_op jit(solution)/shard_map/ppermute | solution.py:365
  50.2 24.9 %collective-permute-start.2 = (bf16[640,768]{1,0:T(8,128)(2,1)}, bf16[640,768]{1,0:T(8,128)(2,1)}, u32[]{:S(2)}, u32[]{:S(2)}) collective-permute-start(bf16[640,768]{1,0:T(8,128)(2,1)} %collective-permute-done.1), channel_id=1, source_target_pairs={{0,4},{4,0},{8,12},{12,8},{16,20},{20,16},{24,28},{28,24},{1,5},{5... | collective-permute-start | bytes 2949128 | tf_op jit(solution)/shard_map/ppermute | solution.py:365
  53.1 43.7 %collective-permute-start.12 = (bf16[640,768]{1,0:T(8,128)(2,1)}, bf16[640,768]{1,0:T(8,128)(2,1)}, u32[]{:S(2)}, u32[]{:S(2)}) collective-permute-start(bf16[640,768]{1,0:T(8,128)(2,1)} %param.20), channel_id=1, source_target_pairs={{0,8},{4,12},{8,0},{12,4},{16,24},{20,28},{24,16},{28,20},{1,9},{5... | collective-permute-start | bytes 2949128 | tf_op jit(solution)/shard_map/ppermute | solution.py:365
  62.8 15.1 %collective-permute-start.7 = (bf16[512,640]{1,0:T(8,128)(2,1)}, bf16[512,640]{1,0:T(8,128)(2,1)S(1)}, u32[]{:S(2)}, u32[]{:S(2)}) collective-permute-start(bf16[512,640]{1,0:T(8,128)(2,1)} %collective-permute-done.6), channel_id=1, source_target_pairs={{0,1},{1,0},{2,3},{3,2},{4,5},{5,4},{6,7},{7,6},{8,9},{9,8},{10,11... | collective-permute-start | bytes 1966088 | tf_op jit(solution)/shard_map/ppermute | solution.py:365
  71.0 29.6 %collective-permute-start.11 = (bf16[640,768]{1,0:T(8,128)(2,1)}, bf16[640,768]{1,0:T(8,128)(2,1)}, u32[]{:S(2)}, u32[]{:S(2)}) collective-permute-start(bf16[640,768]{1,0:T(8,128)(2,1)} %collective-permute-done.10), channel_id=1, source_target_pairs={{0,4},{4,0},{8,12},{12,8},{16,20},{20,16},{24,28},{28,24},{1,5},{5... | collective-permute-start | bytes 2949128 | tf_op jit(solution)/shard_map/ppermute | solution.py:365
  75.1 42.1 %collective-permute-start.13 = (bf16[640,768]{1,0:T(8,128)(2,1)}, bf16[640,768]{1,0:T(8,128)(2,1)}, u32[]{:S(2)}, u32[]{:S(2)}) collective-permute-start(bf16[640,768]{1,0:T(8,128)(2,1)} %param.20), channel_id=1, source_target_pairs={{0,4},{4,0},{8,12},{12,8},{16,20},{20,16},{24,28},{28,24},{1,5},{5... | collective-permute-start | bytes 2949128 | tf_op jit(solution)/shard_map/ppermute | solution.py:365
  80.3 36.9 %collective-permute-start.9 = (bf16[512,768]{1,0:T(8,128)(2,1)S(1)}, bf16[512,768]{1,0:T(8,128)(2,1)S(1)}, u32[]{:S(2)}, u32[]{:S(2)}) collective-permute-start(bf16[512,768]{1,0:T(8,128)(2,1)S(1)} %convolution_convert_fusion.2), channel_id=1, source_target_pairs={{0,16},{4,20},{8,24},{12,28},{16,0},{20,4},{24,8},{28,12},{1,17},{... | collective-permute-start | bytes 2359304 | tf_op jit(solution)/shard_map/ppermute | solution.py:365
  96.7 41.6 %collective-permute-start.18 = (bf16[640,768]{1,0:T(8,128)(2,1)}, bf16[640,768]{1,0:T(8,128)(2,1)}, u32[]{:S(2)}, u32[]{:S(2)}) collective-permute-start(bf16[640,768]{1,0:T(8,128)(2,1)} %collective-permute-done.12), channel_id=1, source_target_pairs={{0,4},{4,0},{8,12},{12,8},{16,20},{20,16},{24,28},{28,24},{1,5},{5... | collective-permute-start | bytes 2949128 | tf_op jit(solution)/shard_map/ppermute | solution.py:365
  121.9 36.7 %collective-permute-start.17 = (bf16[8,64,768]{2,1,0:T(8,128)(2,1)}, bf16[8,64,768]{2,1,0:T(8,128)(2,1)S(1)}, u32[]{:S(2)}, u32[]{:S(2)}) collective-permute-start(bf16[8,64,768]{2,1,0:T(8,128)(2,1)} %bitcast.92), channel_id=1, source_target_pairs={{0,16},{4,20},{8,24},{12,28},{16,0},{20,4},{24,8},{28,12},{1,17},{... | collective-permute-start | bytes 2359304 | tf_op jit(solution)/shard_map/ppermute | solution.py:365
  124.5 34.3 %collective-permute-start.15 = (bf16[8,64,768]{2,1,0:T(8,128)(2,1)}, bf16[8,64,768]{2,1,0:T(8,128)(2,1)S(1)}, u32[]{:S(2)}, u32[]{:S(2)}) collective-permute-start(bf16[8,64,768]{2,1,0:T(8,128)(2,1)} %bitcast.93), channel_id=1, source_target_pairs={{0,8},{4,12},{8,0},{12,4},{16,24},{20,28},{24,16},{28,20},{1,9},{5... | collective-permute-start | bytes 2359304 | tf_op jit(solution)/shard_map/ppermute | solution.py:365
  126.9 31.9 %collective-permute-start.14 = (bf16[8,64,768]{2,1,0:T(8,128)(2,1)}, bf16[8,64,768]{2,1,0:T(8,128)(2,1)S(1)}, u32[]{:S(2)}, u32[]{:S(2)}) collective-permute-start(bf16[8,64,768]{2,1,0:T(8,128)(2,1)} %bitcast.94), channel_id=1, source_target_pairs={{0,4},{4,0},{8,12},{12,8},{16,20},{20,16},{24,28},{28,24},{1,5},{5... | collective-permute-start | bytes 2359304 | tf_op jit(solution)/shard_map/ppermute | solution.py:365
  158.8 23.6 %collective-permute-start.20 = (bf16[8,64,768]{2,1,0:T(8,128)(2,1)S(1)}, bf16[8,64,768]{2,1,0:T(8,128)(2,1)S(1)}, u32[]{:S(2)}, u32[]{:S(2)}) collective-permute-start(bf16[8,64,768]{2,1,0:T(8,128)(2,1)S(1)} %collective-permute-done.17.refs_4_), channel_id=1, source_target_pairs={{0,8},{4,12},{8,0},{12,4},{16,24},{20,28},{24,16},{28,20},{1,9},{5... | collective-permute-start | bytes 2359304 | tf_op jit(solution)/shard_map/ppermute | solution.py:365
  160.2 20.5 %collective-permute-start.19 = (bf16[8,64,768]{2,1,0:T(8,128)(2,1)S(1)}, bf16[8,64,768]{2,1,0:T(8,128)(2,1)S(1)}, u32[]{:S(2)}, u32[]{:S(2)}) collective-permute-start(bf16[8,64,768]{2,1,0:T(8,128)(2,1)S(1)} %collective-permute-done.17.refs_4_), channel_id=1, source_target_pairs={{0,4},{4,0},{8,12},{12,8},{16,20},{20,16},{24,28},{28,24},{1,5},{5... | collective-permute-start | bytes 2359304 | tf_op jit(solution)/shard_map/ppermute | solution.py:365
  166.7 30.9 %collective-permute-start.16 = (bf16[8,64,768]{2,1,0:T(8,128)(2,1)S(1)}, bf16[8,64,768]{2,1,0:T(8,128)(2,1)S(1)}, u32[]{:S(2)}, u32[]{:S(2)}) collective-permute-start(bf16[8,64,768]{2,1,0:T(8,128)(2,1)S(1)} %collective-permute-done.15.refs_2_), channel_id=1, source_target_pairs={{0,4},{4,0},{8,12},{12,8},{16,20},{20,16},{24,28},{28,24},{1,5},{5... | collective-permute-start | bytes 2359304 | tf_op jit(solution)/shard_map/ppermute | solution.py:365
  180.7 51.5 %collective-permute-start.22 = (bf16[512,768]{1,0:T(8,128)(2,1)S(1)}, bf16[512,768]{1,0:T(8,128)(2,1)S(1)}, u32[]{:S(2)}, u32[]{:S(2)}) collective-permute-start(bf16[512,768]{1,0:T(8,128)(2,1)S(1)} %convolution_convert_fusion.1), channel_id=1, source_target_pairs={{0,16},{4,20},{8,24},{12,28},{16,0},{20,4},{24,8},{28,12},{1,17},{... | collective-permute-start | bytes 2359304 | tf_op jit(solution)/shard_map/ppermute | solution.py:365
  182.4 29.5 %collective-permute-start.21 = (bf16[8,64,768]{2,1,0:T(8,128)(2,1)S(1)}, bf16[8,64,768]{2,1,0:T(8,128)(2,1)S(1)}, u32[]{:S(2)}, u32[]{:S(2)}) collective-permute-start(bf16[8,64,768]{2,1,0:T(8,128)(2,1)S(1)} %collective-permute-done.20.refs_6_), channel_id=1, source_target_pairs={{0,4},{4,0},{8,12},{12,8},{16,20},{20,16},{24,28},{28,24},{1,5},{5... | collective-permute-start | bytes 2359304 | tf_op jit(solution)/shard_map/ppermute | solution.py:365
  189.4 80.9 %collective-permute-start.23 = (bf16[512,768]{1,0:T(8,128)(2,1)S(1)}, bf16[512,768]{1,0:T(8,128)(2,1)S(1)}, u32[]{:S(2)}, u32[]{:S(2)}) collective-permute-start(bf16[512,768]{1,0:T(8,128)(2,1)S(1)} %convolution_convert_fusion), channel_id=1, source_target_pairs={{0,16},{4,20},{8,24},{12,28},{16,0},{20,4},{24,8},{28,12},{1,17},{... | collective-permute-start | bytes 2359304 | tf_op jit(solution)/shard_map/ppermute | solution.py:365
  232.2 76.4 %collective-permute-start.26 = (bf16[640,768]{1,0:T(8,128)(2,1)S(1)}, bf16[640,768]{1,0:T(8,128)(2,1)S(1)}, u32[]{:S(2)}, u32[]{:S(2)}) collective-permute-start(bf16[640,768]{1,0:T(8,128)(2,1)S(1)} %copy-done.1), channel_id=1, source_target_pairs={{0,16},{4,20},{8,24},{12,28},{16,0},{20,4},{24,8},{28,12},{1,17},{... | collective-permute-start | bytes 2949128 | tf_op jit(solution)/shard_map/ppermute | solution.py:365
  232.2 76.4 %collective-permute-start.25 = (bf16[640,768]{1,0:T(8,128)(2,1)S(1)}, bf16[640,768]{1,0:T(8,128)(2,1)S(1)}, u32[]{:S(2)}, u32[]{:S(2)}) collective-permute-start(bf16[640,768]{1,0:T(8,128)(2,1)S(1)} %copy-done.1), channel_id=1, source_target_pairs={{0,4},{4,0},{8,12},{12,8},{16,20},{20,16},{24,28},{28,24},{1,5},{5... | collective-permute-start | bytes 2949128 | tf_op jit(solution)/shard_map/ppermute | solution.py:365
  233.8 74.9 %collective-permute-start.24 = (bf16[640,768]{1,0:T(8,128)(2,1)S(1)}, bf16[640,768]{1,0:T(8,128)(2,1)}, u32[]{:S(2)}, u32[]{:S(2)}) collective-permute-start(bf16[640,768]{1,0:T(8,128)(2,1)S(1)} %copy-done.1), channel_id=1, source_target_pairs={{0,8},{4,12},{8,0},{12,4},{16,24},{20,28},{24,16},{28,20},{1,9},{5... | collective-permute-start | bytes 2949128 | tf_op jit(solution)/shard_map/ppermute | solution.py:365
  308.7 24.6 %collective-permute-start.29 = (bf16[640,768]{1,0:T(8,128)(2,1)S(1)}, bf16[640,768]{1,0:T(8,128)(2,1)}, u32[]{:S(2)}, u32[]{:S(2)}) collective-permute-start(bf16[640,768]{1,0:T(8,128)(2,1)S(1)} %collective-permute-done.26.refs_4_), channel_id=1, source_target_pairs={{0,8},{4,12},{8,0},{12,4},{16,24},{20,28},{24,16},{28,20},{1,9},{5... | collective-permute-start | bytes 2949128 | tf_op jit(solution)/shard_map/ppermute | solution.py:365
  313.1 60.4 %collective-permute-start.28 = (bf16[640,768]{1,0:T(8,128)(2,1)S(1)}, bf16[640,768]{1,0:T(8,128)(2,1)}, u32[]{:S(2)}, u32[]{:S(2)}) collective-permute-start(bf16[640,768]{1,0:T(8,128)(2,1)S(1)} %collective-permute-done.26.refs_4_), channel_id=1, source_target_pairs={{0,4},{4,0},{8,12},{12,8},{16,20},{20,16},{24,28},{28,24},{1,5},{5... | collective-permute-start | bytes 2949128 | tf_op jit(solution)/shard_map/ppermute | solution.py:365
  313.1 60.4 %collective-permute-start.27 = (bf16[640,768]{1,0:T(8,128)(2,1)}, bf16[640,768]{1,0:T(8,128)(2,1)}, u32[]{:S(2)}, u32[]{:S(2)}) collective-permute-start(bf16[640,768]{1,0:T(8,128)(2,1)} %collective-permute-done.24.refs_2_), channel_id=1, source_target_pairs={{0,4},{4,0},{8,12},{12,8},{16,20},{20,16},{24,28},{28,24},{1,5},{5... | collective-permute-start | bytes 2949128 | tf_op jit(solution)/shard_map/ppermute | solution.py:365
  333.2 43.6 %collective-permute-start.30 = (bf16[640,768]{1,0:T(8,128)(2,1)}, bf16[640,768]{1,0:T(8,128)(2,1)}, u32[]{:S(2)}, u32[]{:S(2)}) collective-permute-start(bf16[640,768]{1,0:T(8,128)(2,1)} %collective-permute-done.29.refs_6_), channel_id=1, source_target_pairs={{0,4},{4,0},{8,12},{12,8},{16,20},{20,16},{24,28},{28,24},{1,5},{5... | collective-permute-start | bytes 2949128 | tf_op jit(solution)/shard_map/ppermute | solution.py:365
  377.2 16.2 %collective-permute-start.32 = (bf16[800,256]{1,0:T(8,128)(2,1)}, bf16[800,256]{1,0:T(8,128)(2,1)S(1)}, u32[]{:S(2)}, u32[]{:S(2)}) collective-permute-start(bf16[800,256]{1,0:T(8,128)(2,1)} %get-tuple-element.117), channel_id=1, source_target_pairs={{0,4},{4,0},{8,12},{12,8},{16,20},{20,16},{24,28},{28,24},{1,5},{5... | collective-permute-start | bytes 1228808 | tf_op jit(solution)/shard_map/ppermute | solution.py:365
  377.5 20.6 %collective-permute-start.45 = (bf16[800,256]{1,0:T(8,128)(2,1)}, bf16[800,256]{1,0:T(8,128)(2,1)}, u32[]{:S(2)}, u32[]{:S(2)}) collective-permute-start(bf16[800,256]{1,0:T(8,128)(2,1)} %get-tuple-element.131), channel_id=1, source_target_pairs={{0,8},{4,12},{8,0},{12,4},{16,24},{20,28},{24,16},{28,20},{1,9},{5... | collective-permute-start | bytes 1228808 | tf_op jit(solution)/shard_map/ppermute | solution.py:365
  379.1 27.8 %collective-permute-start.34 = (bf16[800,256]{1,0:T(8,128)(2,1)}, bf16[800,256]{1,0:T(8,128)(2,1)}, u32[]{:S(2)}, u32[]{:S(2)}) collective-permute-start(bf16[800,256]{1,0:T(8,128)(2,1)} %get-tuple-element.119), channel_id=1, source_target_pairs={{0,8},{4,12},{8,0},{12,4},{16,24},{20,28},{24,16},{28,20},{1,9},{5... | collective-permute-start | bytes 1228808 | tf_op jit(solution)/shard_map/ppermute | solution.py:365
  391.4 17.8 %collective-permute-start.36 = (bf16[800,256]{1,0:T(8,128)(2,1)}, bf16[800,256]{1,0:T(8,128)(2,1)}, u32[]{:S(2)}, u32[]{:S(2)}) collective-permute-start(bf16[800,256]{1,0:T(8,128)(2,1)} %merge_partials.18), channel_id=1, source_target_pairs={{0,4},{4,0},{8,12},{12,8},{16,20},{20,16},{24,28},{28,24},{1,5},{5... | collective-permute-start | bytes 1228808 | tf_op jit(solution)/shard_map/ppermute | solution.py:365
  391.7 20.8 %collective-permute-start.31 = (bf16[800,256]{1,0:T(8,128)(2,1)}, bf16[800,256]{1,0:T(8,128)(2,1)}, u32[]{:S(2)}, u32[]{:S(2)}) collective-permute-start(bf16[800,256]{1,0:T(8,128)(2,1)} %copy-done.20), channel_id=1, source_target_pairs={{0,4},{4,0},{8,12},{12,8},{16,20},{20,16},{24,28},{28,24},{1,5},{5... | collective-permute-start | bytes 1228808 | tf_op jit(solution)/shard_map/ppermute | solution.py:365
  393.4 26.9 %collective-permute-start.42 = (bf16[800,256]{1,0:T(8,128)(2,1)}, bf16[800,256]{1,0:T(8,128)(2,1)}, u32[]{:S(2)}, u32[]{:S(2)}) collective-permute-start(bf16[800,256]{1,0:T(8,128)(2,1)} %copy-done.19), channel_id=1, source_target_pairs={{0,4},{4,0},{8,12},{12,8},{16,20},{20,16},{24,28},{28,24},{1,5},{5... | collective-permute-start | bytes 1228808 | tf_op jit(solution)/shard_map/ppermute | solution.py:365
  398.1 25.2 %collective-permute-start.44 = (bf16[800,256]{1,0:T(8,128)(2,1)}, bf16[800,256]{1,0:T(8,128)(2,1)}, u32[]{:S(2)}, u32[]{:S(2)}) collective-permute-start(bf16[800,256]{1,0:T(8,128)(2,1)} %copy-done.18), channel_id=1, source_target_pairs={{0,8},{4,12},{8,0},{12,4},{16,24},{20,28},{24,16},{28,20},{1,9},{5... | collective-permute-start | bytes 1228808 | tf_op jit(solution)/shard_map/ppermute | solution.py:365
  406.9 19.2 %collective-permute-start.46 = (bf16[800,256]{1,0:T(8,128)(2,1)}, bf16[800,256]{1,0:T(8,128)(2,1)}, u32[]{:S(2)}, u32[]{:S(2)}) collective-permute-start(bf16[800,256]{1,0:T(8,128)(2,1)} %merge_partials.25), channel_id=1, source_target_pairs={{0,4},{4,0},{8,12},{12,8},{16,20},{20,16},{24,28},{28,24},{1,5},{5... | collective-permute-start | bytes 1228808 | tf_op jit(solution)/shard_map/ppermute | solution.py:365
  409.2 31.0 %collective-permute-start.33 = (bf16[800,256]{1,0:T(8,128)(2,1)}, bf16[800,256]{1,0:T(8,128)(2,1)}, u32[]{:S(2)}, u32[]{:S(2)}) collective-permute-start(bf16[800,256]{1,0:T(8,128)(2,1)} %merge_partials.15), channel_id=1, source_target_pairs={{0,8},{4,12},{8,0},{12,4},{16,24},{20,28},{24,16},{28,20},{1,9},{5... | collective-permute-start | bytes 1228808 | tf_op jit(solution)/shard_map/ppermute | solution.py:365
  412.5 29.8 %collective-permute-start.37 = (bf16[800,256]{1,0:T(8,128)(2,1)}, bf16[800,256]{1,0:T(8,128)(2,1)}, u32[]{:S(2)}, u32[]{:S(2)}) collective-permute-start(bf16[800,256]{1,0:T(8,128)(2,1)} %merge_partials.19), channel_id=1, source_target_pairs={{0,16},{4,20},{8,24},{12,28},{16,0},{20,4},{24,8},{28,12},{1,17},{... | collective-permute-start | bytes 1228808 | tf_op jit(solution)/shard_map/ppermute | solution.py:365
  420.4 35.1 %collective-permute-start.41 = (bf16[800,256]{1,0:T(8,128)(2,1)S(1)}, bf16[800,256]{1,0:T(8,128)(2,1)}, u32[]{:S(2)}, u32[]{:S(2)}) collective-permute-start(bf16[800,256]{1,0:T(8,128)(2,1)S(1)} %copy-done.17), channel_id=1, source_target_pairs={{0,4},{4,0},{8,12},{12,8},{16,20},{20,16},{24,28},{28,24},{1,5},{5... | collective-permute-start | bytes 1228808 | tf_op jit(solution)/shard_map/ppermute | solution.py:365
  423.3 34.2 %collective-permute-start.43 = (bf16[800,256]{1,0:T(8,128)(2,1)}, bf16[800,256]{1,0:T(8,128)(2,1)}, u32[]{:S(2)}, u32[]{:S(2)}) collective-permute-start(bf16[800,256]{1,0:T(8,128)(2,1)} %merge_partials.22), channel_id=1, source_target_pairs={{0,8},{4,12},{8,0},{12,4},{16,24},{20,28},{24,16},{28,20},{1,9},{5... | collective-permute-start | bytes 1228808 | tf_op jit(solution)/shard_map/ppermute | solution.py:365
  428.1 31.5 %collective-permute-start.47 = (bf16[800,256]{1,0:T(8,128)(2,1)}, bf16[800,256]{1,0:T(8,128)(2,1)}, u32[]{:S(2)}, u32[]{:S(2)}) collective-permute-start(bf16[800,256]{1,0:T(8,128)(2,1)} %merge_partials.26), channel_id=1, source_target_pairs={{0,16},{4,20},{8,24},{12,28},{16,0},{20,4},{24,8},{28,12},{1,17},{... | collective-permute-start | bytes 1228808 | tf_op jit(solution)/shard_map/ppermute | solution.py:365
  455.5 15.6 %collective-permute-start.39 = (bf16[2,256,640]{2,1,0:T(8,128)(2,1)}, bf16[2,256,640]{2,1,0:T(8,128)(2,1)}, u32[]{:S(2)}, u32[]{:S(2)}) collective-permute-start(bf16[2,256,640]{2,1,0:T(8,128)(2,1)} %get-tuple-element.153), channel_id=1, source_target_pairs={{0,1},{1,0},{2,3},{3,2},{4,5},{5,4},{6,7},{7,6},{8,9},{9,8},{10,11... | collective-permute-start | bytes 1966088 | tf_op jit(solution)/shard_map/ppermute | solution.py:663
  473.2 17.6 %collective-permute-start.40 = (bf16[2,256,640]{2,1,0:T(8,128)(2,1)S(1)}, bf16[2,256,640]{2,1,0:T(8,128)(2,1)S(1)}, u32[]{:S(2)}, u32[]{:S(2)}) collective-permute-start(bf16[2,256,640]{2,1,0:T(8,128)(2,1)S(1)} %fusion.5), channel_id=1, source_target_pairs={{0,2},{1,3},{2,0},{3,1},{4,6},{5,7},{6,4},{7,5},{8,10},{9,11},{10,... | collective-permute-start | bytes 1966088 | tf_op jit(solution)/shard_map/ppermute | solution.py:663
  473.3 17.9 %collective-permute-start.48 = (bf16[2,256,640]{2,1,0:T(8,128)(2,1)S(1)}, bf16[2,256,640]{2,1,0:T(8,128)(2,1)S(1)}, u32[]{:S(2)}, u32[]{:S(2)}) collective-permute-start(bf16[2,256,640]{2,1,0:T(8,128)(2,1)S(1)} %get-tuple-element.154), channel_id=1, source_target_pairs={{0,1},{1,0},{2,3},{3,2},{4,5},{5,4},{6,7},{7,6},{8,9},{9,8},{10,11... | collective-permute-start | bytes 1966088 | tf_op jit(solution)/shard_map/ppermute | solution.py:663
  474.0 30.5 %collective-permute-start.50 = (bf16[2,256,640]{2,1,0:T(8,128)(2,1)S(1)}, bf16[2,256,640]{2,1,0:T(8,128)(2,1)S(1)}, u32[]{:S(2)}, u32[]{:S(2)}) collective-permute-start(bf16[2,256,640]{2,1,0:T(8,128)(2,1)S(1)} %fusion.2), channel_id=1, source_target_pairs={{0,2},{1,3},{2,0},{3,1},{4,6},{5,7},{6,4},{7,5},{8,10},{9,11},{10,... | collective-permute-start | bytes 1966088 | tf_op jit(solution)/shard_map/ppermute | solution.py:663
  (52 other events, 723.1 us)

commit v4 on v3

--- a/solution.py
+++ b/solution.py
@@ -557,15 +557,16 @@
     far = after(
         half_axis.step(near), (value_shards, near_tree[(0, 1, 0)], near_tree[(0, 0, 1)])
     )
+    crossed_out = half_axis.step(after(w_out, far))
     trees = [near_tree, gather_tree(far, (z_axis, x_axis))]
     every_query = [trees[key[0]][with_entry(key, 0, 0)] for key in full_order]
 
     sent_key = product(other_rows, key_weight).astype(jnp.bfloat16)
-    received_key = half_axis.step(after(sent_key, (trees[1][(0, 0, 1)], value_shards)))
+    received_key = half_axis.step(after(sent_key, crossed_out))
     new_keys = rotated_sum(product(own_rows, key_weight), received_key, cosine, sine)
     new_keys = new_keys.reshape(piece)
     sent_value = product(other_rows, value_weight).astype(jnp.bfloat16)
-    received_value = half_axis.step(after(sent_value, (trees[1][(0, 0, 1)], value_shards)))
+    received_value = half_axis.step(after(sent_value, crossed_out))
     new_values = (
         (product(own_rows, value_weight) + received_value.astype(jnp.float32))
         .astype(jnp.bfloat16)
@@ -614,15 +615,9 @@
                 found[with_entry(key, second.rank, more)] = item
         return found
 
-    ready = (every_query, received_key)
-    state = cached_attention(
-        after(every_query, (received_key, received_value)), key_cache, value_cache, plan
-    )
-    ready_out = after(w_out, ready)
-    crossed_out = half_axis.step(ready_out)
-    own_out = gather_gated(ready_out, z_axis, x_axis)
-    near_steps = (own_out[(0, 1, 0)], own_out[(0, 0, 1)])
-    far_out = gather_gated(after(crossed_out, (state, near_steps)), z_axis, x_axis)
+    state = cached_attention(every_query, key_cache, value_cache, plan)
+    own_out = gather_gated(after(w_out, every_query), z_axis, x_axis)
+    far_out = gather_gated(after(crossed_out, every_query), x_axis, z_axis)
     out_shards = [(own_out, far_out)[key[0]][with_entry(key, 0, 0)] for key in full_order]
     out_width = model_width // head_size
     lines = [
@@ -633,7 +628,7 @@
     places = jnp.stack(
         [line ^ head_place for line in lines] + [x_axis.before(x) for x in range(x_size)]
     ).astype(jnp.int32)
-    first_steps = (near_steps, crossed_out)
+    first_steps = [tree[key] for tree in (own_out, far_out) for key in ((0, 1, 0), (0, 0, 1))]
     pieces_of = block_attention(seq_size, state, new_keys, after(new_values, first_steps))
     pieces_of = after(pieces_of, out_shards)
     results = []

time: 511 us -> 471 us (0.922)
  waiting for transfers between devices: 262 us -> 241 us
  starting transfers between devices: 64.7 us -> 47.7 us
    ppermute x45, waiting for transfers between devices: 234 us -> 212 us  [step(): return lax.ppermute(value, self.mesh_axis, pairs)]
    ppermute x45, starting transfers between devices: 61.6 us -> 44.7 us  [step(): return lax.ppermute(value, self.mesh_axis, pairs)]
    unnamed x107 -> x115, local copies, waits for them, and re-layouts: 29.9 us -> 28 us
  transfers between devices with their start and end apart: 51 -> 51, of which waited for: 25 -> 24; matrix products, arithmetic and copies ran while one was open for 11% -> 11% of each run, Pallas kernels for 21% -> 23%
where the time goes in v4:
time: 471 us; the launch traced here: 468 us
  waiting for transfers between devices  241 us (51%)
  Pallas kernels  108 us (23%)
  starting transfers between devices  47.7 us (10%)
  local copies, waits for them, and re-layouts  37.8 us (8%)
  matrix products  19.7 us (4%)
  other arithmetic  12.5 us (3%)
    ppermute x45, waiting for transfers between devices, step(): return lax.ppermute(value, self.mesh_axis, pairs)  212 us
    ppermute x45, starting transfers between devices, step(): return lax.ppermute(value, self.mesh_axis, pairs)  44.7 us
    pallas_call x1, Pallas kernels, cached_attention(): pl.pallas_call(functools.partial(cached_kernel, sources), out_shape=[jax....  38.8 us
    pallas_call x14, Pallas kernels, merge(): pl.pallas_call(merge_kernel, out_shape=jax.ShapeDtypeStruct(own.shape, ow...  28.8 us
    ppermute x6, waiting for transfers between devices, per_device(): lax.ppermute(value, 'head', pairs).astype(jnp.float32)  28.4 us
    unnamed x115, local copies, waits for them, and re-layouts  28 us
    dot_general x6, matrix products, product(): return jnp.dot(left, weight, preferred_element_type=jnp.float32)  19.7 us
    pallas_call x1, Pallas kernels, block_attention(): pl.pallas_call(functools.partial(block_kernel, sources), out_shape=[piece...  19.3 us
  transfers between devices with their start and end apart: 51, of which 24 were waited for; matrix products, arithmetic and copies ran while one was open for 11% of the time, Pallas kernels for 23%

profile of v4, /device:TPU:0, one launch (start us, length us, event | category | flops | bytes accessed | tf_op | source)
XLA Modules:
  0.0 468.3 jit_solution(1822778395515011371)
XLA Ops:
  0.6 3.0 collective-permute-start
  4.3 2.5 dynamic-slice_bitcast_fusion.4
  7.8 2.6 collective-permute-start.3
  16.3 23.0 %collective-permute-done.3 = bf16[512,640]{1,0:T(8,128)(2,1)S(1)} collective-permute-done((bf16[512,640]{1,0:T(8,128)(2,1)}, bf16[512,640]{1,0:T(8,128)(2,1)S(1)}, u32[]{:S(2)}, u32[]{:S(2)}) %collective-permute-start.3) | collective-permute-done | bytes 655392 | tf_op jit(solution)/shard_map/ppermute | solution.py:365
  40.1 6.7 %collective-permute-done.4 = bf16[640,768]{1,0:T(8,128)(2,1)} collective-permute-done((bf16[640,768]{1,0:T(8,128)(2,1)}, bf16[640,768]{1,0:T(8,128)(2,1)}, u32[]{:S(2)}, u32[]{:S(2)}) %collective-permute-start.4) | collective-permute-done | bytes 983072 | tf_op jit(solution)/shard_map/ppermute | solution.py:365
  48.5 2.2 constant_dynamic-update-slice_fusion.3
  55.9 2.2 constant_dynamic-update-slice_fusion.2
  58.1 4.7 %collective-permute-done.6 = bf16[512,640]{1,0:T(8,128)(2,1)} collective-permute-done((bf16[512,640]{1,0:T(8,128)(2,1)S(1)}, bf16[512,640]{1,0:T(8,128)(2,1)}, u32[]{:S(2)}, u32[]{:S(2)}) %collective-permute-start.6) | collective-permute-done | bytes 655392 | tf_op jit(solution)/shard_map/ppermute | solution.py:365
  64.5 6.5 %collective-permute-done.10 = bf16[640,768]{1,0:T(8,128)(2,1)} collective-permute-done((bf16[640,768]{1,0:T(8,128)(2,1)}, bf16[640,768]{1,0:T(8,128)(2,1)}, u32[]{:S(2)}, u32[]{:S(2)}) %collective-permute-start.10) | collective-permute-done | bytes 983072 | tf_op jit(solution)/shard_map/ppermute | solution.py:365
  73.6 2.7 collective-permute-done.2
  79.3 2.3 convolution_convert_fusion.2
  81.6 2.7 collective-permute-start.9
  85.0 10.5 %collective-permute-done.12 = bf16[640,768]{1,0:T(8,128)(2,1)} collective-permute-done((bf16[640,768]{1,0:T(8,128)(2,1)}, bf16[640,768]{1,0:T(8,128)(2,1)}, u32[]{:S(2)}, u32[]{:S(2)}) %collective-permute-start.12) | collective-permute-done | bytes 983072 | tf_op jit(solution)/shard_map/ppermute | solution.py:365
  96.0 3.4 fusion.21.own
  99.4 19.0 %collective-permute-done.13 = bf16[640,768]{1,0:T(8,128)(2,1)S(1)} collective-permute-done((bf16[640,768]{1,0:T(8,128)(2,1)S(1)}, bf16[640,768]{1,0:T(8,128)(2,1)S(1)}, u32[]{:S(2)}, u32[]{:S(2)}) %collective-permute-start.13) | collective-permute-done | bytes 983072 | tf_op jit(solution)/shard_map/ppermute | solution.py:365
  121.0 3.1 rotate_rows.2
  124.1 2.6 collective-permute-start.17
  130.3 9.3 %collective-permute-done.18 = bf16[640,768]{1,0:T(8,128)(2,1)} collective-permute-done((bf16[640,768]{1,0:T(8,128)(2,1)}, bf16[640,768]{1,0:T(8,128)(2,1)}, u32[]{:S(2)}, u32[]{:S(2)}) %collective-permute-start.18) | collective-permute-done | bytes 983072 | tf_op jit(solution)/shard_map/ppermute | solution.py:365
  139.6 21.2 %collective-permute-done.17.refs_4_ = bf16[8,64,768]{2,1,0:T(8,128)(2,1)S(1)} collective-permute-done((bf16[8,64,768]{2,1,0:T(8,128)(2,1)}, bf16[8,64,768]{2,1,0:T(8,128)(2,1)S(1)}, u32[]{:S(2)}, u32[]{:S(2)}) %collective-permute-start.17) | collective-permute-done | bytes 786464 | tf_op jit(solution)/shard_map/ppermute | solution.py:365
  165.6 2.4 collective-permute-start.22
  170.1 22.4 %collective-permute-done.20.refs_6_ = bf16[8,64,768]{2,1,0:T(8,128)(2,1)S(1)} collective-permute-done((bf16[8,64,768]{2,1,0:T(8,128)(2,1)S(1)}, bf16[8,64,768]{2,1,0:T(8,128)(2,1)S(1)}, u32[]{:S(2)}, u32[]{:S(2)}) %collective-permute-start.20) | collective-permute-done | bytes 786464 | tf_op jit(solution)/shard_map/ppermute | solution.py:365
  194.0 2.3 convolution_convert_fusion.1
  197.7 7.8 %collective-permute-done.16.refs_3_ = bf16[8,64,768]{2,1,0:T(8,128)(2,1)S(1)} collective-permute-done((bf16[8,64,768]{2,1,0:T(8,128)(2,1)S(1)}, bf16[8,64,768]{2,1,0:T(8,128)(2,1)S(1)}, u32[]{:S(2)}, u32[]{:S(2)}) %collective-permute-start.16) | collective-permute-done | bytes 786464 | tf_op jit(solution)/shard_map/ppermute | solution.py:365
  205.5 15.3 %collective-permute-done.21.refs_7_ = bf16[8,64,768]{2,1,0:T(8,128)(2,1)S(1)} collective-permute-done((bf16[8,64,768]{2,1,0:T(8,128)(2,1)S(1)}, bf16[8,64,768]{2,1,0:T(8,128)(2,1)S(1)}, u32[]{:S(2)}, u32[]{:S(2)}) %collective-permute-start.21) | collective-permute-done | bytes 786464 | tf_op jit(solution)/shard_map/ppermute | solution.py:365
  224.2 3.2 convolution_convert_fusion
  227.4 2.8 collective-permute-start.24
  230.7 38.8 %cached_attention.1 = (bf16[8,6,128,512]{3,2,1,0:T(8,128)(2,1)S(1)}, f32[8,6,128,512]{3,2,1,0:T(8,128)}, f32[8,8,512]{2,1,0:T(8,128)S(1)}, f32[8,8,512]{2,1,0:T(8,128)S(1)}) custom-call(s32[80]{0:T(128)S(1)} %broadcast_add_fusion.1.order, s32[80]{0:T(128)S(1)} %get-tuple-element.120.counts, s32[9]{0:T(128)S(1)} %select_reduce_fusion.4.starts, ...), custom_call_target="tpu_custom_call" | custom-call | flops 805306368 | bytes 1572864 | tf_op jit(solution)/shard_map/cached_attention/pallas_call | solution.py:162
  269.6 2.6 copy-done
  272.2 7.0 %collective-permute-done.23.received = bf16[512,768]{1,0:T(8,128)(2,1)} collective-permute-done((bf16[512,768]{1,0:T(8,128)(2,1)S(1)}, bf16[512,768]{1,0:T(8,128)(2,1)}, u32[]{:S(2)}, u32[]{:S(2)}) %collective-permute-start.23) | collective-permute-done | bytes 786464 | tf_op jit(solution)/shard_map/ppermute | solution.py:365
  279.2 3.3 fusion.22.own
  282.5 3.1 rotate_rows.3
  285.6 7.7 %collective-permute-done.24 = bf16[512,768]{1,0:T(8,128)(2,1)} collective-permute-done((bf16[512,768]{1,0:T(8,128)(2,1)}, bf16[512,768]{1,0:T(8,128)(2,1)}, u32[]{:S(2)}, u32[]{:S(2)}) %collective-permute-start.24) | collective-permute-done | bytes 786464 | tf_op jit(solution)/shard_map/ppermute | solution.py:365
  293.3 5.3 %add_convert_fusion = bf16[512,768]{1,0:T(8,128)(2,1)S(1)} fusion(bf16[512,768]{1,0:T(8,128)(2,1)} %collective-permute-done.24, bf16[512,2560]{1,0:T(8,128)(2,1)} %copy-done.25, bf16[2560,768]{1,0:T(8,128)(2,1)} %copy-done.40), kind=kOutput, calls=%fused_computation.7 | convolution fusion | flops 2014445568 | bytes 8126464 | tf_op jit(solution)/shard_map/dot_general | solution.py:529
  298.6 14.1 %collective-permute-done.27.refs_6_ = bf16[640,768]{1,0:T(8,128)(2,1)} collective-permute-done((bf16[640,768]{1,0:T(8,128)(2,1)S(1)}, bf16[640,768]{1,0:T(8,128)(2,1)}, u32[]{:S(2)}, u32[]{:S(2)}) %collective-permute-start.27) | collective-permute-done | bytes 983072 | tf_op jit(solution)/shard_map/ppermute | solution.py:365
  312.7 19.3 %block_attention.1 = (bf16[800,256]{1,0:T(8,128)(2,1)S(1)}, bf16[800,256]{1,0:T(8,128)(2,1)S(1)}, bf16[800,256]{1,0:T(8,128)(2,1)S(1)}, bf16[800,256]{1,0:T(8,12...) custom-call(bf16[8,6,128,512]{3,2,1,0:T(8,128)(2,1)} %copy-done, ...), custom_call_target="tpu_custom_call" | custom-call | flops 201326592 | bytes 3145728 | tf_op jit(solution)/shard_map/block_attention/pallas_call | solution.py:256
  343.3 10.3 %collective-permute-done.35.other = bf16[800,256]{1,0:T(8,128)(2,1)} collective-permute-done((bf16[800,256]{1,0:T(8,128)(2,1)S(1)}, bf16[800,256]{1,0:T(8,128)(2,1)}, u32[]{:S(2)}, u32[]{:S(2)}) %collective-permute-start.35) | collective-permute-done | bytes 409632 | tf_op jit(solution)/shard_map/ppermute | solution.py:365
  353.7 2.1 merge_partials.18
  362.4 2.1 merge_partials.25
  364.5 11.1 %collective-permute-done.34.other = bf16[800,256]{1,0:T(8,128)(2,1)} collective-permute-done((bf16[800,256]{1,0:T(8,128)(2,1)}, bf16[800,256]{1,0:T(8,128)(2,1)}, u32[]{:S(2)}, u32[]{:S(2)}) %collective-permute-start.34) | collective-permute-done | bytes 409632 | tf_op jit(solution)/shard_map/ppermute | solution.py:365
  377.7 2.1 merge_partials.19
  384.6 2.1 merge_partials.22
  386.7 2.7 collective-permute-done.44.other
  395.0 7.0 %collective-permute-done.33.other = bf16[800,256]{1,0:T(8,128)(2,1)} collective-permute-done((bf16[800,256]{1,0:T(8,128)(2,1)}, bf16[800,256]{1,0:T(8,128)(2,1)}, u32[]{:S(2)}, u32[]{:S(2)}) %collective-permute-start.33) | collective-permute-done | bytes 409632 | tf_op jit(solution)/shard_map/ppermute | solution.py:365
  407.1 7.5 %project_out.2 = (f32[2,2,256,640]{3,2,1,0:T(8,128)S(1)}, bf16[2,2,256,640]{3,2,1,0:T(8,128)(2,1)S(1)}) custom-call(s32[6]{0:T(128)S(1)} %stack.50.places, bf16[800,256]{1,0:T(8,128)(2,1)S(1)} %copy-done.7, bf16[640,768]{1,0:T(8,128)(2,1)S(1)} %copy-done.1, bf16[640,768]{1,0:T(8,128)(2,1)} %collective-permute-done.26.refs_1_, ...), custom_call_target="tpu_custom_call" | custom-call | flops 2013265920 | bytes 7864320 | tf_op jit(solution)/shard_map/project_out/pallas_call | solution.py:335
  419.4 2.1 merge_partials.23.own
  424.5 7.6 %project_out.3 = (f32[2,2,256,640]{3,2,1,0:T(8,128)S(1)}, bf16[2,2,256,640]{3,2,1,0:T(8,128)(2,1)S(1)}) custom-call(s32[6]{0:T(128)S(1)} %stack.50.places, bf16[800,256]{1,0:T(8,128)(2,1)S(1)} %copy-done.6, bf16[640,768]{1,0:T(8,128)(2,1)S(1)} %copy-done.1, bf16[640,768]{1,0:T(8,128)(2,1)} %collective-permute-done.26.refs_1_, ...), custom_call_target="tpu_custom_call" | custom-call | flops 2013265920 | bytes 7864320 | tf_op jit(solution)/shard_map/project_out/pallas_call | solution.py:335
  437.6 15.1 %collective-permute-done.40 = bf16[2,256,640]{2,1,0:T(8,128)(2,1)S(1)} collective-permute-done((bf16[2,256,640]{2,1,0:T(8,128)(2,1)S(1)}, bf16[2,256,640]{2,1,0:T(8,128)(2,1)S(1)}, u32[]{:S(2)}, u32[]{:S(2)}) %collective-permute-start.40) | collective-permute-done | bytes 655392 | tf_op jit(solution)/shard_map/ppermute | solution.py:658
  453.0 13.3 %collective-permute-done.50 = bf16[2,256,640]{2,1,0:T(8,128)(2,1)S(1)} collective-permute-done((bf16[2,256,640]{2,1,0:T(8,128)(2,1)S(1)}, bf16[2,256,640]{2,1,0:T(8,128)(2,1)S(1)}, u32[]{:S(2)}, u32[]{:S(2)}) %collective-permute-start.50) | collective-permute-done | bytes 655392 | tf_op jit(solution)/shard_map/ppermute | solution.py:658
  (251 shorter events, 94.1 us)
Async XLA Ops:
  0.6 53.7 %collective-permute-start = (bf16[640,768]{1,0:T(8,128)(2,1)}, bf16[640,768]{1,0:T(8,128)(2,1)}, u32[]{:S(2)}, u32[]{:S(2)}) collective-permute-start(bf16[640,768]{1,0:T(8,128)(2,1)} %param.18), channel_id=1, source_target_pairs={{0,4},{4,0},{8,12},{12,8},{16,20},{20,16},{24,28},{28,24},{1,5},{5... | collective-permute-start | bytes 2949128 | tf_op jit(solution)/shard_map/ppermute | solution.py:365
  7.8 31.6 %collective-permute-start.3 = (bf16[512,640]{1,0:T(8,128)(2,1)}, bf16[512,640]{1,0:T(8,128)(2,1)S(1)}, u32[]{:S(2)}, u32[]{:S(2)}) collective-permute-start(bf16[512,640]{1,0:T(8,128)(2,1)} %bitcast.18), channel_id=1, source_target_pairs={{0,16},{4,20},{8,24},{12,28},{16,0},{20,4},{24,8},{28,12},{1,17},{... | collective-permute-start | bytes 1966088 | tf_op jit(solution)/shard_map/ppermute | solution.py:365
  11.6 39.8 %collective-permute-start.8 = (f32[8,64]{1,0:T(8,128)S(1)}, f32[8,64]{1,0:T(8,128)S(1)}, u32[]{:S(2)}, u32[]{:S(2)}) collective-permute-start(f32[8,64]{1,0:T(8,128)S(1)} %rsqrt.16), channel_id=1, source_target_pairs={{0,16},{4,20},{8,24},{12,28},{16,0},{20,4},{24,8},{28,12},{1,17},{... | collective-permute-start | bytes 6152 | tf_op jit(solution)/shard_map/ppermute | solution.py:365
  11.9 39.5 %collective-permute-start.1 = (bf16[640,768]{1,0:T(8,128)(2,1)}, bf16[640,768]{1,0:T(8,128)(2,1)}, u32[]{:S(2)}, u32[]{:S(2)}) collective-permute-start(bf16[640,768]{1,0:T(8,128)(2,1)} %param.18), channel_id=1, source_target_pairs={{0,8},{4,12},{8,0},{12,4},{16,24},{20,28},{24,16},{28,20},{1,9},{5... | collective-permute-start | bytes 2949128 | tf_op jit(solution)/shard_map/ppermute | solution.py:365
  13.5 33.3 %collective-permute-start.4 = (bf16[640,768]{1,0:T(8,128)(2,1)}, bf16[640,768]{1,0:T(8,128)(2,1)}, u32[]{:S(2)}, u32[]{:S(2)}) collective-permute-start(bf16[640,768]{1,0:T(8,128)(2,1)} %param.19), channel_id=1, source_target_pairs={{0,4},{4,0},{8,12},{12,8},{16,20},{20,16},{24,28},{28,24},{1,5},{5... | collective-permute-start | bytes 2949128 | tf_op jit(solution)/shard_map/ppermute | solution.py:365
  39.3 31.7 %collective-permute-start.10 = (bf16[640,768]{1,0:T(8,128)(2,1)}, bf16[640,768]{1,0:T(8,128)(2,1)}, u32[]{:S(2)}, u32[]{:S(2)}) collective-permute-start(bf16[640,768]{1,0:T(8,128)(2,1)} %param.19), channel_id=1, source_target_pairs={{0,8},{4,12},{8,0},{12,4},{16,24},{20,28},{24,16},{28,20},{1,9},{5... | collective-permute-start | bytes 2949128 | tf_op jit(solution)/shard_map/ppermute | solution.py:365
  46.8 16.0 %collective-permute-start.6 = (bf16[512,640]{1,0:T(8,128)(2,1)S(1)}, bf16[512,640]{1,0:T(8,128)(2,1)}, u32[]{:S(2)}, u32[]{:S(2)}) collective-permute-start(bf16[512,640]{1,0:T(8,128)(2,1)S(1)} %collective-permute-done.3), channel_id=1, source_target_pairs={{0,2},{1,3},{2,0},{3,1},{4,6},{5,7},{6,4},{7,5},{8,10},{9,11},{10,... | collective-permute-start | bytes 1966088 | tf_op jit(solution)/shard_map/ppermute | solution.py:365
  51.4 19.8 %collective-permute-start.5 = (bf16[512,640]{1,0:T(8,128)(2,1)S(1)}, bf16[512,640]{1,0:T(8,128)(2,1)}, u32[]{:S(2)}, u32[]{:S(2)}) collective-permute-start(bf16[512,640]{1,0:T(8,128)(2,1)S(1)} %collective-permute-done.3), channel_id=1, source_target_pairs={{0,1},{1,0},{2,3},{3,2},{4,5},{5,4},{6,7},{7,6},{8,9},{9,8},{10,11... | collective-permute-start | bytes 1966088 | tf_op jit(solution)/shard_map/ppermute | solution.py:365
  51.4 24.9 %collective-permute-start.2 = (bf16[640,768]{1,0:T(8,128)(2,1)}, bf16[640,768]{1,0:T(8,128)(2,1)}, u32[]{:S(2)}, u32[]{:S(2)}) collective-permute-start(bf16[640,768]{1,0:T(8,128)(2,1)} %collective-permute-done.1), channel_id=1, source_target_pairs={{0,4},{4,0},{8,12},{12,8},{16,20},{20,16},{24,28},{28,24},{1,5},{5... | collective-permute-start | bytes 2949128 | tf_op jit(solution)/shard_map/ppermute | solution.py:365
  54.3 41.1 %collective-permute-start.12 = (bf16[640,768]{1,0:T(8,128)(2,1)}, bf16[640,768]{1,0:T(8,128)(2,1)}, u32[]{:S(2)}, u32[]{:S(2)}) collective-permute-start(bf16[640,768]{1,0:T(8,128)(2,1)} %param.20), channel_id=1, source_target_pairs={{0,8},{4,12},{8,0},{12,4},{16,24},{20,28},{24,16},{28,20},{1,9},{5... | collective-permute-start | bytes 2949128 | tf_op jit(solution)/shard_map/ppermute | solution.py:365
  62.8 16.3 %collective-permute-start.7 = (bf16[512,640]{1,0:T(8,128)(2,1)}, bf16[512,640]{1,0:T(8,128)(2,1)S(1)}, u32[]{:S(2)}, u32[]{:S(2)}) collective-permute-start(bf16[512,640]{1,0:T(8,128)(2,1)} %collective-permute-done.6), channel_id=1, source_target_pairs={{0,1},{1,0},{2,3},{3,2},{4,5},{5,4},{6,7},{7,6},{8,9},{9,8},{10,11... | collective-permute-start | bytes 1966088 | tf_op jit(solution)/shard_map/ppermute | solution.py:365
  71.0 28.3 %collective-permute-start.11 = (bf16[640,768]{1,0:T(8,128)(2,1)}, bf16[640,768]{1,0:T(8,128)(2,1)S(1)}, u32[]{:S(2)}, u32[]{:S(2)}) collective-permute-start(bf16[640,768]{1,0:T(8,128)(2,1)} %collective-permute-done.10), channel_id=1, source_target_pairs={{0,4},{4,0},{8,12},{12,8},{16,20},{20,16},{24,28},{28,24},{1,5},{5... | collective-permute-start | bytes 2949128 | tf_op jit(solution)/shard_map/ppermute | solution.py:365
  76.4 42.0 %collective-permute-start.13 = (bf16[640,768]{1,0:T(8,128)(2,1)S(1)}, bf16[640,768]{1,0:T(8,128)(2,1)S(1)}, u32[]{:S(2)}, u32[]{:S(2)}) collective-permute-start(bf16[640,768]{1,0:T(8,128)(2,1)S(1)} %copy-done.28), channel_id=1, source_target_pairs={{0,4},{4,0},{8,12},{12,8},{16,20},{20,16},{24,28},{28,24},{1,5},{5... | collective-permute-start | bytes 2949128 | tf_op jit(solution)/shard_map/ppermute | solution.py:365
  81.6 36.8 %collective-permute-start.9 = (bf16[512,768]{1,0:T(8,128)(2,1)S(1)}, bf16[512,768]{1,0:T(8,128)(2,1)S(1)}, u32[]{:S(2)}, u32[]{:S(2)}) collective-permute-start(bf16[512,768]{1,0:T(8,128)(2,1)S(1)} %convolution_convert_fusion.2), channel_id=1, source_target_pairs={{0,16},{4,20},{8,24},{12,28},{16,0},{20,4},{24,8},{28,12},{1,17},{... | collective-permute-start | bytes 2359304 | tf_op jit(solution)/shard_map/ppermute | solution.py:365
  95.5 44.1 %collective-permute-start.18 = (bf16[640,768]{1,0:T(8,128)(2,1)}, bf16[640,768]{1,0:T(8,128)(2,1)}, u32[]{:S(2)}, u32[]{:S(2)}) collective-permute-start(bf16[640,768]{1,0:T(8,128)(2,1)} %collective-permute-done.12), channel_id=1, source_target_pairs={{0,4},{4,0},{8,12},{12,8},{16,20},{20,16},{24,28},{28,24},{1,5},{5... | collective-permute-start | bytes 2949128 | tf_op jit(solution)/shard_map/ppermute | solution.py:365
  124.1 36.7 %collective-permute-start.17 = (bf16[8,64,768]{2,1,0:T(8,128)(2,1)}, bf16[8,64,768]{2,1,0:T(8,128)(2,1)S(1)}, u32[]{:S(2)}, u32[]{:S(2)}) collective-permute-start(bf16[8,64,768]{2,1,0:T(8,128)(2,1)} %bitcast.92), channel_id=1, source_target_pairs={{0,16},{4,20},{8,24},{12,28},{16,0},{20,4},{24,8},{28,12},{1,17},{... | collective-permute-start | bytes 2359304 | tf_op jit(solution)/shard_map/ppermute | solution.py:365
  126.6 34.3 %collective-permute-start.15 = (bf16[8,64,768]{2,1,0:T(8,128)(2,1)}, bf16[8,64,768]{2,1,0:T(8,128)(2,1)S(1)}, u32[]{:S(2)}, u32[]{:S(2)}) collective-permute-start(bf16[8,64,768]{2,1,0:T(8,128)(2,1)} %bitcast.93), channel_id=1, source_target_pairs={{0,8},{4,12},{8,0},{12,4},{16,24},{20,28},{24,16},{28,20},{1,9},{5... | collective-permute-start | bytes 2359304 | tf_op jit(solution)/shard_map/ppermute | solution.py:365
  128.2 32.7 %collective-permute-start.14 = (bf16[8,64,768]{2,1,0:T(8,128)(2,1)}, bf16[8,64,768]{2,1,0:T(8,128)(2,1)S(1)}, u32[]{:S(2)}, u32[]{:S(2)}) collective-permute-start(bf16[8,64,768]{2,1,0:T(8,128)(2,1)} %bitcast.94), channel_id=1, source_target_pairs={{0,4},{4,0},{8,12},{12,8},{16,20},{20,16},{24,28},{28,24},{1,5},{5... | collective-permute-start | bytes 2359304 | tf_op jit(solution)/shard_map/ppermute | solution.py:365
  161.0 31.6 %collective-permute-start.20 = (bf16[8,64,768]{2,1,0:T(8,128)(2,1)S(1)}, bf16[8,64,768]{2,1,0:T(8,128)(2,1)S(1)}, u32[]{:S(2)}, u32[]{:S(2)}) collective-permute-start(bf16[8,64,768]{2,1,0:T(8,128)(2,1)S(1)} %collective-permute-done.17.refs_4_), channel_id=1, source_target_pairs={{0,8},{4,12},{8,0},{12,4},{16,24},{20,28},{24,16},{28,20},{1,9},{5... | collective-permute-start | bytes 2359304 | tf_op jit(solution)/shard_map/ppermute | solution.py:365
  165.6 55.4 %collective-permute-start.22 = (bf16[640,768]{1,0:T(8,128)(2,1)S(1)}, bf16[640,768]{1,0:T(8,128)(2,1)S(1)}, u32[]{:S(2)}, u32[]{:S(2)}) collective-permute-start(bf16[640,768]{1,0:T(8,128)(2,1)S(1)} %copy-done.1), channel_id=1, source_target_pairs={{0,16},{4,20},{8,24},{12,28},{16,0},{20,4},{24,8},{28,12},{1,17},{... | collective-permute-start | bytes 2949128 | tf_op jit(solution)/shard_map/ppermute | solution.py:365
  168.1 37.4 %collective-permute-start.19 = (bf16[8,64,768]{2,1,0:T(8,128)(2,1)S(1)}, bf16[8,64,768]{2,1,0:T(8,128)(2,1)S(1)}, u32[]{:S(2)}, u32[]{:S(2)}) collective-permute-start(bf16[8,64,768]{2,1,0:T(8,128)(2,1)S(1)} %collective-permute-done.17.refs_4_), channel_id=1, source_target_pairs={{0,4},{4,0},{8,12},{12,8},{16,20},{20,16},{24,28},{28,24},{1,5},{5... | collective-permute-start | bytes 2359304 | tf_op jit(solution)/shard_map/ppermute | solution.py:365
  169.6 35.8 %collective-permute-start.16 = (bf16[8,64,768]{2,1,0:T(8,128)(2,1)S(1)}, bf16[8,64,768]{2,1,0:T(8,128)(2,1)S(1)}, u32[]{:S(2)}, u32[]{:S(2)}) collective-permute-start(bf16[8,64,768]{2,1,0:T(8,128)(2,1)S(1)} %collective-permute-done.15.refs_2_), channel_id=1, source_target_pairs={{0,4},{4,0},{8,12},{12,8},{16,20},{20,16},{24,28},{28,24},{1,5},{5... | collective-permute-start | bytes 2359304 | tf_op jit(solution)/shard_map/ppermute | solution.py:365
  192.5 28.2 %collective-permute-start.21 = (bf16[8,64,768]{2,1,0:T(8,128)(2,1)S(1)}, bf16[8,64,768]{2,1,0:T(8,128)(2,1)S(1)}, u32[]{:S(2)}, u32[]{:S(2)}) collective-permute-start(bf16[8,64,768]{2,1,0:T(8,128)(2,1)S(1)} %collective-permute-done.20.refs_6_), channel_id=1, source_target_pairs={{0,4},{4,0},{8,12},{12,8},{16,20},{20,16},{24,28},{28,24},{1,5},{5... | collective-permute-start | bytes 2359304 | tf_op jit(solution)/shard_map/ppermute | solution.py:365
  220.7 51.4 %collective-permute-start.25 = (bf16[640,768]{1,0:T(8,128)(2,1)S(1)}, bf16[640,768]{1,0:T(8,128)(2,1)S(1)}, u32[]{:S(2)}, u32[]{:S(2)}) collective-permute-start(bf16[640,768]{1,0:T(8,128)(2,1)S(1)} %copy-done.1), channel_id=1, source_target_pairs={{0,8},{4,12},{8,0},{12,4},{16,24},{20,28},{24,16},{28,20},{1,9},{5... | collective-permute-start | bytes 2949128 | tf_op jit(solution)/shard_map/ppermute | solution.py:365
  221.0 51.1 %collective-permute-start.28 = (bf16[640,768]{1,0:T(8,128)(2,1)S(1)}, bf16[640,768]{1,0:T(8,128)(2,1)}, u32[]{:S(2)}, u32[]{:S(2)}) collective-permute-start(bf16[640,768]{1,0:T(8,128)(2,1)S(1)} %collective-permute-done.22.refs_4_), channel_id=1, source_target_pairs={{0,4},{4,0},{8,12},{12,8},{16,20},{20,16},{24,28},{28,24},{1,5},{5... | collective-permute-start | bytes 2949128 | tf_op jit(solution)/shard_map/ppermute | solution.py:365
  223.8 55.4 %collective-permute-start.23 = (bf16[512,768]{1,0:T(8,128)(2,1)S(1)}, bf16[512,768]{1,0:T(8,128)(2,1)}, u32[]{:S(2)}, u32[]{:S(2)}) collective-permute-start(bf16[512,768]{1,0:T(8,128)(2,1)S(1)} %convolution_convert_fusion.1), channel_id=1, source_target_pairs={{0,16},{4,20},{8,24},{12,28},{16,0},{20,4},{24,8},{28,12},{1,17},{... | collective-permute-start | bytes 2359304 | tf_op jit(solution)/shard_map/ppermute | solution.py:365
  227.4 66.0 %collective-permute-start.24 = (bf16[512,768]{1,0:T(8,128)(2,1)}, bf16[512,768]{1,0:T(8,128)(2,1)}, u32[]{:S(2)}, u32[]{:S(2)}) collective-permute-start(bf16[512,768]{1,0:T(8,128)(2,1)} %convolution_convert_fusion), channel_id=1, source_target_pairs={{0,16},{4,20},{8,24},{12,28},{16,0},{20,4},{24,8},{28,12},{1,17},{... | collective-permute-start | bytes 2359304 | tf_op jit(solution)/shard_map/ppermute | solution.py:365
  230.2 68.4 %collective-permute-start.26 = (bf16[640,768]{1,0:T(8,128)(2,1)S(1)}, bf16[640,768]{1,0:T(8,128)(2,1)}, u32[]{:S(2)}, u32[]{:S(2)}) collective-permute-start(bf16[640,768]{1,0:T(8,128)(2,1)S(1)} %copy-done.1), channel_id=1, source_target_pairs={{0,4},{4,0},{8,12},{12,8},{16,20},{20,16},{24,28},{28,24},{1,5},{5... | collective-permute-start | bytes 2949128 | tf_op jit(solution)/shard_map/ppermute | solution.py:365
  272.1 40.6 %collective-permute-start.27 = (bf16[640,768]{1,0:T(8,128)(2,1)S(1)}, bf16[640,768]{1,0:T(8,128)(2,1)}, u32[]{:S(2)}, u32[]{:S(2)}) collective-permute-start(bf16[640,768]{1,0:T(8,128)(2,1)S(1)} %collective-permute-done.22.refs_4_), channel_id=1, source_target_pairs={{0,8},{4,12},{8,0},{12,4},{16,24},{20,28},{24,16},{28,20},{1,9},{5... | collective-permute-start | bytes 2949128 | tf_op jit(solution)/shard_map/ppermute | solution.py:365
  272.1 69.0 %collective-permute-start.29 = (bf16[640,768]{1,0:T(8,128)(2,1)S(1)}, bf16[640,768]{1,0:T(8,128)(2,1)}, u32[]{:S(2)}, u32[]{:S(2)}) collective-permute-start(bf16[640,768]{1,0:T(8,128)(2,1)S(1)} %collective-permute-done.25.refs_2_), channel_id=1, source_target_pairs={{0,4},{4,0},{8,12},{12,8},{16,20},{20,16},{24,28},{28,24},{1,5},{5... | collective-permute-start | bytes 2949128 | tf_op jit(solution)/shard_map/ppermute | solution.py:365
  279.2 62.0 %collective-permute-start.30 = (bf16[640,768]{1,0:T(8,128)(2,1)}, bf16[640,768]{1,0:T(8,128)(2,1)}, u32[]{:S(2)}, u32[]{:S(2)}) collective-permute-start(bf16[640,768]{1,0:T(8,128)(2,1)} %collective-permute-done.28.refs_5_), channel_id=1, source_target_pairs={{0,8},{4,12},{8,0},{12,4},{16,24},{20,28},{24,16},{28,20},{1,9},{5... | collective-permute-start | bytes 2949128 | tf_op jit(solution)/shard_map/ppermute | solution.py:365
  341.2 16.6 %collective-permute-start.32 = (bf16[800,256]{1,0:T(8,128)(2,1)}, bf16[800,256]{1,0:T(8,128)(2,1)S(1)}, u32[]{:S(2)}, u32[]{:S(2)}) collective-permute-start(bf16[800,256]{1,0:T(8,128)(2,1)} %get-tuple-element.103), channel_id=1, source_target_pairs={{0,4},{4,0},{8,12},{12,8},{16,20},{20,16},{24,28},{28,24},{1,5},{5... | collective-permute-start | bytes 1228808 | tf_op jit(solution)/shard_map/ppermute | solution.py:365
  341.2 21.2 %collective-permute-start.45 = (bf16[800,256]{1,0:T(8,128)(2,1)}, bf16[800,256]{1,0:T(8,128)(2,1)}, u32[]{:S(2)}, u32[]{:S(2)}) collective-permute-start(bf16[800,256]{1,0:T(8,128)(2,1)} %get-tuple-element.117), channel_id=1, source_target_pairs={{0,8},{4,12},{8,0},{12,4},{16,24},{20,28},{24,16},{28,20},{1,9},{5... | collective-permute-start | bytes 1228808 | tf_op jit(solution)/shard_map/ppermute | solution.py:365
  343.2 32.4 %collective-permute-start.34 = (bf16[800,256]{1,0:T(8,128)(2,1)}, bf16[800,256]{1,0:T(8,128)(2,1)}, u32[]{:S(2)}, u32[]{:S(2)}) collective-permute-start(bf16[800,256]{1,0:T(8,128)(2,1)} %get-tuple-element.105), channel_id=1, source_target_pairs={{0,8},{4,12},{8,0},{12,4},{16,24},{20,28},{24,16},{28,20},{1,9},{5... | collective-permute-start | bytes 1228808 | tf_op jit(solution)/shard_map/ppermute | solution.py:365
  355.7 21.9 %collective-permute-start.36 = (bf16[800,256]{1,0:T(8,128)(2,1)}, bf16[800,256]{1,0:T(8,128)(2,1)}, u32[]{:S(2)}, u32[]{:S(2)}) collective-permute-start(bf16[800,256]{1,0:T(8,128)(2,1)} %merge_partials.18), channel_id=1, source_target_pairs={{0,4},{4,0},{8,12},{12,8},{16,20},{20,16},{24,28},{28,24},{1,5},{5... | collective-permute-start | bytes 1228808 | tf_op jit(solution)/shard_map/ppermute | solution.py:365
  355.7 24.0 %collective-permute-start.31 = (bf16[800,256]{1,0:T(8,128)(2,1)}, bf16[800,256]{1,0:T(8,128)(2,1)}, u32[]{:S(2)}, u32[]{:S(2)}) collective-permute-start(bf16[800,256]{1,0:T(8,128)(2,1)} %copy-done.20), channel_id=1, source_target_pairs={{0,4},{4,0},{8,12},{12,8},{16,20},{20,16},{24,28},{28,24},{1,5},{5... | collective-permute-start | bytes 1228808 | tf_op jit(solution)/shard_map/ppermute | solution.py:365
  357.8 26.8 %collective-permute-start.42 = (bf16[800,256]{1,0:T(8,128)(2,1)}, bf16[800,256]{1,0:T(8,128)(2,1)}, u32[]{:S(2)}, u32[]{:S(2)}) collective-permute-start(bf16[800,256]{1,0:T(8,128)(2,1)} %copy-done.19), channel_id=1, source_target_pairs={{0,4},{4,0},{8,12},{12,8},{16,20},{20,16},{24,28},{28,24},{1,5},{5... | collective-permute-start | bytes 1228808 | tf_op jit(solution)/shard_map/ppermute | solution.py:365
  362.4 27.0 %collective-permute-start.44 = (bf16[800,256]{1,0:T(8,128)(2,1)}, bf16[800,256]{1,0:T(8,128)(2,1)}, u32[]{:S(2)}, u32[]{:S(2)}) collective-permute-start(bf16[800,256]{1,0:T(8,128)(2,1)} %copy-done.18), channel_id=1, source_target_pairs={{0,8},{4,12},{8,0},{12,4},{16,24},{20,28},{24,16},{28,20},{1,9},{5... | collective-permute-start | bytes 1228808 | tf_op jit(solution)/shard_map/ppermute | solution.py:365
  375.6 15.9 %collective-permute-start.46 = (bf16[800,256]{1,0:T(8,128)(2,1)}, bf16[800,256]{1,0:T(8,128)(2,1)}, u32[]{:S(2)}, u32[]{:S(2)}) collective-permute-start(bf16[800,256]{1,0:T(8,128)(2,1)} %merge_partials.25), channel_id=1, source_target_pairs={{0,4},{4,0},{8,12},{12,8},{16,20},{20,16},{24,28},{28,24},{1,5},{5... | collective-permute-start | bytes 1228808 | tf_op jit(solution)/shard_map/ppermute | solution.py:365
  377.7 24.4 %collective-permute-start.33 = (bf16[800,256]{1,0:T(8,128)(2,1)}, bf16[800,256]{1,0:T(8,128)(2,1)}, u32[]{:S(2)}, u32[]{:S(2)}) collective-permute-start(bf16[800,256]{1,0:T(8,128)(2,1)} %merge_partials.15), channel_id=1, source_target_pairs={{0,8},{4,12},{8,0},{12,4},{16,24},{20,28},{24,16},{28,20},{1,9},{5... | collective-permute-start | bytes 1228808 | tf_op jit(solution)/shard_map/ppermute | solution.py:365
  379.7 24.4 %collective-permute-start.37 = (bf16[800,256]{1,0:T(8,128)(2,1)}, bf16[800,256]{1,0:T(8,128)(2,1)}, u32[]{:S(2)}, u32[]{:S(2)}) collective-permute-start(bf16[800,256]{1,0:T(8,128)(2,1)} %merge_partials.19), channel_id=1, source_target_pairs={{0,16},{4,20},{8,24},{12,28},{16,0},{20,4},{24,8},{28,12},{1,17},{... | collective-permute-start | bytes 1228808 | tf_op jit(solution)/shard_map/ppermute | solution.py:365
  384.6 32.7 %collective-permute-start.41 = (bf16[800,256]{1,0:T(8,128)(2,1)S(1)}, bf16[800,256]{1,0:T(8,128)(2,1)}, u32[]{:S(2)}, u32[]{:S(2)}) collective-permute-start(bf16[800,256]{1,0:T(8,128)(2,1)S(1)} %copy-done.17), channel_id=1, source_target_pairs={{0,4},{4,0},{8,12},{12,8},{16,20},{20,16},{24,28},{28,24},{1,5},{5... | collective-permute-start | bytes 1228808 | tf_op jit(solution)/shard_map/ppermute | solution.py:365
  389.5 29.9 %collective-permute-start.43 = (bf16[800,256]{1,0:T(8,128)(2,1)}, bf16[800,256]{1,0:T(8,128)(2,1)}, u32[]{:S(2)}, u32[]{:S(2)}) collective-permute-start(bf16[800,256]{1,0:T(8,128)(2,1)} %merge_partials.22), channel_id=1, source_target_pairs={{0,8},{4,12},{8,0},{12,4},{16,24},{20,28},{24,16},{28,20},{1,9},{5... | collective-permute-start | bytes 1228808 | tf_op jit(solution)/shard_map/ppermute | solution.py:365
  393.6 27.9 %collective-permute-start.47 = (bf16[800,256]{1,0:T(8,128)(2,1)}, bf16[800,256]{1,0:T(8,128)(2,1)}, u32[]{:S(2)}, u32[]{:S(2)}) collective-permute-start(bf16[800,256]{1,0:T(8,128)(2,1)} %merge_partials.26), channel_id=1, source_target_pairs={{0,16},{4,20},{8,24},{12,28},{16,0},{20,4},{24,8},{28,12},{1,17},{... | collective-permute-start | bytes 1228808 | tf_op jit(solution)/shard_map/ppermute | solution.py:365
  417.3 15.6 %collective-permute-start.39 = (bf16[2,256,640]{2,1,0:T(8,128)(2,1)}, bf16[2,256,640]{2,1,0:T(8,128)(2,1)}, u32[]{:S(2)}, u32[]{:S(2)}) collective-permute-start(bf16[2,256,640]{2,1,0:T(8,128)(2,1)} %get-tuple-element.139), channel_id=1, source_target_pairs={{0,1},{1,0},{2,3},{3,2},{4,5},{5,4},{6,7},{7,6},{8,9},{9,8},{10,11... | collective-permute-start | bytes 1966088 | tf_op jit(solution)/shard_map/ppermute | solution.py:658
  435.1 17.6 %collective-permute-start.40 = (bf16[2,256,640]{2,1,0:T(8,128)(2,1)S(1)}, bf16[2,256,640]{2,1,0:T(8,128)(2,1)S(1)}, u32[]{:S(2)}, u32[]{:S(2)}) collective-permute-start(bf16[2,256,640]{2,1,0:T(8,128)(2,1)S(1)} %fusion.5), channel_id=1, source_target_pairs={{0,2},{1,3},{2,0},{3,1},{4,6},{5,7},{6,4},{7,5},{8,10},{9,11},{10,... | collective-permute-start | bytes 1966088 | tf_op jit(solution)/shard_map/ppermute | solution.py:658
  436.4 16.7 %collective-permute-start.48 = (bf16[2,256,640]{2,1,0:T(8,128)(2,1)S(1)}, bf16[2,256,640]{2,1,0:T(8,128)(2,1)S(1)}, u32[]{:S(2)}, u32[]{:S(2)}) collective-permute-start(bf16[2,256,640]{2,1,0:T(8,128)(2,1)S(1)} %get-tuple-element.140), channel_id=1, source_target_pairs={{0,1},{1,0},{2,3},{3,2},{4,5},{5,4},{6,7},{7,6},{8,9},{9,8},{10,11... | collective-permute-start | bytes 1966088 | tf_op jit(solution)/shard_map/ppermute | solution.py:658
  436.7 29.6 %collective-permute-start.50 = (bf16[2,256,640]{2,1,0:T(8,128)(2,1)S(1)}, bf16[2,256,640]{2,1,0:T(8,128)(2,1)S(1)}, u32[]{:S(2)}, u32[]{:S(2)}) collective-permute-start(bf16[2,256,640]{2,1,0:T(8,128)(2,1)S(1)} %fusion.2), channel_id=1, source_target_pairs={{0,2},{1,3},{2,0},{3,1},{4,6},{5,7},{6,4},{7,5},{8,10},{9,11},{10,... | collective-permute-start | bytes 1966088 | tf_op jit(solution)/shard_map/ppermute | solution.py:658
  (56 other events, 683.4 us)

commit v5 on v4

--- a/solution.py
+++ b/solution.py
@@ -628,7 +628,7 @@
     places = jnp.stack(
         [line ^ head_place for line in lines] + [x_axis.before(x) for x in range(x_size)]
     ).astype(jnp.int32)
-    first_steps = [tree[key] for tree in (own_out, far_out) for key in ((0, 1, 0), (0, 0, 1))]
+    first_steps = (own_out[(0, 1, 0)], own_out[(0, 0, 1)], far_out[(0, 0, 1)])
     pieces_of = block_attention(seq_size, state, new_keys, after(new_values, first_steps))
     pieces_of = after(pieces_of, out_shards)
     results = []

time: 471 us -> 460 us (0.977)
  waiting for transfers between devices: 241 us -> 214 us
  starting transfers between devices: 47.7 us -> 66.3 us
  Pallas kernels: 108 us -> 103 us
    ppermute x45, waiting for transfers between devices: 212 us -> 186 us  [step(): return lax.ppermute(value, self.mesh_axis, pairs)]
    ppermute x45, starting transfers between devices: 44.7 us -> 63.3 us  [step(): return lax.ppermute(value, self.mesh_axis, pairs)]
    pallas_call x1, Pallas kernels: 38.8 us -> 33.2 us  [cached_attention(): pl.pallas_call(functools.partial(cached_kernel, sources), out_shape=[jax....]
  transfers between devices with their start and end apart: 51 -> 51, of which waited for: 24 -> 22; matrix products, arithmetic and copies ran while one was open for 11% -> 11% of each run, Pallas kernels for 23% -> 23%
where the time goes in v5:
time: 460 us; the launch traced here: 454 us
  waiting for transfers between devices  214 us (47%)
  Pallas kernels  103 us (22%)
  starting transfers between devices  66.3 us (14%)
  local copies, waits for them, and re-layouts  37.1 us (8%)
  matrix products  19.7 us (4%)
  other arithmetic  12.5 us (3%)
    ppermute x45, waiting for transfers between devices, step(): return lax.ppermute(value, self.mesh_axis, pairs)  186 us
    ppermute x45, starting transfers between devices, step(): return lax.ppermute(value, self.mesh_axis, pairs)  63.3 us
    pallas_call x1, Pallas kernels, cached_attention(): pl.pallas_call(functools.partial(cached_kernel, sources), out_shape=[jax....  33.2 us
    pallas_call x14, Pallas kernels, merge(): pl.pallas_call(merge_kernel, out_shape=jax.ShapeDtypeStruct(own.shape, ow...  28.8 us
    ppermute x6, waiting for transfers between devices, per_device(): lax.ppermute(value, 'head', pairs).astype(jnp.float32)  28.4 us
    unnamed x115, local copies, waits for them, and re-layouts  27.3 us
    dot_general x6, matrix products, product(): return jnp.dot(left, weight, preferred_element_type=jnp.float32)  19.7 us
    pallas_call x1, Pallas kernels, block_attention(): pl.pallas_call(functools.partial(block_kernel, sources), out_shape=[piece...  19.3 us
  transfers between devices with their start and end apart: 51, of which 22 were waited for; matrix products, arithmetic and copies ran while one was open for 11% of the time, Pallas kernels for 23%

profile of v5, /device:TPU:0, one launch (start us, length us, event | category | flops | bytes accessed | tf_op | source)
XLA Modules:
  0.0 454.0 jit_solution(5601543623453982851)
XLA Ops:
  0.6 3.0 collective-permute-start
  4.3 2.5 dynamic-slice_bitcast_fusion.4
  7.8 2.6 collective-permute-start.3
  16.3 23.0 %collective-permute-done.3 = bf16[512,640]{1,0:T(8,128)(2,1)S(1)} collective-permute-done((bf16[512,640]{1,0:T(8,128)(2,1)}, bf16[512,640]{1,0:T(8,128)(2,1)S(1)}, u32[]{:S(2)}, u32[]{:S(2)}) %collective-permute-start.3) | collective-permute-done | bytes 655392 | tf_op jit(solution)/shard_map/ppermute | solution.py:365
  40.1 6.7 %collective-permute-done.4 = bf16[640,768]{1,0:T(8,128)(2,1)} collective-permute-done((bf16[640,768]{1,0:T(8,128)(2,1)}, bf16[640,768]{1,0:T(8,128)(2,1)}, u32[]{:S(2)}, u32[]{:S(2)}) %collective-permute-start.4) | collective-permute-done | bytes 983072 | tf_op jit(solution)/shard_map/ppermute | solution.py:365
  48.5 2.2 constant_dynamic-update-slice_fusion.3
  55.9 2.2 constant_dynamic-update-slice_fusion.2
  58.1 4.7 %collective-permute-done.6 = bf16[512,640]{1,0:T(8,128)(2,1)} collective-permute-done((bf16[512,640]{1,0:T(8,128)(2,1)S(1)}, bf16[512,640]{1,0:T(8,128)(2,1)}, u32[]{:S(2)}, u32[]{:S(2)}) %collective-permute-start.6) | collective-permute-done | bytes 655392 | tf_op jit(solution)/shard_map/ppermute | solution.py:365
  64.5 6.5 %collective-permute-done.10 = bf16[640,768]{1,0:T(8,128)(2,1)} collective-permute-done((bf16[640,768]{1,0:T(8,128)(2,1)}, bf16[640,768]{1,0:T(8,128)(2,1)}, u32[]{:S(2)}, u32[]{:S(2)}) %collective-permute-start.10) | collective-permute-done | bytes 983072 | tf_op jit(solution)/shard_map/ppermute | solution.py:365
  73.6 2.7 collective-permute-done.2
  79.3 2.3 convolution_convert_fusion.2
  81.6 2.7 collective-permute-start.9
  85.0 10.5 %collective-permute-done.12 = bf16[640,768]{1,0:T(8,128)(2,1)} collective-permute-done((bf16[640,768]{1,0:T(8,128)(2,1)}, bf16[640,768]{1,0:T(8,128)(2,1)}, u32[]{:S(2)}, u32[]{:S(2)}) %collective-permute-start.12) | collective-permute-done | bytes 983072 | tf_op jit(solution)/shard_map/ppermute | solution.py:365
  96.0 3.4 fusion.21.own
  99.4 19.0 %collective-permute-done.13 = bf16[640,768]{1,0:T(8,128)(2,1)S(1)} collective-permute-done((bf16[640,768]{1,0:T(8,128)(2,1)S(1)}, bf16[640,768]{1,0:T(8,128)(2,1)S(1)}, u32[]{:S(2)}, u32[]{:S(2)}) %collective-permute-start.13) | collective-permute-done | bytes 983072 | tf_op jit(solution)/shard_map/ppermute | solution.py:365
  121.0 3.1 rotate_rows.2
  124.1 2.6 collective-permute-start.17
  130.3 9.3 %collective-permute-done.18 = bf16[640,768]{1,0:T(8,128)(2,1)} collective-permute-done((bf16[640,768]{1,0:T(8,128)(2,1)}, bf16[640,768]{1,0:T(8,128)(2,1)}, u32[]{:S(2)}, u32[]{:S(2)}) %collective-permute-start.18) | collective-permute-done | bytes 983072 | tf_op jit(solution)/shard_map/ppermute | solution.py:365
  139.6 21.2 %collective-permute-done.17.refs_4_ = bf16[8,64,768]{2,1,0:T(8,128)(2,1)S(1)} collective-permute-done((bf16[8,64,768]{2,1,0:T(8,128)(2,1)}, bf16[8,64,768]{2,1,0:T(8,128)(2,1)S(1)}, u32[]{:S(2)}, u32[]{:S(2)}) %collective-permute-start.17) | collective-permute-done | bytes 786464 | tf_op jit(solution)/shard_map/ppermute | solution.py:365
  165.6 2.4 collective-permute-start.22
  170.1 22.4 %collective-permute-done.20.refs_6_ = bf16[8,64,768]{2,1,0:T(8,128)(2,1)S(1)} collective-permute-done((bf16[8,64,768]{2,1,0:T(8,128)(2,1)S(1)}, bf16[8,64,768]{2,1,0:T(8,128)(2,1)S(1)}, u32[]{:S(2)}, u32[]{:S(2)}) %collective-permute-start.20) | collective-permute-done | bytes 786464 | tf_op jit(solution)/shard_map/ppermute | solution.py:365
  194.0 2.3 convolution_convert_fusion.1
  197.7 7.8 %collective-permute-done.16.refs_3_ = bf16[8,64,768]{2,1,0:T(8,128)(2,1)S(1)} collective-permute-done((bf16[8,64,768]{2,1,0:T(8,128)(2,1)S(1)}, bf16[8,64,768]{2,1,0:T(8,128)(2,1)S(1)}, u32[]{:S(2)}, u32[]{:S(2)}) %collective-permute-start.16) | collective-permute-done | bytes 786464 | tf_op jit(solution)/shard_map/ppermute | solution.py:365
  205.5 15.3 %collective-permute-done.21.refs_7_ = bf16[8,64,768]{2,1,0:T(8,128)(2,1)S(1)} collective-permute-done((bf16[8,64,768]{2,1,0:T(8,128)(2,1)S(1)}, bf16[8,64,768]{2,1,0:T(8,128)(2,1)S(1)}, u32[]{:S(2)}, u32[]{:S(2)}) %collective-permute-start.21) | collective-permute-done | bytes 786464 | tf_op jit(solution)/shard_map/ppermute | solution.py:365
  224.2 3.2 convolution_convert_fusion
  227.4 2.8 collective-permute-start.24
  230.7 33.2 %cached_attention.1 = (bf16[8,6,128,512]{3,2,1,0:T(8,128)(2,1)S(1)}, f32[8,6,128,512]{3,2,1,0:T(8,128)}, f32[8,8,512]{2,1,0:T(8,128)S(1)}, f32[8,8,512]{2,1,0:T(8,128)S(1)}) custom-call(s32[80]{0:T(128)S(1)} %broadcast_add_fusion.1.order, s32[80]{0:T(128)S(1)} %get-tuple-element.120.counts, s32[9]{0:T(128)S(1)} %select_reduce_fusion.4.starts, ...), custom_call_target="tpu_custom_call" | custom-call | flops 805306368 | bytes 1572864 | tf_op jit(solution)/shard_map/cached_attention/pallas_call | solution.py:162
  264.0 2.6 copy-done
  266.5 2.7 collective-permute-start.29
  270.5 8.6 %collective-permute-done.23.received = bf16[512,768]{1,0:T(8,128)(2,1)} collective-permute-done((bf16[512,768]{1,0:T(8,128)(2,1)S(1)}, bf16[512,768]{1,0:T(8,128)(2,1)}, u32[]{:S(2)}, u32[]{:S(2)}) %collective-permute-start.23) | collective-permute-done | bytes 786464 | tf_op jit(solution)/shard_map/ppermute | solution.py:365
  279.2 3.3 fusion.22.own
  282.5 3.1 rotate_rows.3
  285.6 7.7 %collective-permute-done.24 = bf16[512,768]{1,0:T(8,128)(2,1)} collective-permute-done((bf16[512,768]{1,0:T(8,128)(2,1)}, bf16[512,768]{1,0:T(8,128)(2,1)}, u32[]{:S(2)}, u32[]{:S(2)}) %collective-permute-start.24) | collective-permute-done | bytes 786464 | tf_op jit(solution)/shard_map/ppermute | solution.py:365
  293.3 5.3 %add_convert_fusion = bf16[512,768]{1,0:T(8,128)(2,1)S(1)} fusion(bf16[512,768]{1,0:T(8,128)(2,1)} %collective-permute-done.24, bf16[512,2560]{1,0:T(8,128)(2,1)} %copy-done.25, bf16[2560,768]{1,0:T(8,128)(2,1)} %copy-done.40), kind=kOutput, calls=%fused_computation.7 | convolution fusion | flops 2014445568 | bytes 8126464 | tf_op jit(solution)/shard_map/dot_general | solution.py:529
  298.6 19.3 %block_attention.1 = (bf16[800,256]{1,0:T(8,128)(2,1)S(1)}, bf16[800,256]{1,0:T(8,128)(2,1)S(1)}, bf16[800,256]{1,0:T(8,128)(2,1)S(1)}, bf16[800,256]{1,0:T(8,12...) custom-call(bf16[8,6,128,512]{3,2,1,0:T(8,128)(2,1)} %copy-done, ...), custom_call_target="tpu_custom_call" | custom-call | flops 201326592 | bytes 3145728 | tf_op jit(solution)/shard_map/block_attention/pallas_call | solution.py:256
  327.1 2.3 collective-permute-start.32
  331.5 8.2 %collective-permute-done.35.other = bf16[800,256]{1,0:T(8,128)(2,1)} collective-permute-done((bf16[800,256]{1,0:T(8,128)(2,1)S(1)}, bf16[800,256]{1,0:T(8,128)(2,1)}, u32[]{:S(2)}, u32[]{:S(2)}) %collective-permute-start.35) | collective-permute-done | bytes 409632 | tf_op jit(solution)/shard_map/ppermute | solution.py:365
  341.7 2.3 collective-permute-start.36
  348.4 2.1 merge_partials.25
  350.5 6.7 %collective-permute-done.34.other = bf16[800,256]{1,0:T(8,128)(2,1)} collective-permute-done((bf16[800,256]{1,0:T(8,128)(2,1)}, bf16[800,256]{1,0:T(8,128)(2,1)}, u32[]{:S(2)}, u32[]{:S(2)}) %collective-permute-start.34) | collective-permute-done | bytes 409632 | tf_op jit(solution)/shard_map/ppermute | solution.py:365
  357.2 2.3 collective-permute-start.46
  363.6 7.5 %collective-permute-start.37 = (bf16[800,256]{1,0:T(8,128)(2,1)}, bf16[800,256]{1,0:T(8,128)(2,1)}, u32[]{:S(2)}, u32[]{:S(2)}) collective-permute-start(bf16[800,256]{1,0:T(8,128)(2,1)} %merge_partials.19), channel_id=1, source_target_pairs={{0,16},{4,20},{8,24},{12,28},{16,0},{20,4},{24,8},{28,12},{1,17},{... | collective-permute-start | bytes 1228808 | tf_op jit(solution)/shard_map/ppermute | solution.py:365
  375.2 2.1 merge_partials.22
  383.0 4.0 collective-permute-done.33.other
  392.8 7.5 %project_out.2 = (f32[2,2,256,640]{3,2,1,0:T(8,128)S(1)}, bf16[2,2,256,640]{3,2,1,0:T(8,128)(2,1)S(1)}) custom-call(s32[6]{0:T(128)S(1)} %stack.50.places, bf16[800,256]{1,0:T(8,128)(2,1)S(1)} %copy-done.7, bf16[640,768]{1,0:T(8,128)(2,1)S(1)} %copy-done.1, bf16[640,768]{1,0:T(8,128)(2,1)} %collective-permute-done.26.refs_1_, ...), custom_call_target="tpu_custom_call" | custom-call | flops 2013265920 | bytes 7864320 | tf_op jit(solution)/shard_map/project_out/pallas_call | solution.py:335
  410.2 7.6 %project_out.3 = (f32[2,2,256,640]{3,2,1,0:T(8,128)S(1)}, bf16[2,2,256,640]{3,2,1,0:T(8,128)(2,1)S(1)}) custom-call(s32[6]{0:T(128)S(1)} %stack.50.places, bf16[800,256]{1,0:T(8,128)(2,1)S(1)} %copy-done.6, bf16[640,768]{1,0:T(8,128)(2,1)S(1)} %copy-done.1, bf16[640,768]{1,0:T(8,128)(2,1)} %collective-permute-done.26.refs_1_, ...), custom_call_target="tpu_custom_call" | custom-call | flops 2013265920 | bytes 7864320 | tf_op jit(solution)/shard_map/project_out/pallas_call | solution.py:335
  423.3 15.1 %collective-permute-done.40 = bf16[2,256,640]{2,1,0:T(8,128)(2,1)S(1)} collective-permute-done((bf16[2,256,640]{2,1,0:T(8,128)(2,1)S(1)}, bf16[2,256,640]{2,1,0:T(8,128)(2,1)S(1)}, u32[]{:S(2)}, u32[]{:S(2)}) %collective-permute-start.40) | collective-permute-done | bytes 655392 | tf_op jit(solution)/shard_map/ppermute | solution.py:658
  438.7 13.3 %collective-permute-done.50 = bf16[2,256,640]{2,1,0:T(8,128)(2,1)S(1)} collective-permute-done((bf16[2,256,640]{2,1,0:T(8,128)(2,1)S(1)}, bf16[2,256,640]{2,1,0:T(8,128)(2,1)S(1)}, u32[]{:S(2)}, u32[]{:S(2)}) %collective-permute-start.50) | collective-permute-done | bytes 655392 | tf_op jit(solution)/shard_map/ppermute | solution.py:658
  (251 shorter events, 99.3 us)
Async XLA Ops:
  0.6 53.7 %collective-permute-start = (bf16[640,768]{1,0:T(8,128)(2,1)}, bf16[640,768]{1,0:T(8,128)(2,1)}, u32[]{:S(2)}, u32[]{:S(2)}) collective-permute-start(bf16[640,768]{1,0:T(8,128)(2,1)} %param.18), channel_id=1, source_target_pairs={{0,4},{4,0},{8,12},{12,8},{16,20},{20,16},{24,28},{28,24},{1,5},{5... | collective-permute-start | bytes 2949128 | tf_op jit(solution)/shard_map/ppermute | solution.py:365
  7.8 31.6 %collective-permute-start.3 = (bf16[512,640]{1,0:T(8,128)(2,1)}, bf16[512,640]{1,0:T(8,128)(2,1)S(1)}, u32[]{:S(2)}, u32[]{:S(2)}) collective-permute-start(bf16[512,640]{1,0:T(8,128)(2,1)} %bitcast.18), channel_id=1, source_target_pairs={{0,16},{4,20},{8,24},{12,28},{16,0},{20,4},{24,8},{28,12},{1,17},{... | collective-permute-start | bytes 1966088 | tf_op jit(solution)/shard_map/ppermute | solution.py:365
  11.6 39.8 %collective-permute-start.8 = (f32[8,64]{1,0:T(8,128)S(1)}, f32[8,64]{1,0:T(8,128)S(1)}, u32[]{:S(2)}, u32[]{:S(2)}) collective-permute-start(f32[8,64]{1,0:T(8,128)S(1)} %rsqrt.16), channel_id=1, source_target_pairs={{0,16},{4,20},{8,24},{12,28},{16,0},{20,4},{24,8},{28,12},{1,17},{... | collective-permute-start | bytes 6152 | tf_op jit(solution)/shard_map/ppermute | solution.py:365
  11.9 39.5 %collective-permute-start.1 = (bf16[640,768]{1,0:T(8,128)(2,1)}, bf16[640,768]{1,0:T(8,128)(2,1)}, u32[]{:S(2)}, u32[]{:S(2)}) collective-permute-start(bf16[640,768]{1,0:T(8,128)(2,1)} %param.18), channel_id=1, source_target_pairs={{0,8},{4,12},{8,0},{12,4},{16,24},{20,28},{24,16},{28,20},{1,9},{5... | collective-permute-start | bytes 2949128 | tf_op jit(solution)/shard_map/ppermute | solution.py:365
  13.5 33.3 %collective-permute-start.4 = (bf16[640,768]{1,0:T(8,128)(2,1)}, bf16[640,768]{1,0:T(8,128)(2,1)}, u32[]{:S(2)}, u32[]{:S(2)}) collective-permute-start(bf16[640,768]{1,0:T(8,128)(2,1)} %param.19), channel_id=1, source_target_pairs={{0,4},{4,0},{8,12},{12,8},{16,20},{20,16},{24,28},{28,24},{1,5},{5... | collective-permute-start | bytes 2949128 | tf_op jit(solution)/shard_map/ppermute | solution.py:365
  39.3 31.7 %collective-permute-start.10 = (bf16[640,768]{1,0:T(8,128)(2,1)}, bf16[640,768]{1,0:T(8,128)(2,1)}, u32[]{:S(2)}, u32[]{:S(2)}) collective-permute-start(bf16[640,768]{1,0:T(8,128)(2,1)} %param.19), channel_id=1, source_target_pairs={{0,8},{4,12},{8,0},{12,4},{16,24},{20,28},{24,16},{28,20},{1,9},{5... | collective-permute-start | bytes 2949128 | tf_op jit(solution)/shard_map/ppermute | solution.py:365
  46.8 16.0 %collective-permute-start.6 = (bf16[512,640]{1,0:T(8,128)(2,1)S(1)}, bf16[512,640]{1,0:T(8,128)(2,1)}, u32[]{:S(2)}, u32[]{:S(2)}) collective-permute-start(bf16[512,640]{1,0:T(8,128)(2,1)S(1)} %collective-permute-done.3), channel_id=1, source_target_pairs={{0,2},{1,3},{2,0},{3,1},{4,6},{5,7},{6,4},{7,5},{8,10},{9,11},{10,... | collective-permute-start | bytes 1966088 | tf_op jit(solution)/shard_map/ppermute | solution.py:365
  51.4 19.8 %collective-permute-start.5 = (bf16[512,640]{1,0:T(8,128)(2,1)S(1)}, bf16[512,640]{1,0:T(8,128)(2,1)}, u32[]{:S(2)}, u32[]{:S(2)}) collective-permute-start(bf16[512,640]{1,0:T(8,128)(2,1)S(1)} %collective-permute-done.3), channel_id=1, source_target_pairs={{0,1},{1,0},{2,3},{3,2},{4,5},{5,4},{6,7},{7,6},{8,9},{9,8},{10,11... | collective-permute-start | bytes 1966088 | tf_op jit(solution)/shard_map/ppermute | solution.py:365
  51.4 24.9 %collective-permute-start.2 = (bf16[640,768]{1,0:T(8,128)(2,1)}, bf16[640,768]{1,0:T(8,128)(2,1)}, u32[]{:S(2)}, u32[]{:S(2)}) collective-permute-start(bf16[640,768]{1,0:T(8,128)(2,1)} %collective-permute-done.1), channel_id=1, source_target_pairs={{0,4},{4,0},{8,12},{12,8},{16,20},{20,16},{24,28},{28,24},{1,5},{5... | collective-permute-start | bytes 2949128 | tf_op jit(solution)/shard_map/ppermute | solution.py:365
  54.3 41.1 %collective-permute-start.12 = (bf16[640,768]{1,0:T(8,128)(2,1)}, bf16[640,768]{1,0:T(8,128)(2,1)}, u32[]{:S(2)}, u32[]{:S(2)}) collective-permute-start(bf16[640,768]{1,0:T(8,128)(2,1)} %param.20), channel_id=1, source_target_pairs={{0,8},{4,12},{8,0},{12,4},{16,24},{20,28},{24,16},{28,20},{1,9},{5... | collective-permute-start | bytes 2949128 | tf_op jit(solution)/shard_map/ppermute | solution.py:365
  62.8 16.3 %collective-permute-start.7 = (bf16[512,640]{1,0:T(8,128)(2,1)}, bf16[512,640]{1,0:T(8,128)(2,1)S(1)}, u32[]{:S(2)}, u32[]{:S(2)}) collective-permute-start(bf16[512,640]{1,0:T(8,128)(2,1)} %collective-permute-done.6), channel_id=1, source_target_pairs={{0,1},{1,0},{2,3},{3,2},{4,5},{5,4},{6,7},{7,6},{8,9},{9,8},{10,11... | collective-permute-start | bytes 1966088 | tf_op jit(solution)/shard_map/ppermute | solution.py:365
  71.0 28.3 %collective-permute-start.11 = (bf16[640,768]{1,0:T(8,128)(2,1)}, bf16[640,768]{1,0:T(8,128)(2,1)S(1)}, u32[]{:S(2)}, u32[]{:S(2)}) collective-permute-start(bf16[640,768]{1,0:T(8,128)(2,1)} %collective-permute-done.10), channel_id=1, source_target_pairs={{0,4},{4,0},{8,12},{12,8},{16,20},{20,16},{24,28},{28,24},{1,5},{5... | collective-permute-start | bytes 2949128 | tf_op jit(solution)/shard_map/ppermute | solution.py:365
  76.4 42.0 %collective-permute-start.13 = (bf16[640,768]{1,0:T(8,128)(2,1)S(1)}, bf16[640,768]{1,0:T(8,128)(2,1)S(1)}, u32[]{:S(2)}, u32[]{:S(2)}) collective-permute-start(bf16[640,768]{1,0:T(8,128)(2,1)S(1)} %copy-done.28), channel_id=1, source_target_pairs={{0,4},{4,0},{8,12},{12,8},{16,20},{20,16},{24,28},{28,24},{1,5},{5... | collective-permute-start | bytes 2949128 | tf_op jit(solution)/shard_map/ppermute | solution.py:365
  81.6 36.8 %collective-permute-start.9 = (bf16[512,768]{1,0:T(8,128)(2,1)S(1)}, bf16[512,768]{1,0:T(8,128)(2,1)S(1)}, u32[]{:S(2)}, u32[]{:S(2)}) collective-permute-start(bf16[512,768]{1,0:T(8,128)(2,1)S(1)} %convolution_convert_fusion.2), channel_id=1, source_target_pairs={{0,16},{4,20},{8,24},{12,28},{16,0},{20,4},{24,8},{28,12},{1,17},{... | collective-permute-start | bytes 2359304 | tf_op jit(solution)/shard_map/ppermute | solution.py:365
  95.5 44.1 %collective-permute-start.18 = (bf16[640,768]{1,0:T(8,128)(2,1)}, bf16[640,768]{1,0:T(8,128)(2,1)}, u32[]{:S(2)}, u32[]{:S(2)}) collective-permute-start(bf16[640,768]{1,0:T(8,128)(2,1)} %collective-permute-done.12), channel_id=1, source_target_pairs={{0,4},{4,0},{8,12},{12,8},{16,20},{20,16},{24,28},{28,24},{1,5},{5... | collective-permute-start | bytes 2949128 | tf_op jit(solution)/shard_map/ppermute | solution.py:365
  124.1 36.7 %collective-permute-start.17 = (bf16[8,64,768]{2,1,0:T(8,128)(2,1)}, bf16[8,64,768]{2,1,0:T(8,128)(2,1)S(1)}, u32[]{:S(2)}, u32[]{:S(2)}) collective-permute-start(bf16[8,64,768]{2,1,0:T(8,128)(2,1)} %bitcast.92), channel_id=1, source_target_pairs={{0,16},{4,20},{8,24},{12,28},{16,0},{20,4},{24,8},{28,12},{1,17},{... | collective-permute-start | bytes 2359304 | tf_op jit(solution)/shard_map/ppermute | solution.py:365
  126.6 34.3 %collective-permute-start.15 = (bf16[8,64,768]{2,1,0:T(8,128)(2,1)}, bf16[8,64,768]{2,1,0:T(8,128)(2,1)S(1)}, u32[]{:S(2)}, u32[]{:S(2)}) collective-permute-start(bf16[8,64,768]{2,1,0:T(8,128)(2,1)} %bitcast.93), channel_id=1, source_target_pairs={{0,8},{4,12},{8,0},{12,4},{16,24},{20,28},{24,16},{28,20},{1,9},{5... | collective-permute-start | bytes 2359304 | tf_op jit(solution)/shard_map/ppermute | solution.py:365
  128.2 32.7 %collective-permute-start.14 = (bf16[8,64,768]{2,1,0:T(8,128)(2,1)}, bf16[8,64,768]{2,1,0:T(8,128)(2,1)S(1)}, u32[]{:S(2)}, u32[]{:S(2)}) collective-permute-start(bf16[8,64,768]{2,1,0:T(8,128)(2,1)} %bitcast.94), channel_id=1, source_target_pairs={{0,4},{4,0},{8,12},{12,8},{16,20},{20,16},{24,28},{28,24},{1,5},{5... | collective-permute-start | bytes 2359304 | tf_op jit(solution)/shard_map/ppermute | solution.py:365
  161.0 31.6 %collective-permute-start.20 = (bf16[8,64,768]{2,1,0:T(8,128)(2,1)S(1)}, bf16[8,64,768]{2,1,0:T(8,128)(2,1)S(1)}, u32[]{:S(2)}, u32[]{:S(2)}) collective-permute-start(bf16[8,64,768]{2,1,0:T(8,128)(2,1)S(1)} %collective-permute-done.17.refs_4_), channel_id=1, source_target_pairs={{0,8},{4,12},{8,0},{12,4},{16,24},{20,28},{24,16},{28,20},{1,9},{5... | collective-permute-start | bytes 2359304 | tf_op jit(solution)/shard_map/ppermute | solution.py:365
  165.6 55.4 %collective-permute-start.22 = (bf16[640,768]{1,0:T(8,128)(2,1)S(1)}, bf16[640,768]{1,0:T(8,128)(2,1)S(1)}, u32[]{:S(2)}, u32[]{:S(2)}) collective-permute-start(bf16[640,768]{1,0:T(8,128)(2,1)S(1)} %copy-done.1), channel_id=1, source_target_pairs={{0,16},{4,20},{8,24},{12,28},{16,0},{20,4},{24,8},{28,12},{1,17},{... | collective-permute-start | bytes 2949128 | tf_op jit(solution)/shard_map/ppermute | solution.py:365
  168.1 37.4 %collective-permute-start.19 = (bf16[8,64,768]{2,1,0:T(8,128)(2,1)S(1)}, bf16[8,64,768]{2,1,0:T(8,128)(2,1)S(1)}, u32[]{:S(2)}, u32[]{:S(2)}) collective-permute-start(bf16[8,64,768]{2,1,0:T(8,128)(2,1)S(1)} %collective-permute-done.17.refs_4_), channel_id=1, source_target_pairs={{0,4},{4,0},{8,12},{12,8},{16,20},{20,16},{24,28},{28,24},{1,5},{5... | collective-permute-start | bytes 2359304 | tf_op jit(solution)/shard_map/ppermute | solution.py:365
  169.6 35.8 %collective-permute-start.16 = (bf16[8,64,768]{2,1,0:T(8,128)(2,1)S(1)}, bf16[8,64,768]{2,1,0:T(8,128)(2,1)S(1)}, u32[]{:S(2)}, u32[]{:S(2)}) collective-permute-start(bf16[8,64,768]{2,1,0:T(8,128)(2,1)S(1)} %collective-permute-done.15.refs_2_), channel_id=1, source_target_pairs={{0,4},{4,0},{8,12},{12,8},{16,20},{20,16},{24,28},{28,24},{1,5},{5... | collective-permute-start | bytes 2359304 | tf_op jit(solution)/shard_map/ppermute | solution.py:365
  192.5 28.2 %collective-permute-start.21 = (bf16[8,64,768]{2,1,0:T(8,128)(2,1)S(1)}, bf16[8,64,768]{2,1,0:T(8,128)(2,1)S(1)}, u32[]{:S(2)}, u32[]{:S(2)}) collective-permute-start(bf16[8,64,768]{2,1,0:T(8,128)(2,1)S(1)} %collective-permute-done.20.refs_6_), channel_id=1, source_target_pairs={{0,4},{4,0},{8,12},{12,8},{16,20},{20,16},{24,28},{28,24},{1,5},{5... | collective-permute-start | bytes 2359304 | tf_op jit(solution)/shard_map/ppermute | solution.py:365
  220.7 48.5 %collective-permute-start.25 = (bf16[640,768]{1,0:T(8,128)(2,1)S(1)}, bf16[640,768]{1,0:T(8,128)(2,1)S(1)}, u32[]{:S(2)}, u32[]{:S(2)}) collective-permute-start(bf16[640,768]{1,0:T(8,128)(2,1)S(1)} %copy-done.1), channel_id=1, source_target_pairs={{0,8},{4,12},{8,0},{12,4},{16,24},{20,28},{24,16},{28,20},{1,9},{5... | collective-permute-start | bytes 2949128 | tf_op jit(solution)/shard_map/ppermute | solution.py:365
  221.0 45.5 %collective-permute-start.27 = (bf16[640,768]{1,0:T(8,128)(2,1)S(1)}, bf16[640,768]{1,0:T(8,128)(2,1)}, u32[]{:S(2)}, u32[]{:S(2)}) collective-permute-start(bf16[640,768]{1,0:T(8,128)(2,1)S(1)} %collective-permute-done.22.refs_4_), channel_id=1, source_target_pairs={{0,4},{4,0},{8,12},{12,8},{16,20},{20,16},{24,28},{28,24},{1,5},{5... | collective-permute-start | bytes 2949128 | tf_op jit(solution)/shard_map/ppermute | solution.py:365
  223.8 55.4 %collective-permute-start.23 = (bf16[512,768]{1,0:T(8,128)(2,1)S(1)}, bf16[512,768]{1,0:T(8,128)(2,1)}, u32[]{:S(2)}, u32[]{:S(2)}) collective-permute-start(bf16[512,768]{1,0:T(8,128)(2,1)S(1)} %convolution_convert_fusion.1), channel_id=1, source_target_pairs={{0,16},{4,20},{8,24},{12,28},{16,0},{20,4},{24,8},{28,12},{1,17},{... | collective-permute-start | bytes 2359304 | tf_op jit(solution)/shard_map/ppermute | solution.py:365
  227.4 66.0 %collective-permute-start.24 = (bf16[512,768]{1,0:T(8,128)(2,1)}, bf16[512,768]{1,0:T(8,128)(2,1)}, u32[]{:S(2)}, u32[]{:S(2)}) collective-permute-start(bf16[512,768]{1,0:T(8,128)(2,1)} %convolution_convert_fusion), channel_id=1, source_target_pairs={{0,16},{4,20},{8,24},{12,28},{16,0},{20,4},{24,8},{28,12},{1,17},{... | collective-permute-start | bytes 2359304 | tf_op jit(solution)/shard_map/ppermute | solution.py:365
  230.2 68.4 %collective-permute-start.26 = (bf16[640,768]{1,0:T(8,128)(2,1)S(1)}, bf16[640,768]{1,0:T(8,128)(2,1)}, u32[]{:S(2)}, u32[]{:S(2)}) collective-permute-start(bf16[640,768]{1,0:T(8,128)(2,1)S(1)} %copy-done.1), channel_id=1, source_target_pairs={{0,4},{4,0},{8,12},{12,8},{16,20},{20,16},{24,28},{28,24},{1,5},{5... | collective-permute-start | bytes 2949128 | tf_op jit(solution)/shard_map/ppermute | solution.py:365
  266.5 60.5 %collective-permute-start.29 = (bf16[640,768]{1,0:T(8,128)(2,1)S(1)}, bf16[640,768]{1,0:T(8,128)(2,1)}, u32[]{:S(2)}, u32[]{:S(2)}) collective-permute-start(bf16[640,768]{1,0:T(8,128)(2,1)S(1)} %collective-permute-done.22.refs_4_), channel_id=1, source_target_pairs={{0,8},{4,12},{8,0},{12,4},{16,24},{20,28},{24,16},{28,20},{1,9},{5... | collective-permute-start | bytes 2949128 | tf_op jit(solution)/shard_map/ppermute | solution.py:365
  269.2 57.8 %collective-permute-start.28 = (bf16[640,768]{1,0:T(8,128)(2,1)S(1)}, bf16[640,768]{1,0:T(8,128)(2,1)}, u32[]{:S(2)}, u32[]{:S(2)}) collective-permute-start(bf16[640,768]{1,0:T(8,128)(2,1)S(1)} %collective-permute-done.25.refs_2_), channel_id=1, source_target_pairs={{0,4},{4,0},{8,12},{12,8},{16,20},{20,16},{24,28},{28,24},{1,5},{5... | collective-permute-start | bytes 2949128 | tf_op jit(solution)/shard_map/ppermute | solution.py:365
  279.2 47.9 %collective-permute-start.30 = (bf16[640,768]{1,0:T(8,128)(2,1)}, bf16[640,768]{1,0:T(8,128)(2,1)}, u32[]{:S(2)}, u32[]{:S(2)}) collective-permute-start(bf16[640,768]{1,0:T(8,128)(2,1)} %collective-permute-done.27.refs_5_), channel_id=1, source_target_pairs={{0,8},{4,12},{8,0},{12,4},{16,24},{20,28},{24,16},{28,20},{1,9},{5... | collective-permute-start | bytes 2949128 | tf_op jit(solution)/shard_map/ppermute | solution.py:365
  327.1 16.9 %collective-permute-start.32 = (bf16[800,256]{1,0:T(8,128)(2,1)}, bf16[800,256]{1,0:T(8,128)(2,1)S(1)}, u32[]{:S(2)}, u32[]{:S(2)}) collective-permute-start(bf16[800,256]{1,0:T(8,128)(2,1)} %get-tuple-element.103), channel_id=1, source_target_pairs={{0,4},{4,0},{8,12},{12,8},{16,20},{20,16},{24,28},{28,24},{1,5},{5... | collective-permute-start | bytes 1228808 | tf_op jit(solution)/shard_map/ppermute | solution.py:365
  329.4 19.0 %collective-permute-start.45 = (bf16[800,256]{1,0:T(8,128)(2,1)}, bf16[800,256]{1,0:T(8,128)(2,1)}, u32[]{:S(2)}, u32[]{:S(2)}) collective-permute-start(bf16[800,256]{1,0:T(8,128)(2,1)} %get-tuple-element.117), channel_id=1, source_target_pairs={{0,8},{4,12},{8,0},{12,4},{16,24},{20,28},{24,16},{28,20},{1,9},{5... | collective-permute-start | bytes 1228808 | tf_op jit(solution)/shard_map/ppermute | solution.py:365
  331.4 25.7 %collective-permute-start.34 = (bf16[800,256]{1,0:T(8,128)(2,1)}, bf16[800,256]{1,0:T(8,128)(2,1)}, u32[]{:S(2)}, u32[]{:S(2)}) collective-permute-start(bf16[800,256]{1,0:T(8,128)(2,1)} %get-tuple-element.105), channel_id=1, source_target_pairs={{0,8},{4,12},{8,0},{12,4},{16,24},{20,28},{24,16},{28,20},{1,9},{5... | collective-permute-start | bytes 1228808 | tf_op jit(solution)/shard_map/ppermute | solution.py:365
  341.7 19.8 %collective-permute-start.36 = (bf16[800,256]{1,0:T(8,128)(2,1)}, bf16[800,256]{1,0:T(8,128)(2,1)}, u32[]{:S(2)}, u32[]{:S(2)}) collective-permute-start(bf16[800,256]{1,0:T(8,128)(2,1)} %merge_partials.18), channel_id=1, source_target_pairs={{0,4},{4,0},{8,12},{12,8},{16,20},{20,16},{24,28},{28,24},{1,5},{5... | collective-permute-start | bytes 1228808 | tf_op jit(solution)/shard_map/ppermute | solution.py:365
  344.0 19.6 %collective-permute-start.31 = (bf16[800,256]{1,0:T(8,128)(2,1)}, bf16[800,256]{1,0:T(8,128)(2,1)}, u32[]{:S(2)}, u32[]{:S(2)}) collective-permute-start(bf16[800,256]{1,0:T(8,128)(2,1)} %copy-done.20), channel_id=1, source_target_pairs={{0,4},{4,0},{8,12},{12,8},{16,20},{20,16},{24,28},{28,24},{1,5},{5... | collective-permute-start | bytes 1228808 | tf_op jit(solution)/shard_map/ppermute | solution.py:365
  344.0 29.2 %collective-permute-start.42 = (bf16[800,256]{1,0:T(8,128)(2,1)}, bf16[800,256]{1,0:T(8,128)(2,1)}, u32[]{:S(2)}, u32[]{:S(2)}) collective-permute-start(bf16[800,256]{1,0:T(8,128)(2,1)} %copy-done.19), channel_id=1, source_target_pairs={{0,4},{4,0},{8,12},{12,8},{16,20},{20,16},{24,28},{28,24},{1,5},{5... | collective-permute-start | bytes 1228808 | tf_op jit(solution)/shard_map/ppermute | solution.py:365
  348.4 28.9 %collective-permute-start.44 = (bf16[800,256]{1,0:T(8,128)(2,1)}, bf16[800,256]{1,0:T(8,128)(2,1)}, u32[]{:S(2)}, u32[]{:S(2)}) collective-permute-start(bf16[800,256]{1,0:T(8,128)(2,1)} %copy-done.18), channel_id=1, source_target_pairs={{0,8},{4,12},{8,0},{12,4},{16,24},{20,28},{24,16},{28,20},{1,9},{5... | collective-permute-start | bytes 1228808 | tf_op jit(solution)/shard_map/ppermute | solution.py:365
  357.2 22.2 %collective-permute-start.46 = (bf16[800,256]{1,0:T(8,128)(2,1)}, bf16[800,256]{1,0:T(8,128)(2,1)}, u32[]{:S(2)}, u32[]{:S(2)}) collective-permute-start(bf16[800,256]{1,0:T(8,128)(2,1)} %merge_partials.25), channel_id=1, source_target_pairs={{0,4},{4,0},{8,12},{12,8},{16,20},{20,16},{24,28},{28,24},{1,5},{5... | collective-permute-start | bytes 1228808 | tf_op jit(solution)/shard_map/ppermute | solution.py:365
  361.5 25.5 %collective-permute-start.33 = (bf16[800,256]{1,0:T(8,128)(2,1)}, bf16[800,256]{1,0:T(8,128)(2,1)}, u32[]{:S(2)}, u32[]{:S(2)}) collective-permute-start(bf16[800,256]{1,0:T(8,128)(2,1)} %merge_partials.15), channel_id=1, source_target_pairs={{0,8},{4,12},{8,0},{12,4},{16,24},{20,28},{24,16},{28,20},{1,9},{5... | collective-permute-start | bytes 1228808 | tf_op jit(solution)/shard_map/ppermute | solution.py:365
  363.6 26.2 %collective-permute-start.37 = (bf16[800,256]{1,0:T(8,128)(2,1)}, bf16[800,256]{1,0:T(8,128)(2,1)}, u32[]{:S(2)}, u32[]{:S(2)}) collective-permute-start(bf16[800,256]{1,0:T(8,128)(2,1)} %merge_partials.19), channel_id=1, source_target_pairs={{0,16},{4,20},{8,24},{12,28},{16,0},{20,4},{24,8},{28,12},{1,17},{... | collective-permute-start | bytes 1228808 | tf_op jit(solution)/shard_map/ppermute | solution.py:365
  373.2 29.8 %collective-permute-start.41 = (bf16[800,256]{1,0:T(8,128)(2,1)S(1)}, bf16[800,256]{1,0:T(8,128)(2,1)}, u32[]{:S(2)}, u32[]{:S(2)}) collective-permute-start(bf16[800,256]{1,0:T(8,128)(2,1)S(1)} %copy-done.17), channel_id=1, source_target_pairs={{0,4},{4,0},{8,12},{12,8},{16,20},{20,16},{24,28},{28,24},{1,5},{5... | collective-permute-start | bytes 1228808 | tf_op jit(solution)/shard_map/ppermute | solution.py:365
  377.3 27.7 %collective-permute-start.43 = (bf16[800,256]{1,0:T(8,128)(2,1)}, bf16[800,256]{1,0:T(8,128)(2,1)}, u32[]{:S(2)}, u32[]{:S(2)}) collective-permute-start(bf16[800,256]{1,0:T(8,128)(2,1)} %merge_partials.22), channel_id=1, source_target_pairs={{0,8},{4,12},{8,0},{12,4},{16,24},{20,28},{24,16},{28,20},{1,9},{5... | collective-permute-start | bytes 1228808 | tf_op jit(solution)/shard_map/ppermute | solution.py:365
  381.4 25.7 %collective-permute-start.47 = (bf16[800,256]{1,0:T(8,128)(2,1)}, bf16[800,256]{1,0:T(8,128)(2,1)}, u32[]{:S(2)}, u32[]{:S(2)}) collective-permute-start(bf16[800,256]{1,0:T(8,128)(2,1)} %merge_partials.26), channel_id=1, source_target_pairs={{0,16},{4,20},{8,24},{12,28},{16,0},{20,4},{24,8},{28,12},{1,17},{... | collective-permute-start | bytes 1228808 | tf_op jit(solution)/shard_map/ppermute | solution.py:365
  403.0 15.6 %collective-permute-start.39 = (bf16[2,256,640]{2,1,0:T(8,128)(2,1)}, bf16[2,256,640]{2,1,0:T(8,128)(2,1)}, u32[]{:S(2)}, u32[]{:S(2)}) collective-permute-start(bf16[2,256,640]{2,1,0:T(8,128)(2,1)} %get-tuple-element.139), channel_id=1, source_target_pairs={{0,1},{1,0},{2,3},{3,2},{4,5},{5,4},{6,7},{7,6},{8,9},{9,8},{10,11... | collective-permute-start | bytes 1966088 | tf_op jit(solution)/shard_map/ppermute | solution.py:658
  420.8 17.6 %collective-permute-start.40 = (bf16[2,256,640]{2,1,0:T(8,128)(2,1)S(1)}, bf16[2,256,640]{2,1,0:T(8,128)(2,1)S(1)}, u32[]{:S(2)}, u32[]{:S(2)}) collective-permute-start(bf16[2,256,640]{2,1,0:T(8,128)(2,1)S(1)} %fusion.5), channel_id=1, source_target_pairs={{0,2},{1,3},{2,0},{3,1},{4,6},{5,7},{6,4},{7,5},{8,10},{9,11},{10,... | collective-permute-start | bytes 1966088 | tf_op jit(solution)/shard_map/ppermute | solution.py:658
  421.5 17.2 %collective-permute-start.48 = (bf16[2,256,640]{2,1,0:T(8,128)(2,1)S(1)}, bf16[2,256,640]{2,1,0:T(8,128)(2,1)S(1)}, u32[]{:S(2)}, u32[]{:S(2)}) collective-permute-start(bf16[2,256,640]{2,1,0:T(8,128)(2,1)S(1)} %get-tuple-element.140), channel_id=1, source_target_pairs={{0,1},{1,0},{2,3},{3,2},{4,5},{5,4},{6,7},{7,6},{8,9},{9,8},{10,11... | collective-permute-start | bytes 1966088 | tf_op jit(solution)/shard_map/ppermute | solution.py:658
  421.9 30.2 %collective-permute-start.50 = (bf16[2,256,640]{2,1,0:T(8,128)(2,1)S(1)}, bf16[2,256,640]{2,1,0:T(8,128)(2,1)S(1)}, u32[]{:S(2)}, u32[]{:S(2)}) collective-permute-start(bf16[2,256,640]{2,1,0:T(8,128)(2,1)S(1)} %fusion.2), channel_id=1, source_target_pairs={{0,2},{1,3},{2,0},{3,1},{4,6},{5,7},{6,4},{7,5},{8,10},{9,11},{10,... | collective-permute-start | bytes 1966088 | tf_op jit(solution)/shard_map/ppermute | solution.py:658
  (56 other events, 671.1 us)
